TPU v7x, 256 devices: a whole 4x4x8 slice. The times are simulated.
256 devices in a mesh: outer: 16 (over z_lo, y, core), inner: 4 (over z_hi), dp: 4 (over x).
Axes of the slice: x: 4, y: 4, z: 8 (z_hi: 4, z_lo: 2; z = z_hi * 2 + z_lo), core: 2. Of those that a mesh axis runs over, the one named last changes fastest.
Arguments:
- queries: bfloat16 [4, 8192, 2048], P('dp', ('outer', 'inner')), may hold values from -9 to 9
- keys: bfloat16 [4, 8192, 2048], P('dp', ('outer', 'inner')), may hold values from -9 to 9
- values: bfloat16 [4, 8192, 2048], P('dp', ('outer', 'inner')), may hold values from -6 to 6
- out_grad: bfloat16 [4, 8192, 2048], P('dp', ('outer', 'inner')), may hold values from -15 to 15
- gain: float32 [2048], replicated, may hold values from 0.1 to 1.9
- block_order: int32 [128], P(('outer', 'inner')), may hold values from 0 to 127, each once
- start: int32 [1], replicated, may hold values from 1 to 3
Outputs:
- attended: bfloat16 [4, 8192, 2048], P('dp', ('outer', 'inner'))
- query_grad: bfloat16 [4, 8192, 2048], P('dp', ('outer', 'inner'))
- key_grad: bfloat16 [4, 8192, 2048], P('dp', ('outer', 'inner'))
- value_grad: bfloat16 [4, 8192, 2048], P('dp', ('outer', 'inner'))
- gain_grad: float32 [2048], replicated
Inputs may be any that keep to these rules, and one draw needn't show every extreme that they name: `block_order`: a permutation of the block numbers.
All inputs are finite; a program needn't handle non-finite values.
Results may differ from a plain program's by a relative error of at most 0.025.
Values may be sent and summed in bfloat16 or wider, within the bound.
No kernel may reach another device: no remote copies, remote signals or barrier semaphores. Data moves between devices by JAX's collectives and lax.ppermute only.
A program may use at most 128 MiB of HBM per device.

v0:
```python
import math

import jax
import jax.numpy as jnp
from jax import lax
from jax.sharding import PartitionSpec as P

HEAD_DIM = 128


def shifted(value, axis, steps):
    count = lax.axis_size(axis)
    pairs = [(source, (source + steps) % count) for source in range(count)]
    return lax.ppermute(value, axis, pairs)


def attend(query_part, key_part, value_part, grad_part, query_positions, key_positions):
    local_rows, channels = query_part.shape
    key_count = key_part.shape[0]
    span = 4 * HEAD_DIM
    score_scale = HEAD_DIM ** (-0.5)
    visible = key_positions[None, :] <= query_positions[:, None]
    outputs = []
    query_grads = []
    key_grads = []
    value_grads = []
    for column_start in range(0, channels, span):
        query_heads = query_part[:, column_start : column_start + span].reshape(
            local_rows, 4, HEAD_DIM
        )
        key_heads = key_part[:, column_start : column_start + span].reshape(key_count, 4, HEAD_DIM)
        value_heads = value_part[:, column_start : column_start + span].reshape(
            key_count, 4, HEAD_DIM
        )
        grad_heads = grad_part[:, column_start : column_start + span].reshape(
            local_rows, 4, HEAD_DIM
        )
        raw_scores = jnp.einsum(
            "qhd,khd->hqk", query_heads, key_heads, preferred_element_type=jnp.float32
        )
        scores = jnp.where(visible[None], raw_scores * score_scale, -jnp.inf)
        row_max = jnp.max(scores, axis=-1, keepdims=True)
        exp_scores = jnp.exp(scores - row_max)
        inverse_total = 1.0 / jnp.sum(exp_scores, axis=-1, keepdims=True)
        weights_bf = (exp_scores * inverse_total).astype(jnp.bfloat16)
        attended_part = jnp.einsum(
            "hqk,khd->qhd", weights_bf, value_heads, preferred_element_type=jnp.float32
        ).astype(jnp.bfloat16)
        row_dot = jnp.sum(
            grad_heads.astype(jnp.float32) * attended_part.astype(jnp.float32), axis=-1
        )
        prob_grad = jnp.einsum(
            "qhd,khd->hqk", grad_heads, value_heads, preferred_element_type=jnp.float32
        )
        score_grad = (exp_scores * inverse_total * (prob_grad - row_dot.T[:, :, None])).astype(
            jnp.bfloat16
        )
        query_grad_part = (
            jnp.einsum("hqk,khd->qhd", score_grad, key_heads, preferred_element_type=jnp.float32)
            * score_scale
        ).astype(jnp.bfloat16)
        key_grad_part = (
            jnp.einsum("hqk,qhd->khd", score_grad, query_heads, preferred_element_type=jnp.float32)
            * score_scale
        )
        value_grad_part = jnp.einsum(
            "hqk,qhd->khd", weights_bf, grad_heads, preferred_element_type=jnp.float32
        )
        outputs.append(attended_part.reshape(local_rows, span))
        query_grads.append(query_grad_part.reshape(local_rows, span))
        key_grads.append(key_grad_part.reshape(key_count, span))
        value_grads.append(value_grad_part.reshape(key_count, span))
    return (
        jnp.concatenate(outputs, axis=1),
        jnp.concatenate(query_grads, axis=1),
        jnp.concatenate(key_grads, axis=1),
        jnp.concatenate(value_grads, axis=1),
    )


def block_positions(order_part, half_rows):
    return (
        order_part[:, None] * half_rows + jnp.arange(half_rows, dtype=jnp.int32)[None, :]
    ).reshape(-1)


def body(queries, keys, values, out_grad, gain, block_order, start):
    local_rows = queries.shape[1]
    channels = queries.shape[2]
    half_rows = local_rows // 2
    inner_count = lax.axis_size("inner")
    step_index = (lax.axis_index("inner") - start[0]) % inner_count
    keyed = (keys[0].astype(jnp.float32) * gain).astype(jnp.bfloat16)
    value_rows = values[0]
    near_keys, near_values, near_order = (
        lax.all_gather(keyed, "inner", axis=0, tiled=True),
        lax.all_gather(value_rows, "inner", axis=0, tiled=True),
        lax.all_gather(block_order, "inner", axis=0, tiled=True),
    )
    prior_keys, prior_values, prior_order = shifted(
        (near_keys, near_values, near_order), "outer", 1
    )
    step_keys = lax.dynamic_slice_in_dim(near_keys, step_index * local_rows, local_rows, 0)
    step_values = lax.dynamic_slice_in_dim(near_values, step_index * local_rows, local_rows, 0)
    step_order = lax.dynamic_slice_in_dim(near_order, step_index * 2, 2, 0)
    all_keys = jnp.concatenate([keyed, step_keys, prior_keys], axis=0)
    all_values = jnp.concatenate([value_rows, step_values, prior_values], axis=0)
    all_order = jnp.concatenate([block_order, step_order, prior_order], axis=0)
    attended_part, query_grad_part, key_part, value_part = attend(
        queries[0],
        all_keys,
        all_values,
        out_grad[0],
        block_positions(block_order, half_rows),
        block_positions(all_order, half_rows),
    )
    key_round = key_part.astype(jnp.bfloat16)
    value_round = value_part.astype(jnp.bfloat16)
    own_keys = lax.optimization_barrier(key_round[:local_rows]).astype(jnp.float32)
    own_values = lax.optimization_barrier(value_round[:local_rows]).astype(jnp.float32)
    step_key_part = key_round[local_rows : 2 * local_rows].astype(jnp.float32)
    step_value_part = value_round[local_rows : 2 * local_rows].astype(jnp.float32)
    group_keys = key_round[2 * local_rows :].reshape(inner_count, local_rows, channels)
    group_values = value_round[2 * local_rows :].reshape(inner_count, local_rows, channels)
    empty = jnp.zeros((inner_count, local_rows, channels), jnp.float32)
    slot_keys = lax.dynamic_update_slice_in_dim(empty, step_key_part[None], step_index, 0)
    slot_values = lax.dynamic_update_slice_in_dim(empty, step_value_part[None], step_index, 0)
    back_keys, back_values = shifted((group_keys, group_values), "outer", -1)
    from_keys, from_values, near_sum_keys, near_sum_values = (
        lax.psum_scatter(
            back_keys.astype(jnp.float32).astype(jnp.bfloat16),
            "inner",
            scatter_dimension=0,
            tiled=True,
        ).astype(jnp.float32),
        lax.psum_scatter(
            back_values.astype(jnp.float32).astype(jnp.bfloat16),
            "inner",
            scatter_dimension=0,
            tiled=True,
        ).astype(jnp.float32),
        lax.psum_scatter(
            slot_keys.astype(jnp.bfloat16), "inner", scatter_dimension=0, tiled=True
        ).astype(jnp.float32),
        lax.psum_scatter(
            slot_values.astype(jnp.bfloat16), "inner", scatter_dimension=0, tiled=True
        ).astype(jnp.float32),
    )
    total_keys = own_keys + from_keys[0] + near_sum_keys[0]
    total_values = own_values + from_values[0] + near_sum_values[0]
    key_grad = (total_keys * gain).astype(jnp.bfloat16)
    value_grad = total_values.astype(jnp.bfloat16)
    gain_term = jnp.sum(total_keys * keys[0].astype(jnp.float32), axis=0)
    token_count = local_rows * inner_count * lax.axis_size("outer") * lax.axis_size("dp")
    gain_grad = lax.psum(gain_term, ("outer", "inner", "dp")) / math.sqrt(token_count)
    return (attended_part[None], query_grad_part[None], key_grad[None], value_grad[None], gain_grad)


def solution(mesh):
    in_specs = (
        P("dp", ("outer", "inner"), None),
        P("dp", ("outer", "inner"), None),
        P("dp", ("outer", "inner"), None),
        P("dp", ("outer", "inner"), None),
        P(),
        P(("outer", "inner")),
        P(),
    )
    out_specs = (
        P("dp", ("outer", "inner"), None),
        P("dp", ("outer", "inner"), None),
        P("dp", ("outer", "inner"), None),
        P("dp", ("outer", "inner"), None),
        P(),
    )
    return jax.shard_map(body, mesh=mesh, in_specs=in_specs, out_specs=out_specs, check_vma=False)
```

profile of v0, /device:TPU:1, one launch (start us, length us, event | category | flops | bytes accessed | tf_op | source)
XLA Modules:
  0.0 513.5 jit_solution(16353089549904880295)
XLA Ops:
  7.2 1.4 copy.130
  8.6 1.9 fusion.24
  11.3 58.7 %all-gather.4.cloned.1.call-done = bf16[512,2048]{0,1:T(8,128)(2,1)} async-done(((bf16[128,2048]{0,1:T(8,128)(2,1)}), bf16[512,2048]{0,1:T(8,128)(2,1)}) %all-gather.4.cloned.1.call-update) | async-done | bytes 2097168 | tf_op jit(solution)/shard_map/all_gather | solution.py:96
  70.0 1.5 collective-permute-start.2
  73.1 8.5 %all-reduce = s32[8]{0:T(128)} all-reduce(s32[8]{0:T(128)S(1)} %dynamic-update-slice), channel_id=1, replica_groups=mesh['outer'=16,'inner'=4,'dp'=4] {'inner'}, use_global_device_ids=true, to_apply=%add | all-reduce | flops 8 | bytes 64
  81.5 1.7 collective-permute-start.1
  84.6 1.7 copy.163
  86.3 1.3 copy.131
  91.5 3.3 collective-permute-done.1
  95.3 23.7 %all-gather.6.cloned.1.call-done = bf16[1,512,2048]{2,1,0:T(8,128)(2,1)} async-done(((bf16[1,128,2048]{2,1,0:T(8,128)(2,1)}), bf16[1,512,2048]{2,1,0:T(8,128)(2,1)}) %all-gather.6.cloned.1.call-update) | async-done | bytes 2097168 | tf_op jit(solution)/shard_map/all_gather | solution.py:97
  118.9 4.7 collective-permute-start
  123.6 1.9 dynamic-slice_bitcast_fusion
  127.2 2.9 fusion.49
  130.1 2.5 bitcast_select_fusion
  132.6 2.9 fusion.50
  135.5 1.6 bitcast_select_fusion.1
  137.1 1.9 fusion.51
  139.0 1.6 bitcast_select_fusion.2
  140.6 1.9 fusion.52
  142.5 1.7 bitcast_select_fusion.3
  144.2 2.8 collective-permute-done
  146.9 2.0 pad_maximum_fusion
  152.9 3.3 multiply_reduce_fusion
  156.2 1.9 fusion.8
  159.0 1.3 fusion.19
  160.3 1.4 copy.182
  161.7 3.2 multiply_reduce_fusion.1
  164.9 2.0 fusion.9
  169.0 1.4 copy.179
  170.4 3.2 multiply_reduce_fusion.2
  173.7 1.9 fusion.10
  177.8 1.7 copy.176
  179.5 3.2 multiply_reduce_fusion.3
  182.7 1.9 fusion.11
  186.7 1.4 copy.173
  188.1 1.6 broadcast_in_dim.77.clone
  191.4 22.7 %collective-permute-start.3 = (bf16[4,128,2048]{1,2,0:T(8,128)(2,1)S(1)}, bf16[4,128,2048]{1,2,0:T(8,128)(2,1)}, u32[]{:S(2)}, u32[]{:S(2)}) collective-permute-start(bf16[4,128,2048]{1,2,0:T(8,128)(2,1)S(1)} %copy_bitcast_fusion), channel_id=1, source_target_pairs={{0,240},{16,0},{32,16},{48,32},{64,48},{80,64},{96,80},{112,96},{1... | collective-permute-start | bytes 6291464 | tf_op jit(solution)/shard_map/ppermute | solution.py:14
  214.1 3.9 collective-permute-done.3
  218.1 3.5 convolution_convert_fusion
  221.6 3.7 convolution_convert_fusion.1
  225.3 3.5 convolution_convert_fusion.2
  228.8 3.5 convolution_convert_fusion.3
  232.3 1.7 broadcast_in_dim.77.clone.1
  234.1 1.8 convert_dynamic-update-slice_fusion
  235.9 2.0 pad_maximum_fusion.3
  238.0 1.5 slice.105
  239.5 4.0 copy.188
  243.5 4.0 copy.189
  247.4 53.1 %collective-permute-start.4 = (bf16[4,128,2048]{1,2,0:T(8,128)(2,1)}, bf16[4,128,2048]{1,2,0:T(8,128)(2,1)}, u32[]{:S(2)}, u32[]{:S(2)}) collective-permute-start(bf16[4,128,2048]{1,2,0:T(8,128)(2,1)} %copy.189), channel_id=1, source_target_pairs={{0,240},{16,0},{32,16},{48,32},{64,48},{80,64},{96,80},{112,96},{1... | collective-permute-start | bytes 6291464 | tf_op jit(solution)/shard_map/ppermute | solution.py:14
  300.6 4.1 collective-permute-done.4
  306.0 1.7 copy.147
  307.7 2.4 fusion.23
  310.1 1.7 copy.170
  311.7 2.4 fusion.22
  314.1 1.7 copy.169
  315.8 2.4 fusion.21
  318.2 1.7 copy.168
  319.8 2.4 fusion.20
  322.2 1.7 copy.167
  328.6 1.8 fusion.25
  331.5 47.3 %reduce-scatter.11.cloned.1.call-done = bf16[1,128,2048]{1,2,0:T(8,128)(2,1)} async-done(((bf16[4,128,2048]{1,2,0:T(8,128)(2,1)}), bf16[1,128,2048]{1,2,0:T(8,128)(2,1)}) %reduce-scatter.11.cloned.1.call-update) | async-done | bytes 524304 | tf_op jit(solution)/shard_map/reduce_scatter | solution.py:145
  378.8 49.3 %reduce-scatter.9.cloned.1.call-done = bf16[1,128,2048]{1,2,0:T(8,128)(2,1)} async-done(((bf16[4,128,2048]{1,2,0:T(8,128)(2,1)}), bf16[1,128,2048]{1,2,0:T(8,128)(2,1)}) %reduce-scatter.9.cloned.1.call-update) | async-done | bytes 524304 | tf_op jit(solution)/shard_map/reduce_scatter | solution.py:136
  428.1 1.4 fusion.28
  430.5 75.5 %psum.7 = f32[2048]{0:T(1024)S(1)} all-reduce(f32[2048]{0:T(1024)S(1)} %get-tuple-element.23), channel_id=1, replica_groups=mesh['outer'=16,'inner'=4,'dp'=4] {'outer','inner','dp'}, use_global_device_ids=true, to_apply=%region_17.18 | all-reduce | flops 2048 | bytes 16384 | tf_op jit(solution)/shard_map/psum | solution.py:155
  (136 shorter events, 30.0 us)
Async XLA Ops:
  7.2 64.4 %copy-start.38 = (u32[256]{0:T(256)S(1)}, u32[256]{0:T(256)}, u32[]{:S(2)}) copy-start(u32[256]{0:T(256)} %constant.52) | copy-start | bytes 3076
  7.2 65.6 %copy-start.37 = (s32[2]{0:T(128)S(1)}, s32[2]{0:T(128)}, u32[]{:S(2)}) copy-start(s32[2]{0:T(128)} %param.12) | copy-start | bytes 28
  7.2 76.7 %copy-start.33 = (bf16[1,128,2048]{2,1,0:T(8,128)(2,1)S(1)}, bf16[1,128,2048]{2,1,0:T(8,128)(2,1)}, u32[]{:S(2)}) copy-start(bf16[1,128,2048]{2,1,0:T(8,128)(2,1)} %param.10) | copy-start | bytes 1572868
  7.2 62.8 %all-gather.4.cloned.1.call-start = ((), (), s32[]{:S(2)}) async-start(), calls=%async_computation.4 | async-start | bytes 2621440 | tf_op jit(solution)/shard_map/all_gather | solution.py:96
  8.6 76.0 %copy-start.14 = (bf16[1,128,2048]{1,2,0:T(8,128)(2,1)}, bf16[1,128,2048]{1,2,0:T(8,128)(2,1)S(1)}, u32[]{:S(2)}) copy-start(bf16[1,128,2048]{1,2,0:T(8,128)(2,1)S(1)} %copy.130) | copy-start | bytes 1572868
  10.5 108.4 %all-gather.6.cloned.1.call-start = ((), (), s32[]{:S(2)}) async-start(), calls=%async_computation.9 | async-start | bytes 2621440 | tf_op jit(solution)/shard_map/all_gather | solution.py:97
  11.3 316.9 %reduce-scatter.7.cloned.1.call-start = ((), (), s32[]{:S(2)}) async-start(), calls=%async_computation.6 | async-start | bytes 2621440 | tf_op jit(solution)/shard_map/reduce_scatter | solution.py:142
  70.0 56.6 %collective-permute-start.2 = (bf16[512,2048]{0,1:T(8,128)(2,1)}, bf16[512,2048]{0,1:T(8,128)(2,1)S(1)}, u32[]{:S(2)}, u32[]{:S(2)}) collective-permute-start(bf16[512,2048]{0,1:T(8,128)(2,1)} %all-gather.4.cloned.1.call-done), channel_id=1, source_target_pairs={{0,16},{16,32},{32,48},{48,64},{64,80},{80,96},{96,112},{112,128},... | collective-permute-start | bytes 6291464 | tf_op jit(solution)/shard_map/ppermute | solution.py:14
  81.5 13.3 %collective-permute-start.1 = (s32[8]{0:T(128)}, s32[8]{0:T(128)S(1)}, u32[]{:S(2)}, u32[]{:S(2)}) collective-permute-start(s32[8]{0:T(128)} %all-reduce), channel_id=1, source_target_pairs={{0,16},{16,32},{32,48},{48,64},{64,80},{80,96},{96,112},{112,128},... | collective-permute-start | bytes 104 | tf_op jit(solution)/shard_map/ppermute | solution.py:14
  90.8 35.9 %copy-start.16 = (bf16[128,2048]{0,1:T(8,128)(2,1)S(1)}, bf16[128,2048]{0,1:T(8,128)(2,1)}, u32[]{:S(2)}) copy-start(bf16[128,2048]{0,1:T(8,128)(2,1)} %fusion.24) | copy-start | bytes 1572868
  118.9 28.0 %collective-permute-start = (bf16[512,2048]{1,0:T(8,128)(2,1)}, bf16[512,2048]{1,0:T(8,128)(2,1)}, u32[]{:S(2)}, u32[]{:S(2)}) collective-permute-start(bf16[512,2048]{1,0:T(8,128)(2,1)} %bitcast.299), channel_id=1, source_target_pairs={{0,16},{16,32},{32,48},{48,64},{64,80},{80,96},{96,112},{112,128},... | collective-permute-start | bytes 6291464 | tf_op jit(solution)/shard_map/ppermute | solution.py:14
  127.1 2.9 copy-start.9
  127.1 8.3 %copy-start.8 = (bf16[768,512]{0,1:T(8,128)(2,1)}, bf16[768,512]{0,1:T(8,128)(2,1)S(1)}, u32[]{:S(2)}) copy-start(bf16[768,512]{0,1:T(8,128)(2,1)S(1)} %get-tuple-element.17) | copy-start | bytes 2359300
  127.2 11.8 %copy-start.7 = (bf16[768,512]{0,1:T(8,128)(2,1)}, bf16[768,512]{0,1:T(8,128)(2,1)S(1)}, u32[]{:S(2)}) copy-start(bf16[768,512]{0,1:T(8,128)(2,1)S(1)} %get-tuple-element.18) | copy-start | bytes 2359300
  127.2 15.3 %copy-start.6 = (bf16[768,512]{0,1:T(8,128)(2,1)}, bf16[768,512]{0,1:T(8,128)(2,1)S(1)}, u32[]{:S(2)}) copy-start(bf16[768,512]{0,1:T(8,128)(2,1)S(1)} %get-tuple-element.15) | copy-start | bytes 2359300
  132.6 2.9 copy-start.22
  142.5 4.5 copy-start.20
  142.5 4.5 copy-start.21
  151.8 1.1 copy-start.18
  152.1 4.1 copy-start.25
  156.2 2.8 copy-start.24
  158.1 0.9 copy-start.10
  159.0 2.7 copy-start.17
  164.9 2.9 copy-start.23
  166.9 0.9 copy-start.11
  175.6 0.9 copy-start.12
  177.8 1.7 copy-start.27
  184.6 0.9 copy-start.13
  190.6 137.6 %reduce-scatter.5.cloned.1.call-start = ((), (), s32[]{:S(2)}) async-start(), calls=%async_computation.5 | async-start | bytes 2621440 | tf_op jit(solution)/shard_map/reduce_scatter | solution.py:130
  191.4 26.7 %copy-start.26 = (bf16[128,512]{0,1:T(8,128)(2,1)S(1)}, bf16[128,512]{0,1:T(8,128)(2,1)}, u32[]{:S(2)}) copy-start(bf16[128,512]{0,1:T(8,128)(2,1)} %copy.163) | copy-start | bytes 393220
  191.4 26.7 %collective-permute-start.3 = (bf16[4,128,2048]{1,2,0:T(8,128)(2,1)S(1)}, bf16[4,128,2048]{1,2,0:T(8,128)(2,1)}, u32[]{:S(2)}, u32[]{:S(2)}) collective-permute-start(bf16[4,128,2048]{1,2,0:T(8,128)(2,1)S(1)} %copy_bitcast_fusion), channel_id=1, source_target_pairs={{0,240},{16,0},{32,16},{48,32},{64,48},{80,64},{96,80},{112,96},{1... | collective-permute-start | bytes 6291464 | tf_op jit(solution)/shard_map/ppermute | solution.py:14
  218.1 160.8 %reduce-scatter.11.cloned.1.call-start = ((), (), s32[]{:S(2)}) async-start(), calls=%async_computation.8 | async-start | bytes 2621440 | tf_op jit(solution)/shard_map/reduce_scatter | solution.py:145
  232.3 1.7 copy-start
  232.3 1.8 copy-start.2
  235.9 192.2 %reduce-scatter.9.cloned.1.call-start = ((), (), s32[]{:S(2)}) async-start(), calls=%async_computation.7 | async-start | bytes 2621440 | tf_op jit(solution)/shard_map/reduce_scatter | solution.py:136
  247.4 57.3 %copy-start.34 = (bf16[4,128,128]{2,1,0:T(8,128)(2,1)S(1)}, bf16[4,128,128]{2,1,0:T(8,128)(2,1)}, u32[]{:S(2)}) copy-start(bf16[4,128,128]{2,1,0:T(8,128)(2,1)} %get-tuple-element.42) | copy-start | bytes 393220
  247.4 57.4 %copy-start.35 = (bf16[4,128,128]{2,1,0:T(8,128)(2,1)S(1)}, bf16[4,128,128]{2,1,0:T(8,128)(2,1)}, u32[]{:S(2)}) copy-start(bf16[4,128,128]{2,1,0:T(8,128)(2,1)} %get-tuple-element.44) | copy-start | bytes 393220
  247.4 57.3 %collective-permute-start.4 = (bf16[4,128,2048]{1,2,0:T(8,128)(2,1)}, bf16[4,128,2048]{1,2,0:T(8,128)(2,1)}, u32[]{:S(2)}, u32[]{:S(2)}) collective-permute-start(bf16[4,128,2048]{1,2,0:T(8,128)(2,1)} %copy.189), channel_id=1, source_target_pairs={{0,240},{16,0},{32,16},{48,32},{64,48},{80,64},{96,80},{112,96},{1... | collective-permute-start | bytes 6291464 | tf_op jit(solution)/shard_map/ppermute | solution.py:14
  323.9 1.3 copy-start.1
  323.9 1.6 copy-start.3
  323.9 1.8 copy-start.4
  323.9 2.0 copy-start.5
  325.9 0.9 copy-start.28
  325.9 1.0 copy-start.29
  325.9 1.0 copy-start.30
  325.9 1.1 copy-start.31
  325.9 1.2 copy-start.32
  327.1 1.1 copy-start.15
  327.1 1.6 copy-start.19
  327.1 1.6 copy-start.36
Sparse Core Ops, SparseCore 0:
  10.6 59.3 all-gather.3
  71.8 47.0 all-gather.5
  190.7 80.1 reduce-scatter.6
  273.5 52.6 reduce-scatter.4
  328.6 50.1 reduce-scatter.10
  381.4 46.6 reduce-scatter.8
where the time goes:
time: 515 us; the launch traced here: 514 us
  waiting for transfers between devices  194 us (38%)
  starting transfers between devices  84.1 us (16%)
  blocking collectives  84 us (16%)
  matrix products  66.3 us (13%)
  local copies, waits for them, and re-layouts  54 us (10%)
  between operations  15.9 us (3%)
  other arithmetic  15.3 us (3%)
    ppermute x5, starting transfers between devices, shifted(): return lax.ppermute(value, axis, pairs)  83.8 us
    psum x1, blocking collectives, body(): lax.psum(gain_term, ('outer', 'inner', 'dp')) / math.sqrt(token_count)  75.5 us
    all_gather x1, waiting for transfers between devices, body(): lax.all_gather(keyed, 'inner', axis=0, tiled=True)  58.7 us
    reduce_scatter x1, waiting for transfers between devices, body(): lax.psum_scatter(back_values.astype(jnp.float32).astype(jnp.bfloat16), 'i...  49.3 us
    reduce_scatter x1, waiting for transfers between devices, body(): lax.psum_scatter(slot_values.astype(jnp.bfloat16), 'inner', scatter_dimen...  47.3 us
    all_gather x1, waiting for transfers between devices, body(): lax.all_gather(value_rows, 'inner', axis=0, tiled=True)  23.7 us
    ppermute x5, waiting for transfers between devices, shifted(): return lax.ppermute(value, axis, pairs)  14.1 us
    dot_general x4, matrix products, attend(): jnp.einsum('hqk,qhd->khd', weights_bf, grad_heads, preferred_element_type...  14.1 us
  transfers between devices with their start and end apart: 11, of which 8 were waited for; matrix products, arithmetic and copies ran while one was open for 16% of the time, Pallas kernels for 0%

commit v1 on v0

v1 whole, which is shorter than its diff:
```python
import functools
import math

import jax
import jax.numpy as jnp
from jax import lax
from jax.experimental import pallas as pl
from jax.experimental.pallas import tpu as pltpu
from jax.sharding import PartitionSpec as P

HEAD_DIM = 128
ROWS = 128
SHARDS = 4
ORDER_ROWS = 16
CHUNKS = 2
F32 = jnp.float32
BF16 = jnp.bfloat16


def permuted(value, axis, steps):
    count = lax.axis_size(axis)
    pairs = [(source, (source + steps) % count) for source in range(count)]
    return lax.ppermute(value, axis, pairs)


def vmem_spec():
    return pl.BlockSpec(memory_space=pltpu.VMEM)


def smem_spec():
    return pl.BlockSpec(memory_space=pltpu.SMEM)


def pack_kv_kernel(width, place, keys, values, *outs):
    rows = lax.broadcasted_iota(jnp.int32, (ORDER_ROWS, width), 0)
    numbers = jnp.where(rows < ORDER_ROWS // 2, place[1], place[2]).astype(F32).astype(BF16)
    for k, out in enumerate(outs):
        column = pl.multiple_of(lax.rem(place[0] + k, SHARDS) * width, width)
        out[0:ROWS] = keys[0, :, pl.ds(column, width)]
        out[ROWS : 2 * ROWS] = values[0, :, pl.ds(column, width)]
        out[2 * ROWS :] = numbers


def pack_kv(place, keys, values):
    width = keys.shape[2] // SHARDS
    out = jax.ShapeDtypeStruct((2 * ROWS + ORDER_ROWS, width), BF16)
    return pl.pallas_call(
        functools.partial(pack_kv_kernel, width),
        out_shape=(out,) * SHARDS,
        in_specs=[smem_spec(), vmem_spec(), vmem_spec()],
        out_specs=(vmem_spec(),) * SHARDS,
        name="pack_kv",
    )(place, keys, values)


def pack_qd_kernel(width, scalars, queries, grads, *outs):
    part = width // CHUNKS
    for c in range(CHUNKS):
        for k in range(SHARDS):
            start = lax.rem(scalars[0] + k, SHARDS) * width + c * part
            column = pl.multiple_of(start, part)
            out = outs[c * SHARDS + k]
            out[0:ROWS] = queries[0, :, pl.ds(column, part)]
            out[ROWS:] = grads[0, :, pl.ds(column, part)]


def pack_qd(scalars, queries, grads):
    width = queries.shape[2] // SHARDS
    out = jax.ShapeDtypeStruct((2 * ROWS, width // CHUNKS), BF16)
    return pl.pallas_call(
        functools.partial(pack_qd_kernel, width),
        out_shape=(out,) * (CHUNKS * SHARDS),
        in_specs=[smem_spec(), vmem_spec(), vmem_spec()],
        out_specs=(vmem_spec(),) * (CHUNKS * SHARDS),
        name="pack_qd",
    )(scalars, queries, grads)


def unpack_kernel(width, scalars, *refs):
    count = CHUNKS * SHARDS
    parts, outs = refs[:count], refs[count:]
    part = width // CHUNKS
    for c in range(CHUNKS):
        for k in range(SHARDS):
            start = lax.rem(scalars[0] + k, SHARDS) * width + c * part
            column = pl.multiple_of(start, part)
            for n, out in enumerate(outs):
                rows = parts[c * SHARDS + k][n * ROWS : (n + 1) * ROWS]
                out[0, :, pl.ds(column, part)] = rows


def unpack(scalars, parts, name):
    part = parts[0].shape[1]
    out = jax.ShapeDtypeStruct((1, ROWS, part * CHUNKS * SHARDS), BF16)
    return pl.pallas_call(
        functools.partial(unpack_kernel, part * CHUNKS),
        out_shape=(out, out),
        in_specs=[smem_spec()] + [vmem_spec()] * len(parts),
        out_specs=(vmem_spec(), vmem_spec()),
        name=name,
    )(scalars, *parts)


def dot_nn(a, b):
    return lax.dot_general(a, b, (((1,), (0,)), ((), ())), preferred_element_type=F32)


def dot_nt(a, b):
    return lax.dot_general(a, b, (((1,), (1,)), ((), ())), preferred_element_type=F32)


def attend_kernel(scalars, *refs):
    own_kv, prior_kv, qd = refs[0:4], refs[4:8], refs[8:12]
    gain = refs[12]
    ad_out = refs[13:17]
    own_out, prior_out, gain_out = refs[17:20]
    own, own_t, prior, prior_t, kpos, qpos, q_all, s_all, w_self, w_step, w_prior = refs[20:]
    start = scalars[1]
    group = SHARDS * ROWS
    score_scale = HEAD_DIM ** (-0.5)
    exponent_scale = score_scale * math.log2(math.e)
    half = ROWS // 2
    key_at, value_at = 0, 1
    query_at, grad_at = 0, 1
    weight_at, score_at = 0, 1

    @pl.when(pl.program_id(0) == 0)
    def _():
        lane = lax.broadcasted_iota(jnp.int32, (1, ROWS), 1)
        lanes = jnp.where(lane < half, lane, lane - half).astype(F32)
        row = lax.broadcasted_iota(jnp.int32, (half, ROWS), 0).astype(F32)
        for s, ref in enumerate(tuple(own_kv) + tuple(prior_kv)):
            numbers = ref[2 * ROWS : 2 * ROWS + ORDER_ROWS].astype(F32)
            first = numbers[0:1] * half
            second = numbers[ORDER_ROWS // 2 : ORDER_ROWS // 2 + 1] * half
            kpos[s, 0:half] = row + first
            kpos[s, half:ROWS] = row + second
            if s < SHARDS:
                qpos[s : s + 1] = jnp.where(lane < half, first, second) + lanes

    gain_row = gain[...]
    for s in range(SHARDS):
        rows = slice(s * ROWS, (s + 1) * ROWS)
        for n in (key_at, value_at):
            part = own_kv[s][n * ROWS : (n + 1) * ROWS]
            if n == key_at:
                part = (part.astype(F32) * gain_row).astype(BF16)
            own[n, s] = part
            own_t[n, s] = part.T
            part = prior_kv[s][n * ROWS : (n + 1) * ROWS]
            if n == key_at:
                part = (part.astype(F32) * gain_row).astype(BF16)
            prior[n, rows] = part
            prior_t[n, :, rows] = part.T
        q_all[query_at, s] = qd[s][0:ROWS]
        q_all[grad_at, s] = qd[s][ROWS : 2 * ROWS]
    for n in (0, 1):
        s_all[n] = dot_nt(prior[n], q_all[n].reshape(group, HEAD_DIM))

    for a in range(SHARDS):
        step = lax.rem(start + a, SHARDS)
        cols = slice(a * ROWS, (a + 1) * ROWS)
        query, grad = q_all[query_at, a], q_all[grad_at, a]

        def masked(raw, positions):
            return jnp.where(positions <= qpos[a : a + 1], raw * exponent_scale, -jnp.inf)

        scores = jnp.concatenate(
            [
                masked(dot_nt(own[key_at, a], query), kpos[a]),
                masked(dot_nt(own[key_at, step], query), kpos[step]),
                masked(s_all[0, :, cols], kpos[SHARDS:].reshape(group, ROWS)),
            ],
            axis=0,
        )
        exps = jnp.exp2(scores - jnp.max(scores, axis=0, keepdims=True))
        weights = exps * (1.0 / jnp.sum(exps, axis=0, keepdims=True))
        weights_bf = weights.astype(BF16)
        w_self[weight_at, a] = weights_bf[0:ROWS]
        w_step[weight_at, a] = weights_bf[ROWS : 2 * ROWS]
        w_prior[weight_at, :, cols] = weights_bf[2 * ROWS :]
        attended_t = (
            dot_nn(prior_t[value_at], weights_bf[2 * ROWS :])
            + dot_nn(own_t[value_at, a], weights_bf[0:ROWS])
            + dot_nn(own_t[value_at, step], weights_bf[ROWS : 2 * ROWS])
        )
        ad_out[a][0:ROWS] = attended_t.T.astype(BF16)
        rounded = attended_t.astype(BF16).astype(F32)
        row_dot = jnp.sum(grad.astype(F32).T * rounded, axis=0, keepdims=True)
        weight_grad = jnp.concatenate(
            [
                dot_nt(own[value_at, a], grad),
                dot_nt(own[value_at, step], grad),
                s_all[1, :, cols],
            ],
            axis=0,
        )
        score_grad = (weights * (weight_grad - row_dot)).astype(BF16)
        w_self[score_at, a] = score_grad[0:ROWS]
        w_step[score_at, a] = score_grad[ROWS : 2 * ROWS]
        w_prior[score_at, :, cols] = score_grad[2 * ROWS :]
        query_grad_t = (
            dot_nn(prior_t[key_at], score_grad[2 * ROWS :])
            + dot_nn(own_t[key_at, a], score_grad[0:ROWS])
            + dot_nn(own_t[key_at, step], score_grad[ROWS : 2 * ROWS])
        )
        ad_out[a][ROWS : 2 * ROWS] = (query_grad_t * score_scale).T.astype(BF16)

    gain_sum = jnp.zeros((1, HEAD_DIM), F32)
    queries, grads = (q_all[n].reshape(group, HEAD_DIM) for n in (0, 1))
    prior_key = dot_nn(w_prior[score_at], queries) * score_scale
    prior_value = dot_nn(w_prior[weight_at], grads)
    for s in range(SHARDS):
        key_part = prior_key[s * ROWS : (s + 1) * ROWS]
        prior_out[2 * s * ROWS : (2 * s + 1) * ROWS] = key_part.astype(BF16)
        value_part = prior_value[s * ROWS : (s + 1) * ROWS]
        prior_out[(2 * s + 1) * ROWS : (2 * s + 2) * ROWS] = value_part.astype(BF16)
        raw = prior_kv[s][0:ROWS].astype(F32)
        gain_sum += jnp.sum(key_part * raw, axis=0, keepdims=True)
    for s in range(SHARDS):
        other = lax.rem(s + SHARDS - start, SHARDS)
        key_part = (
            dot_nn(w_self[score_at, s], q_all[query_at, s])
            + dot_nn(w_step[score_at, other], q_all[query_at, other])
        ) * score_scale
        value_part = dot_nn(w_self[weight_at, s], q_all[grad_at, s]) + dot_nn(
            w_step[weight_at, other], q_all[grad_at, other]
        )
        own_out[2 * s * ROWS : (2 * s + 1) * ROWS] = key_part
        own_out[(2 * s + 1) * ROWS : (2 * s + 2) * ROWS] = value_part
        raw = own_kv[s][0:ROWS].astype(F32)
        gain_sum += jnp.sum(key_part * raw, axis=0, keepdims=True)
    gain_out[...] = gain_sum


def attend(scalars, chunk, own_kv, prior_kv, qd, gain_row):
    part = qd[0].shape[1]
    heads = part // HEAD_DIM
    first = chunk * heads
    per_device = CHUNKS * heads
    kv_rows = 2 * ROWS + ORDER_ROWS
    group = SHARDS * ROWS
    kv_spec = pl.BlockSpec((kv_rows, HEAD_DIM), lambda h, sc: (0, first + h))
    qd_spec = pl.BlockSpec((2 * ROWS, HEAD_DIM), lambda h, sc: (0, h))
    gain_spec = pl.BlockSpec((1, HEAD_DIM), lambda h, sc: (0, sc[0] * per_device + first + h))
    wide_spec = pl.BlockSpec((2 * group, HEAD_DIM), lambda h, sc: (0, h))
    row_spec = pl.BlockSpec((1, HEAD_DIM), lambda h, sc: (0, h))
    return pl.pallas_call(
        attend_kernel,
        grid_spec=pltpu.PrefetchScalarGridSpec(
            num_scalar_prefetch=1,
            grid=(heads,),
            in_specs=[kv_spec] * 8 + [qd_spec] * 4 + [gain_spec],
            out_specs=[qd_spec] * 4 + [wide_spec, wide_spec, row_spec],
            scratch_shapes=[
                pltpu.VMEM((2, SHARDS, ROWS, HEAD_DIM), BF16),
                pltpu.VMEM((2, SHARDS, HEAD_DIM, ROWS), BF16),
                pltpu.VMEM((2, group, HEAD_DIM), BF16),
                pltpu.VMEM((2, HEAD_DIM, group), BF16),
                pltpu.VMEM((2 * SHARDS, ROWS, ROWS), F32),
                pltpu.VMEM((8, ROWS), F32),
                pltpu.VMEM((2, SHARDS, ROWS, HEAD_DIM), BF16),
                pltpu.VMEM((2, group, group), F32),
                pltpu.VMEM((2, SHARDS, ROWS, ROWS), BF16),
                pltpu.VMEM((2, SHARDS, ROWS, ROWS), BF16),
                pltpu.VMEM((2, group, group), BF16),
            ],
        ),
        out_shape=(jax.ShapeDtypeStruct((2 * ROWS, part), BF16),) * 4
        + (
            jax.ShapeDtypeStruct((2 * group, part), F32),
            jax.ShapeDtypeStruct((2 * group, part), BF16),
            jax.ShapeDtypeStruct((1, part), F32),
        ),
        compiler_params=pltpu.CompilerParams(
            dimension_semantics=("arbitrary",), vmem_limit_bytes=32 * 1024 * 1024
        ),
        cost_estimate=pl.CostEstimate(
            flops=heads * 12 * group * (group + 2 * ROWS) * HEAD_DIM,
            bytes_accessed=heads * 14 * group * HEAD_DIM * 2,
            transcendentals=heads * group * (group + 2 * ROWS),
        ),
        name="attend",
    )(scalars, *own_kv, *prior_kv, *qd, gain_row)


def finish_kernel(scalars, own, back, gain, *outs):
    gain_row = gain[...]
    for s in range(SHARDS):
        rows = pl.ds(2 * s * ROWS, ROWS)
        total = own[rows] + back[rows].astype(F32)
        outs[s][0:ROWS] = (total * gain_row).astype(BF16)
        rows = pl.ds((2 * s + 1) * ROWS, ROWS)
        outs[s][ROWS : 2 * ROWS] = (own[rows] + back[rows].astype(F32)).astype(BF16)


def finish(scalars, chunk, own, back, gain_row):
    part = own.shape[1]
    heads = part // HEAD_DIM
    width = 2 * HEAD_DIM if heads % 2 == 0 else HEAD_DIM
    steps = part // width
    group = SHARDS * ROWS
    wide_spec = pl.BlockSpec((2 * group, width), lambda h, sc: (0, h))
    gain_spec = pl.BlockSpec((1, width), lambda h, sc: (0, (sc[0] * CHUNKS + chunk) * steps + h))
    out_spec = pl.BlockSpec((2 * ROWS, width), lambda h, sc: (0, h))
    return pl.pallas_call(
        finish_kernel,
        grid_spec=pltpu.PrefetchScalarGridSpec(
            num_scalar_prefetch=1,
            grid=(steps,),
            in_specs=[wide_spec, wide_spec, gain_spec],
            out_specs=[out_spec] * SHARDS,
        ),
        out_shape=(jax.ShapeDtypeStruct((2 * ROWS, part), BF16),) * SHARDS,
        compiler_params=pltpu.CompilerParams(
            dimension_semantics=("arbitrary",), vmem_limit_bytes=32 * 1024 * 1024
        ),
        cost_estimate=pl.CostEstimate(
            flops=4 * group * part, bytes_accessed=16 * group * part, transcendentals=0
        ),
        name="finish",
    )(scalars, own, back, gain_row)


def sum_of_four(value, axis, stride):
    return value + (
        permuted(value, axis, stride)
        + permuted(value, axis, 2 * stride)
        + permuted(value, axis, 3 * stride)
    )


def body(queries, keys, values, out_grad, gain, block_order, start):
    inner = lax.axis_index("inner").astype(jnp.int32)
    place = jnp.stack([inner, block_order[0], block_order[1]])
    scalars = jnp.stack([inner, start[0]])
    gain_row = gain[None]

    kv = pack_kv(place, keys, values)
    own_kv = [kv[0]] + [permuted(kv[k], "inner", k) for k in range(1, SHARDS)]
    packed = pack_qd(scalars, queries, out_grad)
    prior_kv = [permuted(part, "outer", 1) for part in own_kv]
    ad_parts, dkv_parts, gain_terms = [], [], []
    for c in range(CHUNKS):
        mine = packed[c * SHARDS : (c + 1) * SHARDS]
        qd = [mine[0]] + [permuted(mine[k], "inner", k) for k in range(1, SHARDS)]
        results = attend(scalars, c, own_kv, prior_kv, qd, gain_row)
        ad, (own, prior, gain_term) = results[:SHARDS], results[SHARDS:]
        gain_terms.append(gain_term)
        ad_parts += [ad[0]] + [permuted(ad[k], "inner", -k) for k in range(1, SHARDS)]
        back = permuted(prior, "outer", -1)
        dkv = finish(scalars, c, own, back, gain_row)
        dkv_parts += [dkv[0]] + [permuted(dkv[k], "inner", -k) for k in range(1, SHARDS)]
    attended, query_grad = unpack(scalars, ad_parts, "unpack_ad")
    key_grad, value_grad = unpack(scalars, dkv_parts, "unpack_dkv")

    term = jnp.concatenate(gain_terms, axis=1)
    term = sum_of_four(term, "dp", 1)
    term = sum_of_four(term, "outer", 4)
    term = sum_of_four(term, "outer", 1)
    terms = jnp.concatenate([term] + [permuted(term, "inner", -k) for k in range(1, SHARDS)])
    terms = jnp.roll(terms, inner, axis=0)
    token_count = (
        ROWS * lax.axis_size("inner") * lax.axis_size("outer") * lax.axis_size("dp")
    )
    gain_grad = terms.reshape(-1) / math.sqrt(token_count)
    return attended, query_grad, key_grad, value_grad, gain_grad


def solution(mesh):
    rows = P("dp", ("outer", "inner"), None)
    in_specs = (rows, rows, rows, rows, P(), P(("outer", "inner")), P())
    out_specs = (rows, rows, rows, rows, P())
    return jax.shard_map(body, mesh=mesh, in_specs=in_specs, out_specs=out_specs, check_vma=False)
```

time: 515 us -> 184 us (0.36)
  waiting for transfers between devices: 194 us -> 47 us
  blocking collectives: 84 us -> 0 us
  matrix products: 66.3 us -> 0 us
  local copies, waits for them, and re-layouts: 54 us -> 4.74 us
  Pallas kernels: 0 us -> 28.1 us
  starting transfers between devices: 84.1 us -> 98.5 us
  between operations: 15.9 us -> 1.59 us
  other arithmetic: 15.3 us -> 1.24 us
    reduce_scatter x4 -> x0, waiting for transfers between devices: 96.6 us -> none  [the longest x1 49.3 us: body(): lax.psum_scatter(back_values.astype(jnp.float32).astype(jnp.bfloat16), 'i...]
    all_gather x2 -> x0, waiting for transfers between devices: 82.4 us -> none  [the longest x1 58.7 us: body(): lax.all_gather(keyed, 'inner', axis=0, tiled=True)]
    psum x1 -> x0, blocking collectives: 75.5 us -> none  [body(): lax.psum(gain_term, ('outer', 'inner', 'dp')) / math.sqrt(token_count)]
    dot_general x24 -> x0, matrix products: 56.8 us -> none  [the longest x4 14.1 us: attend(): jnp.einsum('hqk,qhd->khd', weights_bf, grad_heads, preferred_element_type...]
    ppermute x5 -> x39, waiting for transfers between devices: 14.1 us -> 47 us  [permuted(): return lax.ppermute(value, axis, pairs)]
    pallas_call x0 -> x8, Pallas kernels: none -> 28.1 us  [the longest x2 17.4 us: attend(): pl.pallas_call(attend_kernel, grid_spec=pltpu.PrefetchScalarGridSpec(num_...]
    ppermute x5 -> x39, starting transfers between devices: 83.8 us -> 98.5 us  [permuted(): return lax.ppermute(value, axis, pairs)]
    slice x14 -> x0, local copies, waits for them, and re-layouts: 14.1 us -> none  [the longest x2 5.47 us: body(): value_round[2 * local_rows:].reshape(inner_count, local_rows, channels)]
  transfers between devices with their start and end apart: 11 -> 39, of which waited for: 8 -> 12; matrix products, arithmetic and copies ran while one was open for 16% -> 1% of each run, Pallas kernels for 0% -> 8%
where the time goes in v1:
time: 184 us; the launch traced here: 181 us
  starting transfers between devices  98.5 us (54%)
  waiting for transfers between devices  47 us (26%)
  Pallas kernels  28.1 us (15%)
  local copies, waits for them, and re-layouts  4.74 us (3%)
    ppermute x39, starting transfers between devices, permuted(): return lax.ppermute(value, axis, pairs)  98.5 us
    ppermute x39, waiting for transfers between devices, permuted(): return lax.ppermute(value, axis, pairs)  47 us
    pallas_call x2, Pallas kernels, attend(): pl.pallas_call(attend_kernel, grid_spec=pltpu.PrefetchScalarGridSpec(num_...  17.4 us
    unnamed x46, local copies, waits for them, and re-layouts  4.69 us
    pallas_call x2, Pallas kernels, unpack(): pl.pallas_call(functools.partial(unpack_kernel, part * CHUNKS), out_shape...  4.68 us
  transfers between devices with their start and end apart: 39, of which 12 were waited for; matrix products, arithmetic and copies ran while one was open for 1% of the time, Pallas kernels for 8%

profile of v1, /device:TPU:1, one launch (start us, length us, event | category | flops | bytes accessed | tf_op | source)
XLA Modules:
  0.0 181.2 jit_solution(15711366878375420182)
XLA Ops:
  0.6 0.6 copy-done.21
  1.3 0.7 pad_add_fusion.1.place
  1.9 2.3 %pack_kv.1 = (bf16[272,512]{1,0:T(8,128)(2,1)}, bf16[272,512]{1,0:T(8,128)(2,1)}, bf16[272,512]{1,0:T(8,128)(2,1)}, bf16[272,512]{1,0:T(8,128)(2,1)}) custom-call(s32[3]{0:T(128)} %pad_add_fusion.1.place, bf16[1,128,2048]{2,1,0:T(8,128)(2,1)} %keys.1, bf16[1,128,2048]{2,1,0:T(8,128)(2,1)} %values.1), custom_call_target="tpu_custom_call" | custom-call | tf_op jit(solution)/shard_map/pack_kv/pallas_call | solution.py:47
  4.2 3.8 %collective-permute-start = (bf16[272,512]{1,0:T(8,128)(2,1)}, bf16[272,512]{1,0:T(8,128)(2,1)S(1)}, u32[]{:S(2)}, u32[]{:S(2)}) collective-permute-start(bf16[272,512]{1,0:T(8,128)(2,1)} %get-tuple-element.44), channel_id=1, source_target_pairs={{0,4},{4,8},{8,12},{12,0},{1,5},{5,9},{9,13},{13,1},{2,6},{6,10},{... | collective-permute-start | bytes 835592 | tf_op jit(solution)/shard_map/ppermute | solution.py:23
  8.0 5.1 %collective-permute-start.1 = (bf16[272,512]{1,0:T(8,128)(2,1)}, bf16[272,512]{1,0:T(8,128)(2,1)S(1)}, u32[]{:S(2)}, u32[]{:S(2)}) collective-permute-start(bf16[272,512]{1,0:T(8,128)(2,1)} %get-tuple-element.45), channel_id=1, source_target_pairs={{0,8},{4,12},{8,0},{12,4},{1,9},{5,13},{9,1},{13,5},{2,10},{6,14},... | collective-permute-start | bytes 835592 | tf_op jit(solution)/shard_map/ppermute | solution.py:23
  13.2 2.4 %collective-permute-start.2 = (bf16[272,512]{1,0:T(8,128)(2,1)}, bf16[272,512]{1,0:T(8,128)(2,1)S(1)}, u32[]{:S(2)}, u32[]{:S(2)}) collective-permute-start(bf16[272,512]{1,0:T(8,128)(2,1)} %get-tuple-element.46), channel_id=1, source_target_pairs={{0,12},{4,0},{8,4},{12,8},{1,13},{5,1},{9,5},{13,9},{2,14},{6,2},{... | collective-permute-start | bytes 835592 | tf_op jit(solution)/shard_map/ppermute | solution.py:23
  16.2 0.6 pad_add_fusion.scalars
  16.8 2.4 %pack_qd.1 = (bf16[256,256]{1,0:T(8,128)(2,1)}, bf16[256,256]{1,0:T(8,128)(2,1)}, bf16[256,256]{1,0:T(8,128)(2,1)}, bf16[256,256]{1,0:T(8,128)(2,1)}, bf16[256,2...) custom-call(s32[2]{0:T(128)} %pad_add_fusion.scalars, ...), custom_call_target="tpu_custom_call" | custom-call | tf_op jit(solution)/shard_map/pack_qd/pallas_call | solution.py:70
  19.2 0.0 collective-permute-start.7
  19.2 2.9 %collective-permute-start.3 = (bf16[272,512]{1,0:T(8,128)(2,1)S(1)}, bf16[272,512]{1,0:T(8,128)(2,1)S(1)}, u32[]{:S(2)}, u32[]{:S(2)}) collective-permute-start(bf16[272,512]{1,0:T(8,128)(2,1)S(1)} %copy-done.6), channel_id=1, source_target_pairs={{0,16},{16,32},{32,48},{48,64},{64,80},{80,96},{96,112},{112,128},... | collective-permute-start | bytes 835592 | tf_op jit(solution)/shard_map/ppermute | solution.py:23
  22.1 2.1 %collective-permute-start.4 = (bf16[272,512]{1,0:T(8,128)(2,1)S(1)}, bf16[272,512]{1,0:T(8,128)(2,1)S(1)}, u32[]{:S(2)}, u32[]{:S(2)}) collective-permute-start(bf16[272,512]{1,0:T(8,128)(2,1)S(1)} %collective-permute-done.refs_1_), channel_id=1, source_target_pairs={{0,16},{16,32},{32,48},{48,64},{64,80},{80,96},{96,112},{112,128},... | collective-permute-start | bytes 835592 | tf_op jit(solution)/shard_map/ppermute | solution.py:23
  24.2 5.6 %collective-permute-done.1.refs_2_ = bf16[272,512]{1,0:T(8,128)(2,1)S(1)} collective-permute-done((bf16[272,512]{1,0:T(8,128)(2,1)}, bf16[272,512]{1,0:T(8,128)(2,1)S(1)}, u32[]{:S(2)}, u32[]{:S(2)}) %collective-permute-start.1) | collective-permute-done | bytes 278560 | tf_op jit(solution)/shard_map/ppermute | solution.py:23
  29.8 5.3 %collective-permute-start.5 = (bf16[272,512]{1,0:T(8,128)(2,1)S(1)}, bf16[272,512]{1,0:T(8,128)(2,1)S(1)}, u32[]{:S(2)}, u32[]{:S(2)}) collective-permute-start(bf16[272,512]{1,0:T(8,128)(2,1)S(1)} %collective-permute-done.1.refs_2_), channel_id=1, source_target_pairs={{0,16},{16,32},{32,48},{48,64},{64,80},{80,96},{96,112},{112,128},... | collective-permute-start | bytes 835592 | tf_op jit(solution)/shard_map/ppermute | solution.py:23
  35.1 3.8 %collective-permute-done.2.refs_3_ = bf16[272,512]{1,0:T(8,128)(2,1)S(1)} collective-permute-done((bf16[272,512]{1,0:T(8,128)(2,1)}, bf16[272,512]{1,0:T(8,128)(2,1)S(1)}, u32[]{:S(2)}, u32[]{:S(2)}) %collective-permute-start.2) | collective-permute-done | bytes 278560 | tf_op jit(solution)/shard_map/ppermute | solution.py:23
  38.9 1.7 collective-permute-start.6
  40.6 5.2 %collective-permute-start.8 = (bf16[256,256]{1,0:T(8,128)(2,1)}, bf16[256,256]{1,0:T(8,128)(2,1)S(1)}, u32[]{:S(2)}, u32[]{:S(2)}) collective-permute-start(bf16[256,256]{1,0:T(8,128)(2,1)} %get-tuple-element.49), channel_id=1, source_target_pairs={{0,8},{4,12},{8,0},{12,4},{1,9},{5,13},{9,1},{13,5},{2,10},{6,14},... | collective-permute-start | bytes 393224 | tf_op jit(solution)/shard_map/ppermute | solution.py:23
  45.8 2.8 %collective-permute-done.8.refs_10_ = bf16[256,256]{1,0:T(8,128)(2,1)S(1)} collective-permute-done((bf16[256,256]{1,0:T(8,128)(2,1)}, bf16[256,256]{1,0:T(8,128)(2,1)S(1)}, u32[]{:S(2)}, u32[]{:S(2)}) %collective-permute-start.8) | collective-permute-done | bytes 131104 | tf_op jit(solution)/shard_map/ppermute | solution.py:23
  48.6 7.8 %collective-permute-start.9 = (bf16[256,256]{1,0:T(8,128)(2,1)}, bf16[256,256]{1,0:T(8,128)(2,1)S(1)}, u32[]{:S(2)}, u32[]{:S(2)}) collective-permute-start(bf16[256,256]{1,0:T(8,128)(2,1)} %get-tuple-element.50), channel_id=1, source_target_pairs={{0,12},{4,0},{8,4},{12,8},{1,13},{5,1},{9,5},{13,9},{2,14},{6,2},{... | collective-permute-start | bytes 393224 | tf_op jit(solution)/shard_map/ppermute | solution.py:23
  56.5 3.6 %collective-permute-done.9.refs_11_ = bf16[256,256]{1,0:T(8,128)(2,1)S(1)} collective-permute-done((bf16[256,256]{1,0:T(8,128)(2,1)}, bf16[256,256]{1,0:T(8,128)(2,1)S(1)}, u32[]{:S(2)}, u32[]{:S(2)}) %collective-permute-start.9) | collective-permute-done | bytes 131104 | tf_op jit(solution)/shard_map/ppermute | solution.py:23
  60.1 1.7 collective-permute-start.13
  61.8 4.7 %collective-permute-start.14 = (bf16[256,256]{1,0:T(8,128)(2,1)}, bf16[256,256]{1,0:T(8,128)(2,1)S(1)}, u32[]{:S(2)}, u32[]{:S(2)}) collective-permute-start(bf16[256,256]{1,0:T(8,128)(2,1)} %get-tuple-element.57), channel_id=1, source_target_pairs={{0,8},{4,12},{8,0},{12,4},{1,9},{5,13},{9,1},{13,5},{2,10},{6,14},... | collective-permute-start | bytes 393224 | tf_op jit(solution)/shard_map/ppermute | solution.py:23
  66.5 1.0 collective-permute-start.15
  67.5 0.6 copy-done.5
  68.1 0.9 copy-done.8
  69.0 8.7 %attend.2 = (bf16[256,256]{1,0:T(8,128)(2,1)S(1)}, bf16[256,256]{1,0:T(8,128)(2,1)S(1)}, bf16[256,256]{1,0:T(8,128)(2,1)S(1)}, bf16[256,256]{1,0:T(8,128)(2,1)S(...) custom-call(s32[2]{0:T(128)S(1)} %copy-done.5, bf16[272,512]{1,0:T(8,128)(2,1)S(1)} %copy-done.6, ...), custom_call_target="tpu_custom_call" | custom-call | flops 1207959552 | bytes 3670016 | tf_op jit(solution)/shard_map/attend/pallas_call | solution.py:248
  77.7 0.6 copy-done
  78.4 8.7 %attend.3 = (bf16[256,256]{1,0:T(8,128)(2,1)S(1)}, bf16[256,256]{1,0:T(8,128)(2,1)S(1)}, bf16[256,256]{1,0:T(8,128)(2,1)S(1)}, bf16[256,256]{1,0:T(8,128)(2,1)S(...) custom-call(s32[2]{0:T(128)S(1)} %copy-done.5, bf16[272,512]{1,0:T(8,128)(2,1)S(1)} %copy-done.6, ...), custom_call_target="tpu_custom_call" | custom-call | flops 1207959552 | bytes 3670016 | tf_op jit(solution)/shard_map/attend/pallas_call | solution.py:248
  87.1 2.6 %collective-permute-start.29 = (f32[1,512]{1,0:T(1,128)S(1)}, f32[1,512]{1,0:T(1,128)S(1)}, u32[]{:S(2)}, u32[]{:S(2)}) collective-permute-start(f32[1,512]{1,0:T(1,128)S(1)} %constant_dynamic-update-slice_fusion), channel_id=1, source_target_pairs={{0,3},{1,0},{2,1},{3,2},{4,7},{5,4},{6,5},{7,6},{8,11},{9,8},{10,9... | collective-permute-start | bytes 6152 | tf_op jit(solution)/shard_map/ppermute | solution.py:23
  89.7 0.5 collective-permute-start.28
  90.2 0.6 collective-permute-start.27
  90.8 2.3 %collective-permute-start.23 = (bf16[1024,256]{1,0:T(8,128)(2,1)S(1)}, bf16[1024,256]{1,0:T(8,128)(2,1)S(1)}, u32[]{:S(2)}, u32[]{:S(2)}) collective-permute-start(bf16[1024,256]{1,0:T(8,128)(2,1)S(1)} %get-tuple-element.72), channel_id=1, source_target_pairs={{0,240},{16,0},{32,16},{48,32},{64,48},{80,64},{96,80},{112,96},{1... | collective-permute-start | bytes 1572872 | tf_op jit(solution)/shard_map/ppermute | solution.py:23
  93.1 4.3 %collective-permute-start.19 = (bf16[1024,256]{1,0:T(8,128)(2,1)S(1)}, bf16[1024,256]{1,0:T(8,128)(2,1)S(1)}, u32[]{:S(2)}, u32[]{:S(2)}) collective-permute-start(bf16[1024,256]{1,0:T(8,128)(2,1)S(1)} %get-tuple-element.66), channel_id=1, source_target_pairs={{0,240},{16,0},{32,16},{48,32},{64,48},{80,64},{96,80},{112,96},{1... | collective-permute-start | bytes 1572872 | tf_op jit(solution)/shard_map/ppermute | solution.py:23
  97.4 0.2 collective-permute-start.32
  97.6 2.6 %collective-permute-start.31 = (f32[1,512]{1,0:T(1,128)S(1)}, f32[1,512]{1,0:T(1,128)S(1)}, u32[]{:S(2)}, u32[]{:S(2)}) collective-permute-start(f32[1,512]{1,0:T(1,128)S(1)} %add_add_fusion.2), channel_id=1, source_target_pairs={{0,128},{16,144},{32,160},{48,176},{64,192},{80,208},{96,224},{112... | collective-permute-start | bytes 6152 | tf_op jit(solution)/shard_map/ppermute | solution.py:23
  100.1 2.9 %collective-permute-start.30 = (f32[1,512]{1,0:T(1,128)S(1)}, f32[1,512]{1,0:T(1,128)S(1)}, u32[]{:S(2)}, u32[]{:S(2)}) collective-permute-start(f32[1,512]{1,0:T(1,128)S(1)} %add_add_fusion.2), channel_id=1, source_target_pairs={{0,64},{16,80},{32,96},{48,112},{64,128},{80,144},{96,160},{112,17... | collective-permute-start | bytes 6152 | tf_op jit(solution)/shard_map/ppermute | solution.py:23
  103.0 2.0 %collective-permute-done.30 = f32[1,512]{1,0:T(1,128)S(1)} collective-permute-done((f32[1,512]{1,0:T(1,128)S(1)}, f32[1,512]{1,0:T(1,128)S(1)}, u32[]{:S(2)}, u32[]{:S(2)}) %collective-permute-start.30) | collective-permute-done | bytes 2080 | tf_op jit(solution)/shard_map/ppermute | solution.py:23
  105.0 10.7 %collective-permute-start.35 = (f32[1,512]{1,0:T(1,128)S(1)}, f32[1,512]{1,0:T(1,128)S(1)}, u32[]{:S(2)}, u32[]{:S(2)}) collective-permute-start(f32[1,512]{1,0:T(1,128)S(1)} %add_add_fusion.1), channel_id=1, source_target_pairs={{0,48},{16,64},{32,80},{48,96},{64,112},{80,128},{96,144},{112,160... | collective-permute-start | bytes 6152 | tf_op jit(solution)/shard_map/ppermute | solution.py:23
  115.7 0.0 collective-permute-start.33
  115.8 0.7 collective-permute-done.35
  116.5 0.4 collective-permute-start.16
  116.9 3.4 %collective-permute-done.34 = f32[1,512]{1,0:T(1,128)S(1)} collective-permute-done((f32[1,512]{1,0:T(1,128)S(1)}, f32[1,512]{1,0:T(1,128)S(1)}, u32[]{:S(2)}, u32[]{:S(2)}) %collective-permute-start.34) | collective-permute-done | bytes 2080 | tf_op jit(solution)/shard_map/ppermute | solution.py:23
  120.3 3.1 %collective-permute-start.17 = (bf16[256,256]{1,0:T(8,128)(2,1)S(1)}, bf16[256,256]{1,0:T(8,128)(2,1)S(1)}, u32[]{:S(2)}, u32[]{:S(2)}) collective-permute-start(bf16[256,256]{1,0:T(8,128)(2,1)S(1)} %get-tuple-element.61), channel_id=1, source_target_pairs={{0,8},{4,12},{8,0},{12,4},{1,9},{5,13},{9,1},{13,5},{2,10},{6,14},... | collective-permute-start | bytes 393224 | tf_op jit(solution)/shard_map/ppermute | solution.py:23
  123.4 0.1 collective-permute-start.38
  123.5 8.1 %collective-permute-done.38 = f32[1,512]{1,0:T(1,128)S(1)} collective-permute-done((f32[1,512]{1,0:T(1,128)S(1)}, f32[1,512]{1,0:T(1,128)S(1)}, u32[]{:S(2)}, u32[]{:S(2)}) %collective-permute-start.38) | collective-permute-done | bytes 2080 | tf_op jit(solution)/shard_map/ppermute | solution.py:23
  131.7 0.5 collective-permute-start.36
  132.2 0.6 finish.3
  132.9 5.1 %collective-permute-done.37 = f32[1,512]{1,0:T(1,128)S(1)} collective-permute-done((f32[1,512]{1,0:T(1,128)S(1)}, f32[1,512]{1,0:T(1,128)S(1)}, u32[]{:S(2)}, u32[]{:S(2)}) %collective-permute-start.37) | collective-permute-done | bytes 2080 | tf_op jit(solution)/shard_map/ppermute | solution.py:23
  138.0 3.6 %collective-permute-start.10 = (bf16[256,256]{1,0:T(8,128)(2,1)S(1)}, bf16[256,256]{1,0:T(8,128)(2,1)S(1)}, u32[]{:S(2)}, u32[]{:S(2)}) collective-permute-start(bf16[256,256]{1,0:T(8,128)(2,1)S(1)} %get-tuple-element.52), channel_id=1, source_target_pairs={{0,12},{4,0},{8,4},{12,8},{1,13},{5,1},{9,5},{13,9},{2,14},{6,2},{... | collective-permute-start | bytes 393224 | tf_op jit(solution)/shard_map/ppermute | solution.py:23
  141.6 0.7 collective-permute-start.11
  142.3 1.5 collective-permute-start.12
  143.8 2.1 %collective-permute-start.24 = (bf16[256,256]{1,0:T(8,128)(2,1)S(1)}, bf16[256,256]{1,0:T(8,128)(2,1)S(1)}, u32[]{:S(2)}, u32[]{:S(2)}) collective-permute-start(bf16[256,256]{1,0:T(8,128)(2,1)S(1)} %get-tuple-element.74), channel_id=1, source_target_pairs={{0,12},{4,0},{8,4},{12,8},{1,13},{5,1},{9,5},{13,9},{2,14},{6,2},{... | collective-permute-start | bytes 393224 | tf_op jit(solution)/shard_map/ppermute | solution.py:23
  145.9 0.7 finish.2
  146.6 0.6 copy-done.3
  147.2 4.7 %collective-permute-start.25 = (bf16[256,256]{1,0:T(8,128)(2,1)S(1)}, bf16[256,256]{1,0:T(8,128)(2,1)S(1)}, u32[]{:S(2)}, u32[]{:S(2)}) collective-permute-start(bf16[256,256]{1,0:T(8,128)(2,1)S(1)} %get-tuple-element.75), channel_id=1, source_target_pairs={{0,8},{4,12},{8,0},{12,4},{1,9},{5,13},{9,1},{13,5},{2,10},{6,14},... | collective-permute-start | bytes 393224 | tf_op jit(solution)/shard_map/ppermute | solution.py:23
  151.9 4.6 %collective-permute-done.10.refs_1_ = bf16[256,256]{1,0:T(8,128)(2,1)S(1)} collective-permute-done((bf16[256,256]{1,0:T(8,128)(2,1)S(1)}, bf16[256,256]{1,0:T(8,128)(2,1)S(1)}, u32[]{:S(2)}, u32[]{:S(2)}) %collective-permute-start.10) | collective-permute-done | bytes 131104 | tf_op jit(solution)/shard_map/ppermute | solution.py:23
  156.5 6.0 %collective-permute-start.26 = (bf16[256,256]{1,0:T(8,128)(2,1)S(1)}, bf16[256,256]{1,0:T(8,128)(2,1)S(1)}, u32[]{:S(2)}, u32[]{:S(2)}) collective-permute-start(bf16[256,256]{1,0:T(8,128)(2,1)S(1)} %get-tuple-element.76), channel_id=1, source_target_pairs={{0,4},{4,8},{8,12},{12,0},{1,5},{5,9},{9,13},{13,1},{2,6},{6,10},{... | collective-permute-start | bytes 393224 | tf_op jit(solution)/shard_map/ppermute | solution.py:23
  162.5 3.5 %collective-permute-start.21 = (bf16[256,256]{1,0:T(8,128)(2,1)S(1)}, bf16[256,256]{1,0:T(8,128)(2,1)S(1)}, u32[]{:S(2)}, u32[]{:S(2)}) collective-permute-start(bf16[256,256]{1,0:T(8,128)(2,1)S(1)} %get-tuple-element.69), channel_id=1, source_target_pairs={{0,8},{4,12},{8,0},{12,4},{1,9},{5,13},{9,1},{13,5},{2,10},{6,14},... | collective-permute-start | bytes 393224 | tf_op jit(solution)/shard_map/ppermute | solution.py:23
  166.0 2.0 %collective-permute-start.22 = (bf16[256,256]{1,0:T(8,128)(2,1)S(1)}, bf16[256,256]{1,0:T(8,128)(2,1)S(1)}, u32[]{:S(2)}, u32[]{:S(2)}) collective-permute-start(bf16[256,256]{1,0:T(8,128)(2,1)S(1)} %get-tuple-element.70), channel_id=1, source_target_pairs={{0,4},{4,8},{8,12},{12,0},{1,5},{5,9},{9,13},{13,1},{2,6},{6,10},{... | collective-permute-start | bytes 393224 | tf_op jit(solution)/shard_map/ppermute | solution.py:23
  168.1 0.6 copy.12
  168.7 2.3 %unpack_ad.1 = (bf16[1,128,2048]{2,1,0:T(8,128)(2,1)}, bf16[1,128,2048]{2,1,0:T(8,128)(2,1)}) custom-call(s32[2]{0:T(128)} %pad_add_fusion.scalars, bf16[256,256]{1,0:T(8,128)(2,1)} %copy-done, bf16[256,256]{1,0:T(8,128)(2,1)} %copy-done.13, bf16[256,256]{1,0:T(8,128)(2,1)} %copy-done.14, bf16[256,256]{1,0:T(8,128)(2,1)} %copy-done.16, ...), custom_call_target="tpu_custom_call" | custom-call | tf_op jit(solution)/shard_map/unpack_ad/pallas_call | solution.py:95
  171.1 2.6 %collective-permute-done.21.refs_2_ = bf16[256,256]{1,0:T(8,128)(2,1)S(1)} collective-permute-done((bf16[256,256]{1,0:T(8,128)(2,1)S(1)}, bf16[256,256]{1,0:T(8,128)(2,1)S(1)}, u32[]{:S(2)}, u32[]{:S(2)}) %collective-permute-start.21) | collective-permute-done | bytes 131104 | tf_op jit(solution)/shard_map/ppermute | solution.py:23
  173.7 4.6 %collective-permute-done.22.refs_3_ = bf16[256,256]{1,0:T(8,128)(2,1)S(1)} collective-permute-done((bf16[256,256]{1,0:T(8,128)(2,1)S(1)}, bf16[256,256]{1,0:T(8,128)(2,1)S(1)}, u32[]{:S(2)}, u32[]{:S(2)}) %collective-permute-start.22) | collective-permute-done | bytes 131104 | tf_op jit(solution)/shard_map/ppermute | solution.py:23
  178.2 0.6 copy-done.20
  178.9 2.3 %unpack_dkv.1 = (bf16[1,128,2048]{2,1,0:T(8,128)(2,1)}, bf16[1,128,2048]{2,1,0:T(8,128)(2,1)}) custom-call(s32[2]{0:T(128)} %pad_add_fusion.scalars, bf16[256,256]{1,0:T(8,128)(2,1)} %copy-done.3, bf16[256,256]{1,0:T(8,128)(2,1)} %copy-done.18, bf16[256,256]{1,0:T(8,128)(2,1)} %copy-done.19, bf16[256,256]{1,0:T(8,128)(2,1)} %copy-done.20, ...), custom_call_target="tpu_custom_call" | custom-call | tf_op jit(solution)/shard_map/unpack_dkv/pallas_call | solution.py:95
  (76 shorter events, 0.2 us)
Async XLA Ops:
  0.6 0.7 copy-start.21
  4.2 17.9 %collective-permute-start = (bf16[272,512]{1,0:T(8,128)(2,1)}, bf16[272,512]{1,0:T(8,128)(2,1)S(1)}, u32[]{:S(2)}, u32[]{:S(2)}) collective-permute-start(bf16[272,512]{1,0:T(8,128)(2,1)} %get-tuple-element.44), channel_id=1, source_target_pairs={{0,4},{4,8},{8,12},{12,0},{1,5},{5,9},{9,13},{13,1},{2,6},{6,10},{... | collective-permute-start | bytes 835592 | tf_op jit(solution)/shard_map/ppermute | solution.py:23
  8.0 21.8 %collective-permute-start.1 = (bf16[272,512]{1,0:T(8,128)(2,1)}, bf16[272,512]{1,0:T(8,128)(2,1)S(1)}, u32[]{:S(2)}, u32[]{:S(2)}) collective-permute-start(bf16[272,512]{1,0:T(8,128)(2,1)} %get-tuple-element.45), channel_id=1, source_target_pairs={{0,8},{4,12},{8,0},{12,4},{1,9},{5,13},{9,1},{13,5},{2,10},{6,14},... | collective-permute-start | bytes 835592 | tf_op jit(solution)/shard_map/ppermute | solution.py:23
  13.2 25.8 %collective-permute-start.2 = (bf16[272,512]{1,0:T(8,128)(2,1)}, bf16[272,512]{1,0:T(8,128)(2,1)S(1)}, u32[]{:S(2)}, u32[]{:S(2)}) collective-permute-start(bf16[272,512]{1,0:T(8,128)(2,1)} %get-tuple-element.46), channel_id=1, source_target_pairs={{0,12},{4,0},{8,4},{12,8},{1,13},{5,1},{9,5},{13,9},{2,14},{6,2},{... | collective-permute-start | bytes 835592 | tf_op jit(solution)/shard_map/ppermute | solution.py:23
  16.7 2.4 %copy-start.6 = (bf16[272,512]{1,0:T(8,128)(2,1)S(1)}, bf16[272,512]{1,0:T(8,128)(2,1)}, u32[]{:S(2)}) copy-start(bf16[272,512]{1,0:T(8,128)(2,1)} %get-tuple-element.43.refs_0_) | copy-start | bytes 835588
  19.2 48.3 %copy-start.4 = (f32[2048]{0:T(1024)S(1)}, f32[2048]{0:T(1024)}, u32[]{:S(2)}) copy-start(f32[2048]{0:T(1024)} %param.11) | copy-start | bytes 24580
  19.2 21.4 %collective-permute-start.7 = (bf16[256,256]{1,0:T(8,128)(2,1)}, bf16[256,256]{1,0:T(8,128)(2,1)S(1)}, u32[]{:S(2)}, u32[]{:S(2)}) collective-permute-start(bf16[256,256]{1,0:T(8,128)(2,1)} %get-tuple-element.48), channel_id=1, source_target_pairs={{0,4},{4,8},{8,12},{12,0},{1,5},{5,9},{9,13},{13,1},{2,6},{6,10},{... | collective-permute-start | bytes 393224 | tf_op jit(solution)/shard_map/ppermute | solution.py:23
  19.2 42.6 %collective-permute-start.3 = (bf16[272,512]{1,0:T(8,128)(2,1)S(1)}, bf16[272,512]{1,0:T(8,128)(2,1)S(1)}, u32[]{:S(2)}, u32[]{:S(2)}) collective-permute-start(bf16[272,512]{1,0:T(8,128)(2,1)S(1)} %copy-done.6), channel_id=1, source_target_pairs={{0,16},{16,32},{32,48},{48,64},{64,80},{80,96},{96,112},{112,128},... | collective-permute-start | bytes 835592 | tf_op jit(solution)/shard_map/ppermute | solution.py:23
  22.1 44.4 %collective-permute-start.4 = (bf16[272,512]{1,0:T(8,128)(2,1)S(1)}, bf16[272,512]{1,0:T(8,128)(2,1)S(1)}, u32[]{:S(2)}, u32[]{:S(2)}) collective-permute-start(bf16[272,512]{1,0:T(8,128)(2,1)S(1)} %collective-permute-done.refs_1_), channel_id=1, source_target_pairs={{0,16},{16,32},{32,48},{48,64},{64,80},{80,96},{96,112},{112,128},... | collective-permute-start | bytes 835592 | tf_op jit(solution)/shard_map/ppermute | solution.py:23
  29.8 37.7 %collective-permute-start.5 = (bf16[272,512]{1,0:T(8,128)(2,1)S(1)}, bf16[272,512]{1,0:T(8,128)(2,1)S(1)}, u32[]{:S(2)}, u32[]{:S(2)}) collective-permute-start(bf16[272,512]{1,0:T(8,128)(2,1)S(1)} %collective-permute-done.1.refs_2_), channel_id=1, source_target_pairs={{0,16},{16,32},{32,48},{48,64},{64,80},{80,96},{96,112},{112,128},... | collective-permute-start | bytes 835592 | tf_op jit(solution)/shard_map/ppermute | solution.py:23
  38.9 28.6 %collective-permute-start.6 = (bf16[272,512]{1,0:T(8,128)(2,1)S(1)}, bf16[272,512]{1,0:T(8,128)(2,1)S(1)}, u32[]{:S(2)}, u32[]{:S(2)}) collective-permute-start(bf16[272,512]{1,0:T(8,128)(2,1)S(1)} %collective-permute-done.2.refs_3_), channel_id=1, source_target_pairs={{0,16},{16,32},{32,48},{48,64},{64,80},{80,96},{96,112},{112,128},... | collective-permute-start | bytes 835592 | tf_op jit(solution)/shard_map/ppermute | solution.py:23
  40.6 8.0 %collective-permute-start.8 = (bf16[256,256]{1,0:T(8,128)(2,1)}, bf16[256,256]{1,0:T(8,128)(2,1)S(1)}, u32[]{:S(2)}, u32[]{:S(2)}) collective-permute-start(bf16[256,256]{1,0:T(8,128)(2,1)} %get-tuple-element.49), channel_id=1, source_target_pairs={{0,8},{4,12},{8,0},{12,4},{1,9},{5,13},{9,1},{13,5},{2,10},{6,14},... | collective-permute-start | bytes 393224 | tf_op jit(solution)/shard_map/ppermute | solution.py:23
  48.6 11.5 %collective-permute-start.9 = (bf16[256,256]{1,0:T(8,128)(2,1)}, bf16[256,256]{1,0:T(8,128)(2,1)S(1)}, u32[]{:S(2)}, u32[]{:S(2)}) collective-permute-start(bf16[256,256]{1,0:T(8,128)(2,1)} %get-tuple-element.50), channel_id=1, source_target_pairs={{0,12},{4,0},{8,4},{12,8},{1,13},{5,1},{9,5},{13,9},{2,14},{6,2},{... | collective-permute-start | bytes 393224 | tf_op jit(solution)/shard_map/ppermute | solution.py:23
  60.1 18.2 %collective-permute-start.13 = (bf16[256,256]{1,0:T(8,128)(2,1)}, bf16[256,256]{1,0:T(8,128)(2,1)S(1)}, u32[]{:S(2)}, u32[]{:S(2)}) collective-permute-start(bf16[256,256]{1,0:T(8,128)(2,1)} %get-tuple-element.56), channel_id=1, source_target_pairs={{0,4},{4,8},{8,12},{12,0},{1,5},{5,9},{9,13},{13,1},{2,6},{6,10},{... | collective-permute-start | bytes 393224 | tf_op jit(solution)/shard_map/ppermute | solution.py:23
  61.8 16.5 %collective-permute-start.14 = (bf16[256,256]{1,0:T(8,128)(2,1)}, bf16[256,256]{1,0:T(8,128)(2,1)S(1)}, u32[]{:S(2)}, u32[]{:S(2)}) collective-permute-start(bf16[256,256]{1,0:T(8,128)(2,1)} %get-tuple-element.57), channel_id=1, source_target_pairs={{0,8},{4,12},{8,0},{12,4},{1,9},{5,13},{9,1},{13,5},{2,10},{6,14},... | collective-permute-start | bytes 393224 | tf_op jit(solution)/shard_map/ppermute | solution.py:23
  66.5 11.8 %collective-permute-start.15 = (bf16[256,256]{1,0:T(8,128)(2,1)}, bf16[256,256]{1,0:T(8,128)(2,1)S(1)}, u32[]{:S(2)}, u32[]{:S(2)}) collective-permute-start(bf16[256,256]{1,0:T(8,128)(2,1)} %get-tuple-element.58), channel_id=1, source_target_pairs={{0,12},{4,0},{8,4},{12,8},{1,13},{5,1},{9,5},{13,9},{2,14},{6,2},{... | collective-permute-start | bytes 393224 | tf_op jit(solution)/shard_map/ppermute | solution.py:23
  67.5 0.6 copy-start.5
  68.1 0.9 copy-start.8
  69.0 9.4 %copy-start.7 = (bf16[256,256]{1,0:T(8,128)(2,1)S(1)}, bf16[256,256]{1,0:T(8,128)(2,1)}, u32[]{:S(2)}) copy-start(bf16[256,256]{1,0:T(8,128)(2,1)} %get-tuple-element.55.refs_8_) | copy-start | bytes 393220
  77.7 0.7 copy-start
  87.1 45.8 %copy-start.1 = (bf16[256,256]{1,0:T(8,128)(2,1)}, bf16[256,256]{1,0:T(8,128)(2,1)S(1)}, u32[]{:S(2)}) copy-start(bf16[256,256]{1,0:T(8,128)(2,1)S(1)} %get-tuple-element.59.refs_4_) | copy-start | bytes 393220
  87.1 10.3 %collective-permute-start.29 = (f32[1,512]{1,0:T(1,128)S(1)}, f32[1,512]{1,0:T(1,128)S(1)}, u32[]{:S(2)}, u32[]{:S(2)}) collective-permute-start(f32[1,512]{1,0:T(1,128)S(1)} %constant_dynamic-update-slice_fusion), channel_id=1, source_target_pairs={{0,3},{1,0},{2,1},{3,2},{4,7},{5,4},{6,5},{7,6},{8,11},{9,8},{10,9... | collective-permute-start | bytes 6152 | tf_op jit(solution)/shard_map/ppermute | solution.py:23
  89.7 7.7 %collective-permute-start.28 = (f32[1,512]{1,0:T(1,128)S(1)}, f32[1,512]{1,0:T(1,128)S(1)}, u32[]{:S(2)}, u32[]{:S(2)}) collective-permute-start(f32[1,512]{1,0:T(1,128)S(1)} %constant_dynamic-update-slice_fusion), channel_id=1, source_target_pairs={{0,2},{1,3},{2,0},{3,1},{4,6},{5,7},{6,4},{7,5},{8,10},{9,11},{10,... | collective-permute-start | bytes 6152 | tf_op jit(solution)/shard_map/ppermute | solution.py:23
  90.2 7.2 %collective-permute-start.27 = (f32[1,512]{1,0:T(1,128)S(1)}, f32[1,512]{1,0:T(1,128)S(1)}, u32[]{:S(2)}, u32[]{:S(2)}) collective-permute-start(f32[1,512]{1,0:T(1,128)S(1)} %constant_dynamic-update-slice_fusion), channel_id=1, source_target_pairs={{0,1},{1,2},{2,3},{3,0},{4,5},{5,6},{6,7},{7,4},{8,9},{9,10},{10,1... | collective-permute-start | bytes 6152 | tf_op jit(solution)/shard_map/ppermute | solution.py:23
  90.8 40.9 %collective-permute-start.23 = (bf16[1024,256]{1,0:T(8,128)(2,1)S(1)}, bf16[1024,256]{1,0:T(8,128)(2,1)S(1)}, u32[]{:S(2)}, u32[]{:S(2)}) collective-permute-start(bf16[1024,256]{1,0:T(8,128)(2,1)S(1)} %get-tuple-element.72), channel_id=1, source_target_pairs={{0,240},{16,0},{32,16},{48,32},{64,48},{80,64},{96,80},{112,96},{1... | collective-permute-start | bytes 1572872 | tf_op jit(solution)/shard_map/ppermute | solution.py:23
  93.1 50.7 %collective-permute-start.19 = (bf16[1024,256]{1,0:T(8,128)(2,1)S(1)}, bf16[1024,256]{1,0:T(8,128)(2,1)S(1)}, u32[]{:S(2)}, u32[]{:S(2)}) collective-permute-start(bf16[1024,256]{1,0:T(8,128)(2,1)S(1)} %get-tuple-element.66), channel_id=1, source_target_pairs={{0,240},{16,0},{32,16},{48,32},{64,48},{80,64},{96,80},{112,96},{1... | collective-permute-start | bytes 1572872 | tf_op jit(solution)/shard_map/ppermute | solution.py:23
  97.4 5.6 %collective-permute-start.32 = (f32[1,512]{1,0:T(1,128)S(1)}, f32[1,512]{1,0:T(1,128)S(1)}, u32[]{:S(2)}, u32[]{:S(2)}) collective-permute-start(f32[1,512]{1,0:T(1,128)S(1)} %add_add_fusion.2), channel_id=1, source_target_pairs={{0,192},{16,208},{32,224},{48,240},{64,0},{80,16},{96,32},{112,48}... | collective-permute-start | bytes 6152 | tf_op jit(solution)/shard_map/ppermute | solution.py:23
  97.6 5.4 %collective-permute-start.31 = (f32[1,512]{1,0:T(1,128)S(1)}, f32[1,512]{1,0:T(1,128)S(1)}, u32[]{:S(2)}, u32[]{:S(2)}) collective-permute-start(f32[1,512]{1,0:T(1,128)S(1)} %add_add_fusion.2), channel_id=1, source_target_pairs={{0,128},{16,144},{32,160},{48,176},{64,192},{80,208},{96,224},{112... | collective-permute-start | bytes 6152 | tf_op jit(solution)/shard_map/ppermute | solution.py:23
  100.1 4.8 %collective-permute-start.30 = (f32[1,512]{1,0:T(1,128)S(1)}, f32[1,512]{1,0:T(1,128)S(1)}, u32[]{:S(2)}, u32[]{:S(2)}) collective-permute-start(f32[1,512]{1,0:T(1,128)S(1)} %add_add_fusion.2), channel_id=1, source_target_pairs={{0,64},{16,80},{32,96},{48,112},{64,128},{80,144},{96,160},{112,17... | collective-permute-start | bytes 6152 | tf_op jit(solution)/shard_map/ppermute | solution.py:23
  105.0 11.5 %collective-permute-start.35 = (f32[1,512]{1,0:T(1,128)S(1)}, f32[1,512]{1,0:T(1,128)S(1)}, u32[]{:S(2)}, u32[]{:S(2)}) collective-permute-start(f32[1,512]{1,0:T(1,128)S(1)} %add_add_fusion.1), channel_id=1, source_target_pairs={{0,48},{16,64},{32,80},{48,96},{64,112},{80,128},{96,144},{112,160... | collective-permute-start | bytes 6152 | tf_op jit(solution)/shard_map/ppermute | solution.py:23
  115.7 4.5 %collective-permute-start.34 = (f32[1,512]{1,0:T(1,128)S(1)}, f32[1,512]{1,0:T(1,128)S(1)}, u32[]{:S(2)}, u32[]{:S(2)}) collective-permute-start(f32[1,512]{1,0:T(1,128)S(1)} %add_add_fusion.1), channel_id=1, source_target_pairs={{0,32},{16,48},{32,64},{48,80},{64,96},{80,112},{96,128},{112,144}... | collective-permute-start | bytes 6152 | tf_op jit(solution)/shard_map/ppermute | solution.py:23
  115.7 7.7 %collective-permute-start.33 = (f32[1,512]{1,0:T(1,128)S(1)}, f32[1,512]{1,0:T(1,128)S(1)}, u32[]{:S(2)}, u32[]{:S(2)}) collective-permute-start(f32[1,512]{1,0:T(1,128)S(1)} %add_add_fusion.1), channel_id=1, source_target_pairs={{0,16},{16,32},{32,48},{48,64},{64,80},{80,96},{96,112},{112,128},... | collective-permute-start | bytes 6152 | tf_op jit(solution)/shard_map/ppermute | solution.py:23
  116.5 25.1 %collective-permute-start.16 = (bf16[256,256]{1,0:T(8,128)(2,1)S(1)}, bf16[256,256]{1,0:T(8,128)(2,1)S(1)}, u32[]{:S(2)}, u32[]{:S(2)}) collective-permute-start(bf16[256,256]{1,0:T(8,128)(2,1)S(1)} %get-tuple-element.60), channel_id=1, source_target_pairs={{0,12},{4,0},{8,4},{12,8},{1,13},{5,1},{9,5},{13,9},{2,14},{6,2},{... | collective-permute-start | bytes 393224 | tf_op jit(solution)/shard_map/ppermute | solution.py:23
  120.3 22.0 %collective-permute-start.17 = (bf16[256,256]{1,0:T(8,128)(2,1)S(1)}, bf16[256,256]{1,0:T(8,128)(2,1)S(1)}, u32[]{:S(2)}, u32[]{:S(2)}) collective-permute-start(bf16[256,256]{1,0:T(8,128)(2,1)S(1)} %get-tuple-element.61), channel_id=1, source_target_pairs={{0,8},{4,12},{8,0},{12,4},{1,9},{5,13},{9,1},{13,5},{2,10},{6,14},... | collective-permute-start | bytes 393224 | tf_op jit(solution)/shard_map/ppermute | solution.py:23
  123.4 8.2 %collective-permute-start.38 = (f32[1,512]{1,0:T(1,128)S(1)}, f32[1,512]{1,0:T(1,128)S(1)}, u32[]{:S(2)}, u32[]{:S(2)}) collective-permute-start(f32[1,512]{1,0:T(1,128)S(1)} %add_add_fusion), channel_id=1, source_target_pairs={{0,4},{4,8},{8,12},{12,0},{1,5},{5,9},{9,13},{13,1},{2,6},{6,10},{... | collective-permute-start | bytes 6152 | tf_op jit(solution)/shard_map/ppermute | solution.py:23
  131.7 6.4 %collective-permute-start.37 = (f32[1,512]{1,0:T(1,128)S(1)}, f32[1,512]{1,0:T(1,128)S(1)}, u32[]{:S(2)}, u32[]{:S(2)}) collective-permute-start(f32[1,512]{1,0:T(1,128)S(1)} %add_add_fusion), channel_id=1, source_target_pairs={{0,8},{4,12},{8,0},{12,4},{1,9},{5,13},{9,1},{13,5},{2,10},{6,14},... | collective-permute-start | bytes 6152 | tf_op jit(solution)/shard_map/ppermute | solution.py:23
  131.7 6.4 %collective-permute-start.36 = (f32[1,512]{1,0:T(1,128)S(1)}, f32[1,512]{1,0:T(1,128)S(1)}, u32[]{:S(2)}, u32[]{:S(2)}) collective-permute-start(f32[1,512]{1,0:T(1,128)S(1)} %add_add_fusion), channel_id=1, source_target_pairs={{0,12},{4,0},{8,4},{12,8},{1,13},{5,1},{9,5},{13,9},{2,14},{6,2},{... | collective-permute-start | bytes 6152 | tf_op jit(solution)/shard_map/ppermute | solution.py:23
  132.9 13.7 %copy-start.2 = (bf16[256,256]{1,0:T(8,128)(2,1)}, bf16[256,256]{1,0:T(8,128)(2,1)S(1)}, u32[]{:S(2)}) copy-start(bf16[256,256]{1,0:T(8,128)(2,1)S(1)} %get-tuple-element.73.refs_4_) | copy-start | bytes 393220
  138.0 9.2 %collective-permute-start.18 = (bf16[256,256]{1,0:T(8,128)(2,1)S(1)}, bf16[256,256]{1,0:T(8,128)(2,1)S(1)}, u32[]{:S(2)}, u32[]{:S(2)}) collective-permute-start(bf16[256,256]{1,0:T(8,128)(2,1)S(1)} %get-tuple-element.62), channel_id=1, source_target_pairs={{0,4},{4,8},{8,12},{12,0},{1,5},{5,9},{9,13},{13,1},{2,6},{6,10},{... | collective-permute-start | bytes 393224 | tf_op jit(solution)/shard_map/ppermute | solution.py:23
  138.0 18.5 %collective-permute-start.10 = (bf16[256,256]{1,0:T(8,128)(2,1)S(1)}, bf16[256,256]{1,0:T(8,128)(2,1)S(1)}, u32[]{:S(2)}, u32[]{:S(2)}) collective-permute-start(bf16[256,256]{1,0:T(8,128)(2,1)S(1)} %get-tuple-element.52), channel_id=1, source_target_pairs={{0,12},{4,0},{8,4},{12,8},{1,13},{5,1},{9,5},{13,9},{2,14},{6,2},{... | collective-permute-start | bytes 393224 | tf_op jit(solution)/shard_map/ppermute | solution.py:23
  141.6 5.0 %copy-start.9 = (bf16[256,256]{1,0:T(8,128)(2,1)}, bf16[256,256]{1,0:T(8,128)(2,1)S(1)}, u32[]{:S(2)}) copy-start(bf16[256,256]{1,0:T(8,128)(2,1)S(1)} %collective-permute-done.16.refs_5_) | copy-start | bytes 393220
  141.6 20.9 %collective-permute-start.11 = (bf16[256,256]{1,0:T(8,128)(2,1)S(1)}, bf16[256,256]{1,0:T(8,128)(2,1)S(1)}, u32[]{:S(2)}, u32[]{:S(2)}) collective-permute-start(bf16[256,256]{1,0:T(8,128)(2,1)S(1)} %get-tuple-element.53), channel_id=1, source_target_pairs={{0,8},{4,12},{8,0},{12,4},{1,9},{5,13},{9,1},{13,5},{2,10},{6,14},... | collective-permute-start | bytes 393224 | tf_op jit(solution)/shard_map/ppermute | solution.py:23
  142.3 4.3 %copy-start.10 = (bf16[256,256]{1,0:T(8,128)(2,1)}, bf16[256,256]{1,0:T(8,128)(2,1)S(1)}, u32[]{:S(2)}) copy-start(bf16[256,256]{1,0:T(8,128)(2,1)S(1)} %collective-permute-done.17.refs_6_) | copy-start | bytes 393220
  142.3 20.2 %collective-permute-start.12 = (bf16[256,256]{1,0:T(8,128)(2,1)S(1)}, bf16[256,256]{1,0:T(8,128)(2,1)S(1)}, u32[]{:S(2)}, u32[]{:S(2)}) collective-permute-start(bf16[256,256]{1,0:T(8,128)(2,1)S(1)} %get-tuple-element.54), channel_id=1, source_target_pairs={{0,4},{4,8},{8,12},{12,0},{1,5},{5,9},{9,13},{13,1},{2,6},{6,10},{... | collective-permute-start | bytes 393224 | tf_op jit(solution)/shard_map/ppermute | solution.py:23
  143.8 22.2 %collective-permute-start.24 = (bf16[256,256]{1,0:T(8,128)(2,1)S(1)}, bf16[256,256]{1,0:T(8,128)(2,1)S(1)}, u32[]{:S(2)}, u32[]{:S(2)}) collective-permute-start(bf16[256,256]{1,0:T(8,128)(2,1)S(1)} %get-tuple-element.74), channel_id=1, source_target_pairs={{0,12},{4,0},{8,4},{12,8},{1,13},{5,1},{9,5},{13,9},{2,14},{6,2},{... | collective-permute-start | bytes 393224 | tf_op jit(solution)/shard_map/ppermute | solution.py:23
  146.6 0.6 copy-start.3
  147.2 21.4 %copy-start.11 = (bf16[256,256]{1,0:T(8,128)(2,1)}, bf16[256,256]{1,0:T(8,128)(2,1)S(1)}, u32[]{:S(2)}) copy-start(bf16[256,256]{1,0:T(8,128)(2,1)S(1)} %collective-permute-done.18.refs_7_) | copy-start | bytes 393220
  147.2 23.8 %collective-permute-start.25 = (bf16[256,256]{1,0:T(8,128)(2,1)S(1)}, bf16[256,256]{1,0:T(8,128)(2,1)S(1)}, u32[]{:S(2)}, u32[]{:S(2)}) collective-permute-start(bf16[256,256]{1,0:T(8,128)(2,1)S(1)} %get-tuple-element.75), channel_id=1, source_target_pairs={{0,8},{4,12},{8,0},{12,4},{1,9},{5,13},{9,1},{13,5},{2,10},{6,14},... | collective-permute-start | bytes 393224 | tf_op jit(solution)/shard_map/ppermute | solution.py:23
  156.5 12.2 %copy-start.13 = (bf16[256,256]{1,0:T(8,128)(2,1)}, bf16[256,256]{1,0:T(8,128)(2,1)S(1)}, u32[]{:S(2)}) copy-start(bf16[256,256]{1,0:T(8,128)(2,1)S(1)} %collective-permute-done.10.refs_1_) | copy-start | bytes 393220
  156.5 14.6 %collective-permute-start.26 = (bf16[256,256]{1,0:T(8,128)(2,1)S(1)}, bf16[256,256]{1,0:T(8,128)(2,1)S(1)}, u32[]{:S(2)}, u32[]{:S(2)}) collective-permute-start(bf16[256,256]{1,0:T(8,128)(2,1)S(1)} %get-tuple-element.76), channel_id=1, source_target_pairs={{0,4},{4,8},{8,12},{12,0},{1,5},{5,9},{9,13},{13,1},{2,6},{6,10},{... | collective-permute-start | bytes 393224 | tf_op jit(solution)/shard_map/ppermute | solution.py:23
  162.5 6.2 %copy-start.14 = (bf16[256,256]{1,0:T(8,128)(2,1)}, bf16[256,256]{1,0:T(8,128)(2,1)S(1)}, u32[]{:S(2)}) copy-start(bf16[256,256]{1,0:T(8,128)(2,1)S(1)} %collective-permute-done.11.refs_2_) | copy-start | bytes 393220
  162.5 8.6 %collective-permute-start.20 = (bf16[256,256]{1,0:T(8,128)(2,1)S(1)}, bf16[256,256]{1,0:T(8,128)(2,1)S(1)}, u32[]{:S(2)}, u32[]{:S(2)}) collective-permute-start(bf16[256,256]{1,0:T(8,128)(2,1)S(1)} %get-tuple-element.68), channel_id=1, source_target_pairs={{0,12},{4,0},{8,4},{12,8},{1,13},{5,1},{9,5},{13,9},{2,14},{6,2},{... | collective-permute-start | bytes 393224 | tf_op jit(solution)/shard_map/ppermute | solution.py:23
  162.5 6.2 %copy-start.16 = (bf16[256,256]{1,0:T(8,128)(2,1)}, bf16[256,256]{1,0:T(8,128)(2,1)S(1)}, u32[]{:S(2)}) copy-start(bf16[256,256]{1,0:T(8,128)(2,1)S(1)} %collective-permute-done.12.refs_3_) | copy-start | bytes 393220
  162.5 11.2 %collective-permute-start.21 = (bf16[256,256]{1,0:T(8,128)(2,1)S(1)}, bf16[256,256]{1,0:T(8,128)(2,1)S(1)}, u32[]{:S(2)}, u32[]{:S(2)}) collective-permute-start(bf16[256,256]{1,0:T(8,128)(2,1)S(1)} %get-tuple-element.69), channel_id=1, source_target_pairs={{0,8},{4,12},{8,0},{12,4},{1,9},{5,13},{9,1},{13,5},{2,10},{6,14},... | collective-permute-start | bytes 393224 | tf_op jit(solution)/shard_map/ppermute | solution.py:23
  166.0 5.0 %copy-start.12 = (bf16[256,256]{1,0:T(8,128)(2,1)}, bf16[256,256]{1,0:T(8,128)(2,1)S(1)}, u32[]{:S(2)}) copy-start(bf16[256,256]{1,0:T(8,128)(2,1)S(1)} %collective-permute-done.24.refs_5_) | copy-start | bytes 393220
  166.0 12.2 %collective-permute-start.22 = (bf16[256,256]{1,0:T(8,128)(2,1)S(1)}, bf16[256,256]{1,0:T(8,128)(2,1)S(1)}, u32[]{:S(2)}, u32[]{:S(2)}) collective-permute-start(bf16[256,256]{1,0:T(8,128)(2,1)S(1)} %get-tuple-element.70), channel_id=1, source_target_pairs={{0,4},{4,8},{8,12},{12,0},{1,5},{5,9},{9,13},{13,1},{2,6},{6,10},{... | collective-permute-start | bytes 393224 | tf_op jit(solution)/shard_map/ppermute | solution.py:23
  171.0 7.2 %copy-start.15 = (bf16[256,256]{1,0:T(8,128)(2,1)}, bf16[256,256]{1,0:T(8,128)(2,1)S(1)}, u32[]{:S(2)}) copy-start(bf16[256,256]{1,0:T(8,128)(2,1)S(1)} %collective-permute-done.25.refs_6_) | copy-start | bytes 393220
  171.0 7.2 %copy-start.17 = (bf16[256,256]{1,0:T(8,128)(2,1)}, bf16[256,256]{1,0:T(8,128)(2,1)S(1)}, u32[]{:S(2)}) copy-start(bf16[256,256]{1,0:T(8,128)(2,1)S(1)} %collective-permute-done.26.refs_7_) | copy-start | bytes 393220
  171.1 7.2 %copy-start.18 = (bf16[256,256]{1,0:T(8,128)(2,1)}, bf16[256,256]{1,0:T(8,128)(2,1)S(1)}, u32[]{:S(2)}) copy-start(bf16[256,256]{1,0:T(8,128)(2,1)S(1)} %collective-permute-done.20.refs_1_) | copy-start | bytes 393220
  173.7 4.6 %copy-start.19 = (bf16[256,256]{1,0:T(8,128)(2,1)}, bf16[256,256]{1,0:T(8,128)(2,1)S(1)}, u32[]{:S(2)}) copy-start(bf16[256,256]{1,0:T(8,128)(2,1)S(1)} %collective-permute-done.21.refs_2_) | copy-start | bytes 393220
  178.2 0.6 copy-start.20

commit v2 on v1

v2 whole, which is shorter than its diff:
```python
import functools
import math

import jax
import jax.numpy as jnp
from jax import lax
from jax.experimental import pallas as pl
from jax.experimental.pallas import tpu as pltpu
from jax.sharding import PartitionSpec as P

HEAD_DIM = 128
ROWS = 128
SHARDS = 4
EXTRA_ROWS = 16
KV_ROWS = 2 * ROWS + EXTRA_ROWS
VMEM_BYTES = 56 * 1024 * 1024
F32 = jnp.float32
BF16 = jnp.bfloat16


def permuted(value, axis, steps):
    count = lax.axis_size(axis)
    pairs = [(source, (source + steps) % count) for source in range(count)]
    return lax.ppermute(value, axis, pairs)


def vmem_spec():
    return pl.BlockSpec(memory_space=pltpu.VMEM)


def smem_spec():
    return pl.BlockSpec(memory_space=pltpu.SMEM)


def any_spec():
    return pl.BlockSpec(memory_space=pl.ANY)


def place_columns(k, width):
    return block_columns(lax.rem(lax.axis_index("inner") + k, SHARDS), width)


def block_columns(place, width):
    half = width // 2
    turn = lax.axis_index("outer") // (lax.axis_size("outer") // 2)
    first = place * width
    second = lax.rem(place + turn, SHARDS) * width + half
    return (
        (pl.ds(pl.multiple_of(first, half), half), slice(0, half)),
        (pl.ds(pl.multiple_of(second, half), half), slice(half, width)),
    )


def put_kv(out, k, order, keys, values):
    width = out.shape[1]
    for columns, here in place_columns(k, width):
        out[0:ROWS, here] = keys[0, :, columns]
        out[ROWS : 2 * ROWS, here] = values[0, :, columns]
    rows = lax.broadcasted_iota(jnp.int32, (EXTRA_ROWS, width), 0)
    numbers = jnp.where(rows < EXTRA_ROWS // 2, order[0], order[1])
    out[2 * ROWS : KV_ROWS] = numbers.astype(F32).astype(BF16)


def put_qd(out, first, k, queries, grads):
    for columns, here in place_columns(k, out.shape[1]):
        out[first : first + ROWS, here] = queries[0, :, columns]
        out[first + ROWS : first + 2 * ROWS, here] = grads[0, :, columns]


def join_kernel(*refs):
    parts, outs = refs[:-2], refs[-2:]
    half = parts[0].shape[1] // 2
    for n, out in enumerate(outs):
        for s, part in enumerate(parts):
            rows = slice(s * KV_ROWS, (s + 1) * KV_ROWS)
            out[rows] = part[0:KV_ROWS, n * half : (n + 1) * half]


def join(parts):
    out = jax.ShapeDtypeStruct((len(parts) * KV_ROWS, parts[0].shape[1] // 2), BF16)
    return pl.pallas_call(
        join_kernel,
        out_shape=(out, out),
        in_specs=[vmem_spec()] * len(parts),
        out_specs=(vmem_spec(),) * 2,
        compiler_params=pltpu.CompilerParams(vmem_limit_bytes=VMEM_BYTES),
        name="join",
    )(*parts)


def pack_kernel(order, queries, keys, values, grads, *outs):
    for k, out in enumerate(outs):
        put_kv(out, k, order, keys, values)
        put_qd(out, KV_ROWS, k, queries, grads)


def pack(order, queries, keys, values, grads):
    out = jax.ShapeDtypeStruct((KV_ROWS + 2 * ROWS, keys.shape[2] // SHARDS), BF16)
    return pl.pallas_call(
        pack_kernel,
        out_shape=(out,) * SHARDS,
        in_specs=[smem_spec()] + [vmem_spec()] * 4,
        out_specs=(vmem_spec(),) * SHARDS,
        compiler_params=pltpu.CompilerParams(vmem_limit_bytes=VMEM_BYTES),
        name="pack",
    )(order, queries, keys, values, grads)


def copies_out(k, part, first, outs, sems):
    copies = []
    for h, (columns, here) in enumerate(place_columns(k, part.shape[1])):
        for n, out in enumerate(outs):
            source = part.at[first + n * ROWS : first + (n + 1) * ROWS, here]
            sem = sems.at[2 * h + n]
            copies.append(pltpu.make_async_copy(source, out.at[0, :, columns], sem))
    return copies


def unpack_early_kernel(part_0, part_1, part_3, attended, query_grad, sems):
    outs = (attended, query_grad)
    copies = copies_out(0, part_0, 0, outs, sems.at[0])
    copies += copies_out(1, part_1, 0, outs, sems.at[1])
    copies += copies_out(3, part_3, 0, outs, sems.at[2])
    for copy in copies:
        copy.start()
    for copy in copies:
        copy.wait()


def unpack_early(parts):
    out = jax.ShapeDtypeStruct((1, ROWS, parts[0].shape[1] * SHARDS), BF16)
    return pl.pallas_call(
        unpack_early_kernel,
        out_shape=(out, out),
        in_specs=[vmem_spec()] * 3,
        out_specs=(any_spec(), any_spec()),
        scratch_shapes=[pltpu.SemaphoreType.DMA((3, 4))],
        compiler_params=pltpu.CompilerParams(vmem_limit_bytes=VMEM_BYTES),
        name="unpack_early",
    )(*parts)


def unpack_kernel(gain_scale, *refs):
    parts, terms = refs[:SHARDS], refs[SHARDS]
    attended, query_grad, key_grad, value_grad, gain_grad, sems = refs[SHARDS + 3 :]
    copies = []
    for k, part in enumerate(parts):
        copies += copies_out(k, part, 0, (key_grad, value_grad), sems.at[k])
    copies += copies_out(2, parts[2], 2 * ROWS, (attended, query_grad), sems.at[SHARDS])
    for copy in copies:
        copy.start()
    for n in range(SHARDS):
        for columns, here in block_columns(lax.axis_index("inner") ^ n, terms.shape[1]):
            gain_grad[:, columns] = terms[n : n + 1, here] * gain_scale
    for copy in copies:
        copy.wait()


def unpack(parts, terms, attended, query_grad, gain_scale):
    out = jax.ShapeDtypeStruct(attended.shape, BF16)
    count = SHARDS + 1
    return pl.pallas_call(
        functools.partial(unpack_kernel, gain_scale),
        out_shape=(out,) * 4 + (jax.ShapeDtypeStruct((1, attended.shape[2]), F32),),
        in_specs=[vmem_spec()] * count + [any_spec()] * 2,
        out_specs=(any_spec(),) * 4 + (vmem_spec(),),
        scratch_shapes=[pltpu.SemaphoreType.DMA((SHARDS + 1, 4))],
        input_output_aliases={count: 0, count + 1: 1},
        compiler_params=pltpu.CompilerParams(vmem_limit_bytes=VMEM_BYTES),
        name="unpack",
    )(*parts, terms, attended, query_grad)


def dot_nn(a, b):
    return lax.dot_general(a, b, (((1,), (0,)), ((), ())), preferred_element_type=F32)


def dot_nt(a, b):
    return lax.dot_general(a, b, (((1,), (1,)), ((), ())), preferred_element_type=F32)


def attend_kernel(scalars, *refs):
    own_kv = refs[0:4]
    qd = [ref.at[KV_ROWS:] for ref in own_kv]
    halves = (refs[4:6], refs[6:8])
    prior_place = ((0, 0), (0, KV_ROWS), (1, 0), (0, 2 * KV_ROWS))
    gain = refs[8]
    ad_out = refs[9:13]
    own_out = refs[13]
    prior_outs, gain_out = refs[14:16], refs[16]
    own, own_t, prior, prior_t, raw_prior, kpos, qpos, q_all, s_all, w_all, step_part = refs[17:]
    head, heads = pl.program_id(0), pl.num_programs(0)
    start = scalars[1]
    group = SHARDS * ROWS
    score_scale = HEAD_DIM ** (-0.5)
    exponent_scale = score_scale * math.log2(math.e)
    half = ROWS // 2
    key_at, value_at = 0, 1
    query_at, grad_at = 0, 1
    weight_at, score_at = 0, 1

    in_first = head < heads // 2
    lane = lax.broadcasted_iota(jnp.int32, (1, ROWS), 1)
    lanes = jnp.where(lane < half, lane, lane - half).astype(F32)
    row = lax.broadcasted_iota(jnp.int32, (half, ROWS), 0).astype(F32)
    own_numbers = [ref[2 * ROWS : KV_ROWS] for ref in own_kv]
    prior_numbers = [
        jnp.where(in_first, *(parts[at][first + 2 * ROWS : first + KV_ROWS] for parts in halves))
        for at, first in prior_place
    ]
    for s, numbers in enumerate(own_numbers + prior_numbers):
        numbers = numbers.astype(F32)
        first = numbers[0:1] * half
        second = numbers[EXTRA_ROWS // 2 : EXTRA_ROWS // 2 + 1] * half
        kpos[s, 0:half] = row + first
        kpos[s, half:ROWS] = row + second
        if s < SHARDS:
            qpos[s : s + 1] = jnp.where(lane < half, first, second) + lanes

    gain_row = gain[...]
    for s in range(SHARDS):
        rows = slice(s * ROWS, (s + 1) * ROWS)
        for n in (key_at, value_at):
            part = own_kv[s][n * ROWS : (n + 1) * ROWS]
            if n == key_at:
                part = (part.astype(F32) * gain_row).astype(BF16)
            own[n, s] = part
            own_t[n, s] = part.T
        q_all[query_at, s] = qd[s][0:ROWS]
        q_all[grad_at, s] = qd[s][ROWS : 2 * ROWS]
    for s, (part_at, first) in enumerate(prior_place):
        rows = slice(s * ROWS, (s + 1) * ROWS)
        raw, value = (
            jnp.where(in_first, *(half[part_at][at : at + ROWS] for half in halves))
            for at in (first, first + ROWS)
        )
        raw_prior[rows] = raw
        key = (raw.astype(F32) * gain_row).astype(BF16)
        for n, part in ((key_at, key), (value_at, value)):
            prior[n, rows] = part
            prior_t[n, :, rows] = part.T

    steps = [lax.rem(start + a, SHARDS) for a in range(SHARDS)]
    columns = [slice(a * ROWS, (a + 1) * ROWS) for a in range(SHARDS)]
    for n in (0, 1):
        s_all[n, 2 * ROWS :] = dot_nt(prior[n], q_all[n].reshape(group, HEAD_DIM))
    for n in (0, 1):
        for a in range(SHARDS):
            s_all[n, 0:ROWS, columns[a]] = dot_nt(own[n, a], q_all[n, a])
            s_all[n, ROWS : 2 * ROWS, columns[a]] = dot_nt(own[n, steps[a]], q_all[n, a])

    for a in range(SHARDS):
        query_pos = qpos[a : a + 1]
        parts = []
        for first, positions in (
            (0, kpos[a]),
            (ROWS, kpos[steps[a]]),
            (2 * ROWS, kpos[SHARDS:].reshape(group, ROWS)),
        ):
            raw = s_all[0, first : first + positions.shape[0], columns[a]] * exponent_scale
            parts.append(jnp.where(positions <= query_pos, raw, -jnp.inf))
        scores = jnp.concatenate(parts, axis=0)
        exps = jnp.exp2(scores - jnp.max(scores, axis=0, keepdims=True))
        weights = exps * (1.0 / jnp.sum(exps, axis=0, keepdims=True))
        s_all[0, :, columns[a]] = weights
        w_all[weight_at, :, columns[a]] = weights.astype(BF16)

    def times_weights(n, which):
        total = dot_nn(prior_t[n], w_all[which, 2 * ROWS :])
        return [
            total[:, columns[a]]
            + dot_nn(own_t[n, a], w_all[which, 0:ROWS, columns[a]])
            + dot_nn(own_t[n, steps[a]], w_all[which, ROWS : 2 * ROWS, columns[a]])
            for a in range(SHARDS)
        ]

    attended_t = times_weights(value_at, weight_at)
    for a in range(SHARDS):
        ad_out[a][0:ROWS] = attended_t[a].T.astype(BF16)
        rounded = attended_t[a].astype(BF16).astype(F32)
        grad_t = q_all[grad_at, a].astype(F32).T
        row_dot = jnp.sum(grad_t * rounded, axis=0, keepdims=True)
        weights = s_all[0, :, columns[a]]
        score_grad = weights * (s_all[1, :, columns[a]] - row_dot)
        w_all[score_at, :, columns[a]] = score_grad.astype(BF16)
    query_grad_t = times_weights(key_at, score_at)
    for a in range(SHARDS):
        ad_out[a][ROWS : 2 * ROWS] = (query_grad_t[a] * score_scale).T.astype(BF16)

    gain_sum = jnp.zeros((1, HEAD_DIM), F32)
    queries, grads = (q_all[n].reshape(group, HEAD_DIM) for n in (0, 1))
    prior_key = dot_nn(w_all[score_at, 2 * ROWS :], queries) * score_scale
    prior_value = dot_nn(w_all[weight_at, 2 * ROWS :], grads)
    gain_sum += jnp.sum(prior_key * raw_prior[...].astype(F32), axis=0, keepdims=True)
    for half_at, out in enumerate(prior_outs):

        @pl.when(head // (heads // 2) == half_at)
        def _(out=out):
            for s in range(SHARDS):
                rows = slice(s * ROWS, (s + 1) * ROWS)
                out[2 * s * ROWS : (2 * s + 1) * ROWS] = prior_key[rows].astype(BF16)
                out[(2 * s + 1) * ROWS : (2 * s + 2) * ROWS] = prior_value[rows].astype(BF16)

    for n in (0, 1):
        which, source = ((score_at, query_at), (weight_at, grad_at))[n]
        for a in range(SHARDS):
            step_part[n, steps[a]] = dot_nn(w_all[which, ROWS : 2 * ROWS, columns[a]], q_all[source, a])
    for s in range(SHARDS):
        key_part = dot_nn(w_all[score_at, 0:ROWS, columns[s]], q_all[query_at, s])
        key_part = (key_part + step_part[0, s]) * score_scale
        value_part = dot_nn(w_all[weight_at, 0:ROWS, columns[s]], q_all[grad_at, s])
        value_part = value_part + step_part[1, s]
        own_out[2 * s * ROWS : (2 * s + 1) * ROWS] = key_part.astype(BF16)
        own_out[(2 * s + 1) * ROWS : (2 * s + 2) * ROWS] = value_part.astype(BF16)
        raw = own_kv[s][0:ROWS].astype(F32)
        gain_sum += jnp.sum(key_part * raw, axis=0, keepdims=True)
    gain_out[...] = jnp.broadcast_to(gain_sum, gain_out.shape)


def attend(scalars, own, prior_kv, gain_row):
    part = own[0].shape[1]
    heads = part // HEAD_DIM
    group = SHARDS * ROWS

    def column_spec(rows):
        return pl.BlockSpec((rows, HEAD_DIM), lambda h, sc: (0, h))

    half = heads // 2

    def half_spec(rows, n):
        if n == 0:
            return pl.BlockSpec((rows, HEAD_DIM), lambda h, sc: (0, jnp.minimum(h, half - 1)))
        return pl.BlockSpec((rows, HEAD_DIM), lambda h, sc: (0, jnp.maximum(h - half, 0)))

    gain_spec = pl.BlockSpec(
        (1, HEAD_DIM), lambda h, sc: (0, jnp.where(h < half, sc[0], sc[2]) * heads + h)
    )
    outs = [(2 * ROWS, part)] * 4 + [(2 * group, part)] + [(2 * group, part // 2)] * 2
    return pl.pallas_call(
        attend_kernel,
        grid_spec=pltpu.PrefetchScalarGridSpec(
            num_scalar_prefetch=1,
            grid=(heads,),
            in_specs=[column_spec(x.shape[0]) for x in own]
            + [half_spec(x.shape[0], n // 2) for n, x in enumerate(prior_kv)]
            + [gain_spec],
            out_specs=[column_spec(rows) for rows, _ in outs[:5]]
            + [half_spec(2 * group, n) for n in (0, 1)]
            + [column_spec(1)],
            scratch_shapes=[
                pltpu.VMEM((2, SHARDS, ROWS, HEAD_DIM), BF16),
                pltpu.VMEM((2, SHARDS, HEAD_DIM, ROWS), BF16),
                pltpu.VMEM((2, group, HEAD_DIM), BF16),
                pltpu.VMEM((2, HEAD_DIM, group), BF16),
                pltpu.VMEM((group, HEAD_DIM), BF16),
                pltpu.VMEM((2 * SHARDS, ROWS, ROWS), F32),
                pltpu.VMEM((8, ROWS), F32),
                pltpu.VMEM((2, SHARDS, ROWS, HEAD_DIM), BF16),
                pltpu.VMEM((2, group + 2 * ROWS, group), F32),
                pltpu.VMEM((2, group + 2 * ROWS, group), BF16),
                pltpu.VMEM((2, SHARDS, ROWS, HEAD_DIM), F32),
            ],
        ),
        out_shape=(
            *(jax.ShapeDtypeStruct(shape, BF16) for shape in outs),
            jax.ShapeDtypeStruct((1, part), F32),
        ),
        compiler_params=pltpu.CompilerParams(
            dimension_semantics=("arbitrary",), vmem_limit_bytes=VMEM_BYTES
        ),
        cost_estimate=pl.CostEstimate(
            flops=heads * 12 * group * (group + 2 * ROWS) * HEAD_DIM,
            bytes_accessed=heads * 14 * group * HEAD_DIM * 2,
            transcendentals=heads * group * (group + 2 * ROWS),
        ),
        name="attend",
    )(scalars, *own, *prior_kv, gain_row)


def finish_kernel(gain, own, back_0, back_1, rest_2, *outs):
    outs[2][2 * ROWS :] = rest_2[...]
    for back, (columns, here) in zip((back_0, back_1), place_columns(0, own.shape[1])):
        gain_row = gain[:, columns]
        for s, out in enumerate(outs):
            rows = pl.ds(2 * s * ROWS, ROWS)
            total = own[rows, here].astype(F32) + back[rows].astype(F32)
            out[0:ROWS, here] = (total * gain_row).astype(BF16)
            rows = pl.ds((2 * s + 1) * ROWS, ROWS)
            total = own[rows, here].astype(F32) + back[rows].astype(F32)
            out[ROWS : 2 * ROWS, here] = total.astype(BF16)


def finish(own, backs, rest_2, gain_row):
    width = own.shape[1]
    return pl.pallas_call(
        finish_kernel,
        in_specs=[vmem_spec()] * 5,
        out_specs=(vmem_spec(),) * SHARDS,
        out_shape=tuple(
            jax.ShapeDtypeStruct(((4 if s == 2 else 2) * ROWS, width), BF16)
            for s in range(SHARDS)
        ),
        cost_estimate=pl.CostEstimate(
            flops=16 * ROWS * width, bytes_accessed=48 * ROWS * width, transcendentals=0
        ),
        compiler_params=pltpu.CompilerParams(vmem_limit_bytes=VMEM_BYTES),
        name="finish",
    )(gain_row, own, *backs, rest_2)


def shifted_halves(first, second, steps):
    outer, inner = lax.axis_size("outer"), lax.axis_size("inner")
    straight, turned = [], []
    for o in range(outer):
        target = (o + steps) % outer
        turn = o // (outer // 2) - target // (outer // 2)
        for i in range(inner):
            straight.append((o * inner + i, target * inner + i))
            turned.append((o * inner + i, target * inner + (i + turn) % inner))
    axes = ("outer", "inner")
    return (
        [lax.ppermute(x, axes, straight) for x in first],
        [lax.ppermute(x, axes, turned) for x in second],
    )


def gathered(term):
    for step in (1, 2):
        pairs = [(source, source ^ step) for source in range(lax.axis_size("inner"))]
        term = jnp.concatenate([term, lax.ppermute(term, "inner", pairs)])
    return term


STEPS = (("dp", 1), ("dp", 2), ("outer", 2), ("outer", 4), ("outer", 1))


def sum_by_steps(steps, term):
    for axis, step in steps:
        pairs = [(source, source ^ step) for source in range(lax.axis_size(axis))]
        term = term + lax.ppermute(term, axis, pairs)
    half = term.shape[1] // 2
    (first,), (second,) = shifted_halves(
        (term[:, :half],), (term[:, half:],), lax.axis_size("outer") // 2
    )
    return gathered(term + jnp.concatenate([first, second], axis=1))


def body(queries, keys, values, out_grad, gain, block_order, start):
    inner = lax.axis_index("inner").astype(jnp.int32)
    turn = lax.axis_index("outer") // (lax.axis_size("outer") // 2)
    scalars = jnp.stack([inner, start[0], lax.rem(inner + turn, SHARDS)])
    gain_row = gain[None]

    own = pack(block_order, queries, keys, values, out_grad)
    own = [own[0]] + [permuted(own[k], "inner", k) for k in range(1, SHARDS)]
    early, late = join([own[0], own[1], own[3]]), join([own[2]])
    prior_0, prior_1 = shifted_halves((early[0], late[0]), (early[1], late[1]), 1)
    *ad, own_part, prior_part_0, prior_part_1, term = attend(
        scalars, own, [*prior_0, *prior_1], gain_row
    )

    (back_0,), (back_1,) = shifted_halves((prior_part_0,), (prior_part_1,), -1)
    ad_1, ad_3 = permuted(ad[1], "inner", -1), permuted(ad[3], "inner", -3)
    back_0, ad_1, ad_3 = lax.optimization_barrier((back_0, ad_1, ad_3))
    parts = finish(own_part, (back_0, back_1), ad[2], gain_row)
    term, ad_0, _ = lax.optimization_barrier((term, ad[0], parts[0]))
    parts = [parts[0]] + [permuted(parts[k], "inner", -k) for k in range(1, SHARDS)]
    attended, query_grad = unpack_early((ad_0, ad_1, ad_3))
    term, attended = lax.optimization_barrier((term, attended))
    terms = lax.cond(
        start[0] >= 0,
        functools.partial(sum_by_steps, STEPS),
        functools.partial(sum_by_steps, STEPS[::-1]),
        term,
    )
    token_count = (
        ROWS * lax.axis_size("inner") * lax.axis_size("outer") * lax.axis_size("dp")
    )
    attended, query_grad, key_grad, value_grad, gain_grad = unpack(
        parts, terms, attended, query_grad, 1.0 / math.sqrt(token_count)
    )
    return attended, query_grad, key_grad, value_grad, gain_grad.reshape(-1)


def solution(mesh):
    rows = P("dp", ("outer", "inner"), None)
    in_specs = (rows, rows, rows, rows, P(), P(("outer", "inner")), P())
    out_specs = (rows, rows, rows, rows, P())
    return jax.shard_map(body, mesh=mesh, in_specs=in_specs, out_specs=out_specs, check_vma=False)
```

time: 184 us -> 163 us (0.89)
  starting transfers between devices: 98.5 us -> 54.1 us
  waiting for transfers between devices: 47 us -> 71.4 us
    ppermute x39 -> x8, starting transfers between devices: 98.5 us -> 19.1 us  [permuted(): return lax.ppermute(value, axis, pairs)]
    ppermute x0 -> x15, starting transfers between devices: none -> 35 us  [the longest x5 18.4 us: sum_by_steps(): term = term + lax.ppermute(term, axis, pairs)]
    ppermute x0 -> x15, waiting for transfers between devices: none -> 24.6 us  [the longest x5 7.34 us: sum_by_steps(): term = term + lax.ppermute(term, axis, pairs)]
    pallas_call x6, Pallas kernels: 10.7 us -> 15.1 us  [the longest x2 4.05 us: join(): pl.pallas_call(join_kernel, out_shape=(out, out), in_specs=[vmem_spec()]...]
    pallas_call x2 -> x1, Pallas kernels: 17.4 us -> 14 us  [attend(): pl.pallas_call(attend_kernel, grid_spec=pltpu.PrefetchScalarGridSpec(num_...]
    ppermute x39 -> x8, waiting for transfers between devices: 47 us -> 46.8 us  [permuted(): return lax.ppermute(value, axis, pairs)]
    unnamed x46 -> x28, local copies, waits for them, and re-layouts: 4.69 us -> 4.45 us
  transfers between devices with their start and end apart: 39 -> 23, of which waited for: 12 -> 14; matrix products, arithmetic and copies ran while one was open for 1% -> 0% of each run, Pallas kernels for 8% -> 4%
where the time goes in v2:
time: 163 us; the launch traced here: 161 us
  waiting for transfers between devices  71.4 us (44%)
  starting transfers between devices  54.1 us (33%)
  Pallas kernels  29.2 us (18%)
  local copies, waits for them, and re-layouts  4.46 us (3%)
    ppermute x8, waiting for transfers between devices, permuted(): return lax.ppermute(value, axis, pairs)  46.8 us
    ppermute x8, starting transfers between devices, permuted(): return lax.ppermute(value, axis, pairs)  19.1 us
    ppermute x5, starting transfers between devices, sum_by_steps(): term = term + lax.ppermute(term, axis, pairs)  18.4 us
    pallas_call x1, Pallas kernels, attend(): pl.pallas_call(attend_kernel, grid_spec=pltpu.PrefetchScalarGridSpec(num_...  14 us
    ppermute x4, starting transfers between devices, shifted_halves(): lax.ppermute(x, axes, straight)  10.5 us
    ppermute x5, waiting for transfers between devices, sum_by_steps(): term = term + lax.ppermute(term, axis, pairs)  7.34 us
    ppermute x2, waiting for transfers between devices, gathered(): term = jnp.concatenate([term, lax.ppermute(term, 'inner', pairs)])  6.67 us
    ppermute x4, waiting for transfers between devices, shifted_halves(): lax.ppermute(x, axes, straight)  5.71 us
  transfers between devices with their start and end apart: 23, of which 14 were waited for; matrix products, arithmetic and copies ran while one was open for 0% of the time, Pallas kernels for 4%

profile of v2, /device:TPU:1, one launch (start us, length us, event | category | flops | bytes accessed | tf_op | source)
XLA Modules:
  0.0 161.3 jit_solution(15671568457198153093)
XLA Ops:
  0.6 3.1 %pack.1 = (bf16[528,512]{1,0:T(8,128)(2,1)}, bf16[528,512]{1,0:T(8,128)(2,1)}, bf16[528,512]{1,0:T(8,128)(2,1)}, bf16[528,512]{1,0:T(8,128)(2,1)}) custom-call(s32[2]{0:T(128)} %order.1, bf16[1,128,2048]{2,1,0:T(8,128)(2,1)} %queries.1, bf16[1,128,2048]{2,1,0:T(8,128)(2,1)} %keys.1, bf16[1,128,2048]{2,1,0:T(8,128)(2,1)} %values.1, bf16[1,128,2048]{2,1,0:T(8,128)(2,1)} %grads.1), custom_call_target="tpu_custom_call" | custom-call | tf_op jit(solution)/shard_map/pack/pallas_call | solution.py:99
  3.8 3.8 %collective-permute-start.18 = (bf16[528,512]{1,0:T(8,128)(2,1)}, bf16[528,512]{1,0:T(8,128)(2,1)S(1)}, u32[]{:S(2)}, u32[]{:S(2)}) collective-permute-start(bf16[528,512]{1,0:T(8,128)(2,1)} %get-tuple-element.45), channel_id=1, source_target_pairs={{0,4},{4,8},{8,12},{12,0},{1,5},{5,9},{9,13},{13,1},{2,6},{6,10},{... | collective-permute-start | bytes 1622024 | tf_op jit(solution)/shard_map/ppermute | solution.py:24
  7.6 3.0 %collective-permute-start.20 = (bf16[528,512]{1,0:T(8,128)(2,1)}, bf16[528,512]{1,0:T(8,128)(2,1)S(1)}, u32[]{:S(2)}, u32[]{:S(2)}) collective-permute-start(bf16[528,512]{1,0:T(8,128)(2,1)} %get-tuple-element.47), channel_id=1, source_target_pairs={{0,12},{4,0},{8,4},{12,8},{1,13},{5,1},{9,5},{13,9},{2,14},{6,2},{... | collective-permute-start | bytes 1622024 | tf_op jit(solution)/shard_map/ppermute | solution.py:24
  10.6 4.5 %collective-permute-start.19 = (bf16[528,512]{1,0:T(8,128)(2,1)}, bf16[528,512]{1,0:T(8,128)(2,1)S(1)}, u32[]{:S(2)}, u32[]{:S(2)}) collective-permute-start(bf16[528,512]{1,0:T(8,128)(2,1)} %get-tuple-element.46), channel_id=1, source_target_pairs={{0,8},{4,12},{8,0},{12,4},{1,9},{5,13},{9,1},{13,5},{2,10},{6,14},... | collective-permute-start | bytes 1622024 | tf_op jit(solution)/shard_map/ppermute | solution.py:24
  15.1 12.1 %collective-permute-done.18.refs_1_ = bf16[528,512]{1,0:T(8,128)(2,1)S(1)} collective-permute-done((bf16[528,512]{1,0:T(8,128)(2,1)}, bf16[528,512]{1,0:T(8,128)(2,1)S(1)}, u32[]{:S(2)}, u32[]{:S(2)}) %collective-permute-start.18) | collective-permute-done | bytes 540704 | tf_op jit(solution)/shard_map/ppermute | solution.py:24
  27.2 21.5 %collective-permute-done.20.refs_2_.refs_3_ = bf16[528,512]{1,0:T(8,128)(2,1)S(1)} collective-permute-done((bf16[528,512]{1,0:T(8,128)(2,1)}, bf16[528,512]{1,0:T(8,128)(2,1)S(1)}, u32[]{:S(2)}, u32[]{:S(2)}) %collective-permute-start.20) | collective-permute-done | bytes 540704 | tf_op jit(solution)/shard_map/ppermute | solution.py:24
  48.7 0.8 copy-done.1
  49.5 2.3 %join.2 = (bf16[816,256]{1,0:T(8,128)(2,1)}, bf16[816,256]{1,0:T(8,128)(2,1)}) custom-call(bf16[528,512]{1,0:T(8,128)(2,1)} %get-tuple-element.44.refs_0_, bf16[528,512]{1,0:T(8,128)(2,1)} %copy-done, bf16[528,512]{1,0:T(8,128)(2,1)} %copy-done.1), custom_call_target="tpu_custom_call" | custom-call | tf_op jit(solution)/shard_map/join/pallas_call | solution.py:81
  51.8 2.2 %collective-permute-start.21 = (bf16[816,256]{1,0:T(8,128)(2,1)}, bf16[816,256]{1,0:T(8,128)(2,1)S(1)}, u32[]{:S(2)}, u32[]{:S(2)}) collective-permute-start(bf16[816,256]{1,0:T(8,128)(2,1)} %get-tuple-element.48), channel_id=1, source_target_pairs={{0,16},{4,20},{8,24},{12,28},{16,32},{20,36},{24,40},{28,44},{32,4... | collective-permute-start | bytes 1253384 | tf_op jit(solution)/shard_map/ppermute | solution.py:422
  54.0 0.0 collective-permute-start.23
  54.0 0.8 copy-done.2
  54.8 1.8 %join.3 = (bf16[272,256]{1,0:T(8,128)(2,1)}, bf16[272,256]{1,0:T(8,128)(2,1)}) custom-call(bf16[528,512]{1,0:T(8,128)(2,1)} %copy-done.2), custom_call_target="tpu_custom_call" | custom-call | tf_op jit(solution)/shard_map/join/pallas_call | solution.py:81
  56.6 1.7 %collective-permute-start.22 = (bf16[272,256]{1,0:T(8,128)(2,1)}, bf16[272,256]{1,0:T(8,128)(2,1)S(1)}, u32[]{:S(2)}, u32[]{:S(2)}) collective-permute-start(bf16[272,256]{1,0:T(8,128)(2,1)} %get-tuple-element.49), channel_id=1, source_target_pairs={{0,16},{4,20},{8,24},{12,28},{16,32},{20,36},{24,40},{28,44},{32,4... | collective-permute-start | bytes 417800 | tf_op jit(solution)/shard_map/ppermute | solution.py:422
  58.3 0.0 collective-permute-start.24
  59.0 0.6 pad_add_fusion.scalars
  59.6 5.7 %collective-permute-done.22.refs_5_ = bf16[272,256]{1,0:T(8,128)(2,1)S(1)} collective-permute-done((bf16[272,256]{1,0:T(8,128)(2,1)}, bf16[272,256]{1,0:T(8,128)(2,1)S(1)}, u32[]{:S(2)}, u32[]{:S(2)}) %collective-permute-start.22) | collective-permute-done | bytes 139296 | tf_op jit(solution)/shard_map/ppermute | solution.py:422
  65.3 1.5 collective-permute-done.24.refs_7_
  66.8 0.0 collective-permute-done.21.refs_4_
  66.8 0.0 collective-permute-done.23.refs_6_
  66.8 0.0 copy-start.11
  66.8 0.6 copy-done.13
  67.4 0.1 copy-done.10
  67.6 0.1 copy-done.11
  67.7 14.0 %attend.1 = (bf16[256,512]{1,0:T(8,128)(2,1)}, bf16[256,512]{1,0:T(8,128)(2,1)}, bf16[256,512]{1,0:T(8,128)(2,1)}, bf16[256,512]{1,0:T(8,128)(2,1)}, bf16[1024,5...) custom-call(s32[3]{0:T(128)} %pad_add_fusion.scalars, ...), custom_call_target="tpu_custom_call" | custom-call | flops 2415919104 | bytes 7340032 | tf_op jit(solution)/shard_map/attend/pallas_call | solution.py:339
  81.7 6.2 %collective-permute-start.25 = (bf16[1024,256]{1,0:T(8,128)(2,1)}, bf16[1024,256]{1,0:T(8,128)(2,1)S(1)}, u32[]{:S(2)}, u32[]{:S(2)}) collective-permute-start(bf16[1024,256]{1,0:T(8,128)(2,1)} %get-tuple-element.53), channel_id=1, source_target_pairs={{0,240},{4,244},{8,248},{12,252},{16,0},{20,4},{24,8},{28,12},{32,... | collective-permute-start | bytes 1572872 | tf_op jit(solution)/shard_map/ppermute | solution.py:422
  88.0 0.1 collective-permute-start.28
  88.1 4.0 %collective-permute-start.26 = (bf16[256,512]{1,0:T(8,128)(2,1)}, bf16[256,512]{1,0:T(8,128)(2,1)S(1)}, u32[]{:S(2)}, u32[]{:S(2)}) collective-permute-start(bf16[256,512]{1,0:T(8,128)(2,1)} %get-tuple-element.54), channel_id=1, source_target_pairs={{0,12},{4,0},{8,4},{12,8},{1,13},{5,1},{9,5},{13,9},{2,14},{6,2},{... | collective-permute-start | bytes 786440 | tf_op jit(solution)/shard_map/ppermute | solution.py:24
  92.1 0.0 collective-permute-start.27
  92.1 9.2 %collective-permute-done.26.part_1 = bf16[256,512]{1,0:T(8,128)(2,1)S(1)} collective-permute-done((bf16[256,512]{1,0:T(8,128)(2,1)}, bf16[256,512]{1,0:T(8,128)(2,1)S(1)}, u32[]{:S(2)}, u32[]{:S(2)}) %collective-permute-start.26) | collective-permute-done | bytes 262176 | tf_op jit(solution)/shard_map/ppermute | solution.py:24
  101.3 4.0 %collective-permute-done.27.part_3 = bf16[256,512]{1,0:T(8,128)(2,1)S(1)} collective-permute-done((bf16[256,512]{1,0:T(8,128)(2,1)}, bf16[256,512]{1,0:T(8,128)(2,1)S(1)}, u32[]{:S(2)}, u32[]{:S(2)}) %collective-permute-start.27) | collective-permute-done | bytes 262176 | tf_op jit(solution)/shard_map/ppermute | solution.py:24
  105.3 0.0 collective-permute-done.25.back_0
  105.3 0.0 collective-permute-done.28.back_1
  105.3 0.0 copy-start.5
  105.3 0.8 copy-done.4
  106.1 0.2 copy-done.5
  106.3 2.8 %finish.1 = (bf16[256,512]{1,0:T(8,128)(2,1)}, bf16[256,512]{1,0:T(8,128)(2,1)}, bf16[512,512]{1,0:T(8,128)(2,1)}, bf16[256,512]{1,0:T(8,128)(2,1)}) custom-call(f32[1,2048]{1,0:T(1,128)} %bitcast.6, bf16[1024,512]{1,0:T(8,128)(2,1)} %get-tuple-element.52.own, bf16[1024,256]{1,0:T(8,128)(2,1)} %copy-done.4, bf16[1024,256]{1,0:T(8,128)(2,1)} %copy-done.5, ...), custom_call_target="tpu_custom_call" | custom-call | flops 1048576 | bytes 3145728 | tf_op jit(solution)/shard_map/finish/pallas_call | solution.py:395
  109.1 1.4 collective-permute-start.30
  110.5 2.0 %collective-permute-start.29 = (bf16[256,512]{1,0:T(8,128)(2,1)}, bf16[256,512]{1,0:T(8,128)(2,1)S(1)}, u32[]{:S(2)}, u32[]{:S(2)}) collective-permute-start(bf16[256,512]{1,0:T(8,128)(2,1)} %get-tuple-element.60), channel_id=1, source_target_pairs={{0,12},{4,0},{8,4},{12,8},{1,13},{5,1},{9,5},{13,9},{2,14},{6,2},{... | collective-permute-start | bytes 786440 | tf_op jit(solution)/shard_map/ppermute | solution.py:24
  112.4 0.4 collective-permute-start.31
  112.8 2.1 %unpack_early.1 = (bf16[1,128,2048]{2,1,0:T(8,128)(2,1)}, bf16[1,128,2048]{2,1,0:T(8,128)(2,1)}) custom-call(bf16[256,512]{1,0:T(8,128)(2,1)} %get-tuple-element.66.part_0, bf16[256,512]{1,0:T(8,128)(2,1)} %copy-done.8, bf16[256,512]{1,0:T(8,128)(2,1)} %copy-done.9), custom_call_target="tpu_custom_call" | custom-call | tf_op jit(solution)/shard_map/unpack_early/pallas_call | solution.py:132
  114.9 42.2 %conditional.1 = (f32[4,512]{1,0:T(4,128)S(1)}) conditional(s32[]{:T(128)} %bitcast.3, f32[1,512]{1,0:T(1,128)S(1)} %get-tuple-element.70, f32[1,512]{1,0:T(1,128)S(1)} %get-tuple-element.70), branch_computations={%region_0.1_spmd, %region_1.2_spmd} | conditional | flops 8704 | bytes 139632 | solution.py:470
  114.9 1.3 collective-permute-start.9
  116.2 1.2 collective-permute-done.9
  117.4 2.7 %collective-permute-start.10 = (f32[1,512]{1,0:T(1,128)S(1)}, f32[1,512]{1,0:T(1,128)S(1)}, u32[]{:S(2)}, u32[]{:S(2)}) collective-permute-start(f32[1,512]{1,0:T(1,128)S(1)} %add.33), channel_id=1, source_target_pairs={{0,2},{1,3},{2,0},{3,1},{4,6},{5,7},{6,4},{7,5},{8,10},{9,11},{10,... | collective-permute-start | bytes 6152 | tf_op jit(solution)/shard_map/cond/branch_1_fun/ppermute | solution.py:440
  120.2 1.2 collective-permute-done.10
  121.4 2.7 %collective-permute-done.11 = f32[1,512]{1,0:T(1,128)S(1)} collective-permute-done((f32[1,512]{1,0:T(1,128)S(1)}, f32[1,512]{1,0:T(1,128)S(1)}, u32[]{:S(2)}, u32[]{:S(2)}) %collective-permute-start.11) | collective-permute-done | bytes 2080 | tf_op jit(solution)/shard_map/cond/branch_1_fun/ppermute | solution.py:440
  124.1 2.9 %collective-permute-start.12 = (f32[1,512]{1,0:T(1,128)S(1)}, f32[1,512]{1,0:T(1,128)S(1)}, u32[]{:S(2)}, u32[]{:S(2)}) collective-permute-start(f32[1,512]{1,0:T(1,128)S(1)} %add.35), channel_id=1, source_target_pairs={{0,64},{16,80},{32,96},{48,112},{64,0},{80,16},{96,32},{112,48},{1... | collective-permute-start | bytes 6152 | tf_op jit(solution)/shard_map/cond/branch_1_fun/ppermute | solution.py:440
  127.0 1.4 collective-permute-done.12
  128.4 11.5 %collective-permute-start.13 = (f32[1,512]{1,0:T(1,128)S(1)}, f32[1,512]{1,0:T(1,128)S(1)}, u32[]{:S(2)}, u32[]{:S(2)}) collective-permute-start(f32[1,512]{1,0:T(1,128)S(1)} %add.36), channel_id=1, source_target_pairs={{0,16},{16,0},{32,48},{48,32},{64,80},{80,64},{96,112},{112,96},{1... | collective-permute-start | bytes 6152 | tf_op jit(solution)/shard_map/cond/branch_1_fun/ppermute | solution.py:440
  139.9 0.8 collective-permute-done.13
  140.7 0.4 collective-permute-start.14
  141.1 2.8 %collective-permute-start.15 = (f32[1,256]{1,0:T(1,128)S(1)}, f32[1,256]{1,0:T(1,128)S(1)}, u32[]{:S(2)}, u32[]{:S(2)}) collective-permute-start(f32[1,256]{1,0:T(1,128)S(1)} %get-tuple-element.81), channel_id=1, source_target_pairs={{0,140},{4,128},{8,132},{12,136},{16,156},{20,144},{24,148},{28,15... | collective-permute-start | bytes 3080 | tf_op jit(solution)/shard_map/cond/branch_1_fun/ppermute | solution.py:423
  143.9 0.0 collective-permute-done.14
  143.9 3.4 %collective-permute-done.15 = f32[1,256]{1,0:T(1,128)S(1)} collective-permute-done((f32[1,256]{1,0:T(1,128)S(1)}, f32[1,256]{1,0:T(1,128)S(1)}, u32[]{:S(2)}, u32[]{:S(2)}) %collective-permute-start.15) | collective-permute-done | bytes 1056 | tf_op jit(solution)/shard_map/cond/branch_1_fun/ppermute | solution.py:423
  147.3 0.6 collective-permute-start.16
  147.9 2.7 %collective-permute-done.16 = f32[1,512]{1,0:T(1,128)S(1)} collective-permute-done((f32[1,512]{1,0:T(1,128)S(1)}, f32[1,512]{1,0:T(1,128)S(1)}, u32[]{:S(2)}, u32[]{:S(2)}) %collective-permute-start.16) | collective-permute-done | bytes 2080 | tf_op jit(solution)/shard_map/cond/branch_1_fun/ppermute | solution.py:430
  150.6 2.5 %collective-permute-start.17 = (f32[2,512]{1,0:T(2,128)S(1)}, f32[2,512]{1,0:T(2,128)S(1)}, u32[]{:S(2)}, u32[]{:S(2)}) collective-permute-start(f32[2,512]{1,0:T(2,128)S(1)} %pad_maximum_fusion.3), channel_id=1, source_target_pairs={{0,8},{4,12},{8,0},{12,4},{1,9},{5,13},{9,1},{13,5},{2,10},{6,14},... | collective-permute-start | bytes 12296 | tf_op jit(solution)/shard_map/cond/branch_1_fun/ppermute | solution.py:430
  153.1 4.0 %collective-permute-done.17 = f32[2,512]{1,0:T(2,128)S(1)} collective-permute-done((f32[2,512]{1,0:T(2,128)S(1)}, f32[2,512]{1,0:T(2,128)S(1)}, u32[]{:S(2)}, u32[]{:S(2)}) %collective-permute-start.17) | collective-permute-done | bytes 4128 | tf_op jit(solution)/shard_map/cond/branch_1_fun/ppermute | solution.py:430
  157.1 0.0 collective-permute-done.29.refs_1_
  157.2 0.0 collective-permute-done.30.refs_2_
  157.2 0.6 copy-done.6
  157.8 0.1 copy-done.7
  157.9 0.2 copy-done.3
  158.1 3.1 %unpack.1 = (bf16[1,128,2048]{2,1,0:T(8,128)(2,1)}, bf16[1,128,2048]{2,1,0:T(8,128)(2,1)}, bf16[1,128,2048]{2,1,0:T(8,128)(2,1)}, bf16[1,128,2048]{2,1,0:T(8,128)(2,1)}, f32[1,2048]{1,0:T(1,128)}) custom-call(bf16[256,512]{1,0:T(8,128)(2,1)} %get-tuple-element.59.refs_0_, bf16[256,512]{1,0:T(8,128)(2,1)} %copy-done.6, ...), custom_call_target="tpu_custom_call", output_to_operand_aliasing={{0}: (5, {}), {1}: (6, {})} | custom-call | tf_op jit(solution)/shard_map/unpack/pallas_call | solution.py:162
  (28 shorter events, 0.1 us)
Async XLA Ops:
  3.8 23.4 %collective-permute-start.18 = (bf16[528,512]{1,0:T(8,128)(2,1)}, bf16[528,512]{1,0:T(8,128)(2,1)S(1)}, u32[]{:S(2)}, u32[]{:S(2)}) collective-permute-start(bf16[528,512]{1,0:T(8,128)(2,1)} %get-tuple-element.45), channel_id=1, source_target_pairs={{0,4},{4,8},{8,12},{12,0},{1,5},{5,9},{9,13},{13,1},{2,6},{6,10},{... | collective-permute-start | bytes 1622024 | tf_op jit(solution)/shard_map/ppermute | solution.py:24
  7.6 41.1 %collective-permute-start.20 = (bf16[528,512]{1,0:T(8,128)(2,1)}, bf16[528,512]{1,0:T(8,128)(2,1)S(1)}, u32[]{:S(2)}, u32[]{:S(2)}) collective-permute-start(bf16[528,512]{1,0:T(8,128)(2,1)} %get-tuple-element.47), channel_id=1, source_target_pairs={{0,12},{4,0},{8,4},{12,8},{1,13},{5,1},{9,5},{13,9},{2,14},{6,2},{... | collective-permute-start | bytes 1622024 | tf_op jit(solution)/shard_map/ppermute | solution.py:24
  10.6 43.4 %collective-permute-start.19 = (bf16[528,512]{1,0:T(8,128)(2,1)}, bf16[528,512]{1,0:T(8,128)(2,1)S(1)}, u32[]{:S(2)}, u32[]{:S(2)}) collective-permute-start(bf16[528,512]{1,0:T(8,128)(2,1)} %get-tuple-element.46), channel_id=1, source_target_pairs={{0,8},{4,12},{8,0},{12,4},{1,9},{5,13},{9,1},{13,5},{2,10},{6,14},... | collective-permute-start | bytes 1622024 | tf_op jit(solution)/shard_map/ppermute | solution.py:24
  27.2 21.5 %copy-start = (bf16[528,512]{1,0:T(8,128)(2,1)}, bf16[528,512]{1,0:T(8,128)(2,1)S(1)}, u32[]{:S(2)}) copy-start(bf16[528,512]{1,0:T(8,128)(2,1)S(1)} %collective-permute-done.18.refs_1_) | copy-start | bytes 1622020
  48.7 0.8 copy-start.1
  51.8 15.0 %collective-permute-start.21 = (bf16[816,256]{1,0:T(8,128)(2,1)}, bf16[816,256]{1,0:T(8,128)(2,1)S(1)}, u32[]{:S(2)}, u32[]{:S(2)}) collective-permute-start(bf16[816,256]{1,0:T(8,128)(2,1)} %get-tuple-element.48), channel_id=1, source_target_pairs={{0,16},{4,20},{8,24},{12,28},{16,32},{20,36},{24,40},{28,44},{32,4... | collective-permute-start | bytes 1253384 | tf_op jit(solution)/shard_map/ppermute | solution.py:422
  54.0 12.8 %collective-permute-start.23 = (bf16[816,256]{1,0:T(8,128)(2,1)}, bf16[816,256]{1,0:T(8,128)(2,1)S(1)}, u32[]{:S(2)}, u32[]{:S(2)}) collective-permute-start(bf16[816,256]{1,0:T(8,128)(2,1)} %get-tuple-element.50), channel_id=1, source_target_pairs={{0,16},{4,20},{8,24},{12,28},{16,32},{20,36},{24,40},{28,44},{32,4... | collective-permute-start | bytes 1253384 | tf_op jit(solution)/shard_map/ppermute | solution.py:423
  54.0 0.8 copy-start.2
  56.6 8.7 %collective-permute-start.22 = (bf16[272,256]{1,0:T(8,128)(2,1)}, bf16[272,256]{1,0:T(8,128)(2,1)S(1)}, u32[]{:S(2)}, u32[]{:S(2)}) collective-permute-start(bf16[272,256]{1,0:T(8,128)(2,1)} %get-tuple-element.49), channel_id=1, source_target_pairs={{0,16},{4,20},{8,24},{12,28},{16,32},{20,36},{24,40},{28,44},{32,4... | collective-permute-start | bytes 417800 | tf_op jit(solution)/shard_map/ppermute | solution.py:422
  58.3 8.5 %collective-permute-start.24 = (bf16[272,256]{1,0:T(8,128)(2,1)}, bf16[272,256]{1,0:T(8,128)(2,1)S(1)}, u32[]{:S(2)}, u32[]{:S(2)}) collective-permute-start(bf16[272,256]{1,0:T(8,128)(2,1)} %get-tuple-element.51), channel_id=1, source_target_pairs={{0,16},{4,20},{8,24},{12,28},{16,32},{20,36},{24,40},{28,44},{32,4... | collective-permute-start | bytes 417800 | tf_op jit(solution)/shard_map/ppermute | solution.py:423
  65.3 1.5 copy-start.12
  66.8 0.7 copy-start.13
  66.8 0.8 copy-start.10
  66.8 0.9 copy-start.11
  81.7 23.5 %collective-permute-start.25 = (bf16[1024,256]{1,0:T(8,128)(2,1)}, bf16[1024,256]{1,0:T(8,128)(2,1)S(1)}, u32[]{:S(2)}, u32[]{:S(2)}) collective-permute-start(bf16[1024,256]{1,0:T(8,128)(2,1)} %get-tuple-element.53), channel_id=1, source_target_pairs={{0,240},{4,244},{8,248},{12,252},{16,0},{20,4},{24,8},{28,12},{32,... | collective-permute-start | bytes 1572872 | tf_op jit(solution)/shard_map/ppermute | solution.py:422
  88.0 17.3 %collective-permute-start.28 = (bf16[1024,256]{1,0:T(8,128)(2,1)}, bf16[1024,256]{1,0:T(8,128)(2,1)S(1)}, u32[]{:S(2)}, u32[]{:S(2)}) collective-permute-start(bf16[1024,256]{1,0:T(8,128)(2,1)} %get-tuple-element.57), channel_id=1, source_target_pairs={{0,252},{4,240},{8,244},{12,248},{16,0},{20,4},{24,8},{28,12},{32,... | collective-permute-start | bytes 1572872 | tf_op jit(solution)/shard_map/ppermute | solution.py:423
  88.1 13.2 %collective-permute-start.26 = (bf16[256,512]{1,0:T(8,128)(2,1)}, bf16[256,512]{1,0:T(8,128)(2,1)S(1)}, u32[]{:S(2)}, u32[]{:S(2)}) collective-permute-start(bf16[256,512]{1,0:T(8,128)(2,1)} %get-tuple-element.54), channel_id=1, source_target_pairs={{0,12},{4,0},{8,4},{12,8},{1,13},{5,1},{9,5},{13,9},{2,14},{6,2},{... | collective-permute-start | bytes 786440 | tf_op jit(solution)/shard_map/ppermute | solution.py:24
  92.1 13.2 %collective-permute-start.27 = (bf16[256,512]{1,0:T(8,128)(2,1)}, bf16[256,512]{1,0:T(8,128)(2,1)S(1)}, u32[]{:S(2)}, u32[]{:S(2)}) collective-permute-start(bf16[256,512]{1,0:T(8,128)(2,1)} %get-tuple-element.55), channel_id=1, source_target_pairs={{0,4},{4,8},{8,12},{12,0},{1,5},{5,9},{9,13},{13,1},{2,6},{6,10},{... | collective-permute-start | bytes 786440 | tf_op jit(solution)/shard_map/ppermute | solution.py:24
  101.3 7.7 %copy-start.8 = (bf16[256,512]{1,0:T(8,128)(2,1)}, bf16[256,512]{1,0:T(8,128)(2,1)S(1)}, u32[]{:S(2)}) copy-start(bf16[256,512]{1,0:T(8,128)(2,1)S(1)} %collective-permute-done.26.part_1) | copy-start | bytes 786436
  105.3 3.8 %copy-start.9 = (bf16[256,512]{1,0:T(8,128)(2,1)}, bf16[256,512]{1,0:T(8,128)(2,1)S(1)}, u32[]{:S(2)}) copy-start(bf16[256,512]{1,0:T(8,128)(2,1)S(1)} %collective-permute-done.27.part_3) | copy-start | bytes 786436
  105.3 0.8 copy-start.4
  105.3 1.0 copy-start.5
  109.1 48.1 %collective-permute-start.30 = (bf16[512,512]{1,0:T(8,128)(2,1)}, bf16[512,512]{1,0:T(8,128)(2,1)S(1)}, u32[]{:S(2)}, u32[]{:S(2)}) collective-permute-start(bf16[512,512]{1,0:T(8,128)(2,1)} %get-tuple-element.61), channel_id=1, source_target_pairs={{0,8},{4,12},{8,0},{12,4},{1,9},{5,13},{9,1},{13,5},{2,10},{6,14},... | collective-permute-start | bytes 1572872 | tf_op jit(solution)/shard_map/ppermute | solution.py:24
  110.5 46.7 %collective-permute-start.29 = (bf16[256,512]{1,0:T(8,128)(2,1)}, bf16[256,512]{1,0:T(8,128)(2,1)S(1)}, u32[]{:S(2)}, u32[]{:S(2)}) collective-permute-start(bf16[256,512]{1,0:T(8,128)(2,1)} %get-tuple-element.60), channel_id=1, source_target_pairs={{0,12},{4,0},{8,4},{12,8},{1,13},{5,1},{9,5},{13,9},{2,14},{6,2},{... | collective-permute-start | bytes 786440 | tf_op jit(solution)/shard_map/ppermute | solution.py:24
  112.4 44.7 %collective-permute-start.31 = (bf16[256,512]{1,0:T(8,128)(2,1)}, bf16[256,512]{1,0:T(8,128)(2,1)S(1)}, u32[]{:S(2)}, u32[]{:S(2)}) collective-permute-start(bf16[256,512]{1,0:T(8,128)(2,1)} %get-tuple-element.62), channel_id=1, source_target_pairs={{0,4},{4,8},{8,12},{12,0},{1,5},{5,9},{9,13},{13,1},{2,6},{6,10},{... | collective-permute-start | bytes 786440 | tf_op jit(solution)/shard_map/ppermute | solution.py:24
  114.9 2.5 %collective-permute-start.9 = (f32[1,512]{1,0:T(1,128)S(1)}, f32[1,512]{1,0:T(1,128)S(1)}, u32[]{:S(2)}, u32[]{:S(2)}) collective-permute-start(f32[1,512]{1,0:T(1,128)S(1)} %param.1), channel_id=1, source_target_pairs={{0,1},{1,0},{2,3},{3,2},{4,5},{5,4},{6,7},{7,6},{8,9},{9,8},{10,11... | collective-permute-start | bytes 6152 | tf_op jit(solution)/shard_map/cond/branch_1_fun/ppermute | solution.py:440
  117.4 3.9 %collective-permute-start.10 = (f32[1,512]{1,0:T(1,128)S(1)}, f32[1,512]{1,0:T(1,128)S(1)}, u32[]{:S(2)}, u32[]{:S(2)}) collective-permute-start(f32[1,512]{1,0:T(1,128)S(1)} %add.33), channel_id=1, source_target_pairs={{0,2},{1,3},{2,0},{3,1},{4,6},{5,7},{6,4},{7,5},{8,10},{9,11},{10,... | collective-permute-start | bytes 6152 | tf_op jit(solution)/shard_map/cond/branch_1_fun/ppermute | solution.py:440
  121.4 2.7 %collective-permute-start.11 = (f32[1,512]{1,0:T(1,128)S(1)}, f32[1,512]{1,0:T(1,128)S(1)}, u32[]{:S(2)}, u32[]{:S(2)}) collective-permute-start(f32[1,512]{1,0:T(1,128)S(1)} %add.34), channel_id=1, source_target_pairs={{0,32},{16,48},{32,0},{48,16},{64,96},{80,112},{96,64},{112,80},{1... | collective-permute-start | bytes 6152 | tf_op jit(solution)/shard_map/cond/branch_1_fun/ppermute | solution.py:440
  124.1 4.2 %collective-permute-start.12 = (f32[1,512]{1,0:T(1,128)S(1)}, f32[1,512]{1,0:T(1,128)S(1)}, u32[]{:S(2)}, u32[]{:S(2)}) collective-permute-start(f32[1,512]{1,0:T(1,128)S(1)} %add.35), channel_id=1, source_target_pairs={{0,64},{16,80},{32,96},{48,112},{64,0},{80,16},{96,32},{112,48},{1... | collective-permute-start | bytes 6152 | tf_op jit(solution)/shard_map/cond/branch_1_fun/ppermute | solution.py:440
  128.4 12.4 %collective-permute-start.13 = (f32[1,512]{1,0:T(1,128)S(1)}, f32[1,512]{1,0:T(1,128)S(1)}, u32[]{:S(2)}, u32[]{:S(2)}) collective-permute-start(f32[1,512]{1,0:T(1,128)S(1)} %add.36), channel_id=1, source_target_pairs={{0,16},{16,0},{32,48},{48,32},{64,80},{80,64},{96,112},{112,96},{1... | collective-permute-start | bytes 6152 | tf_op jit(solution)/shard_map/cond/branch_1_fun/ppermute | solution.py:440
  140.7 3.2 %collective-permute-start.14 = (f32[1,256]{1,0:T(1,128)S(1)}, f32[1,256]{1,0:T(1,128)S(1)}, u32[]{:S(2)}, u32[]{:S(2)}) collective-permute-start(f32[1,256]{1,0:T(1,128)S(1)} %get-tuple-element.80), channel_id=1, source_target_pairs={{0,128},{4,132},{8,136},{12,140},{16,144},{20,148},{24,152},{28,15... | collective-permute-start | bytes 3080 | tf_op jit(solution)/shard_map/cond/branch_1_fun/ppermute | solution.py:422
  141.1 6.2 %collective-permute-start.15 = (f32[1,256]{1,0:T(1,128)S(1)}, f32[1,256]{1,0:T(1,128)S(1)}, u32[]{:S(2)}, u32[]{:S(2)}) collective-permute-start(f32[1,256]{1,0:T(1,128)S(1)} %get-tuple-element.81), channel_id=1, source_target_pairs={{0,140},{4,128},{8,132},{12,136},{16,156},{20,144},{24,148},{28,15... | collective-permute-start | bytes 3080 | tf_op jit(solution)/shard_map/cond/branch_1_fun/ppermute | solution.py:423
  147.3 3.3 %collective-permute-start.16 = (f32[1,512]{1,0:T(1,128)S(1)}, f32[1,512]{1,0:T(1,128)S(1)}, u32[]{:S(2)}, u32[]{:S(2)}) collective-permute-start(f32[1,512]{1,0:T(1,128)S(1)} %maximum_add_fusion.1), channel_id=1, source_target_pairs={{0,4},{4,0},{8,12},{12,8},{1,5},{5,1},{9,13},{13,9},{2,6},{6,2},{1... | collective-permute-start | bytes 6152 | tf_op jit(solution)/shard_map/cond/branch_1_fun/ppermute | solution.py:430
  150.6 6.5 %collective-permute-start.17 = (f32[2,512]{1,0:T(2,128)S(1)}, f32[2,512]{1,0:T(2,128)S(1)}, u32[]{:S(2)}, u32[]{:S(2)}) collective-permute-start(f32[2,512]{1,0:T(2,128)S(1)} %pad_maximum_fusion.3), channel_id=1, source_target_pairs={{0,8},{4,12},{8,0},{12,4},{1,9},{5,13},{9,1},{13,5},{2,10},{6,14},... | collective-permute-start | bytes 12296 | tf_op jit(solution)/shard_map/cond/branch_1_fun/ppermute | solution.py:430
  157.1 0.7 copy-start.6
  157.1 0.8 copy-start.7
  157.2 0.9 copy-start.3

commit v3 on v2

--- a/solution.py
+++ b/solution.py
@@ -116,34 +116,13 @@
     return copies
 
 
-def unpack_early_kernel(part_0, part_1, part_3, attended, query_grad, sems):
-    outs = (attended, query_grad)
-    copies = copies_out(0, part_0, 0, outs, sems.at[0])
-    copies += copies_out(1, part_1, 0, outs, sems.at[1])
-    copies += copies_out(3, part_3, 0, outs, sems.at[2])
-    for copy in copies:
-        copy.start()
-    for copy in copies:
-        copy.wait()
-
-
-def unpack_early(parts):
-    out = jax.ShapeDtypeStruct((1, ROWS, parts[0].shape[1] * SHARDS), BF16)
-    return pl.pallas_call(
-        unpack_early_kernel,
-        out_shape=(out, out),
-        in_specs=[vmem_spec()] * 3,
-        out_specs=(any_spec(), any_spec()),
-        scratch_shapes=[pltpu.SemaphoreType.DMA((3, 4))],
-        compiler_params=pltpu.CompilerParams(vmem_limit_bytes=VMEM_BYTES),
-        name="unpack_early",
-    )(*parts)
-
-
 def unpack_kernel(gain_scale, *refs):
     parts, terms = refs[:SHARDS], refs[SHARDS]
-    attended, query_grad, key_grad, value_grad, gain_grad, sems = refs[SHARDS + 3 :]
+    part_0, part_1, part_3 = refs[SHARDS + 1 : SHARDS + 4]
+    attended, query_grad, key_grad, value_grad, gain_grad, sems = refs[SHARDS + 4 :]
     copies = []
+    for n, (k, part) in enumerate(((0, part_0), (1, part_1), (3, part_3))):
+        copies += copies_out(k, part, 0, (attended, query_grad), sems.at[SHARDS + 1 + n])
     for k, part in enumerate(parts):
         copies += copies_out(k, part, 0, (key_grad, value_grad), sems.at[k])
     copies += copies_out(2, parts[2], 2 * ROWS, (attended, query_grad), sems.at[SHARDS])
@@ -156,19 +135,18 @@
         copy.wait()
 
 
-def unpack(parts, terms, attended, query_grad, gain_scale):
-    out = jax.ShapeDtypeStruct(attended.shape, BF16)
-    count = SHARDS + 1
+def unpack(parts, terms, early, gain_scale):
+    channels = terms.shape[1] * SHARDS
+    out = jax.ShapeDtypeStruct((1, ROWS, channels), BF16)
     return pl.pallas_call(
         functools.partial(unpack_kernel, gain_scale),
-        out_shape=(out,) * 4 + (jax.ShapeDtypeStruct((1, attended.shape[2]), F32),),
-        in_specs=[vmem_spec()] * count + [any_spec()] * 2,
+        out_shape=(out,) * 4 + (jax.ShapeDtypeStruct((1, channels), F32),),
+        in_specs=[vmem_spec()] * (2 * SHARDS),
         out_specs=(any_spec(),) * 4 + (vmem_spec(),),
-        scratch_shapes=[pltpu.SemaphoreType.DMA((SHARDS + 1, 4))],
-        input_output_aliases={count: 0, count + 1: 1},
+        scratch_shapes=[pltpu.SemaphoreType.DMA((2 * SHARDS, 4))],
         compiler_params=pltpu.CompilerParams(vmem_limit_bytes=VMEM_BYTES),
         name="unpack",
-    )(*parts, terms, attended, query_grad)
+    )(*parts, terms, *early)
 
 
 def dot_nn(a, b):
@@ -465,8 +443,6 @@
     parts = finish(own_part, (back_0, back_1), ad[2], gain_row)
     term, ad_0, _ = lax.optimization_barrier((term, ad[0], parts[0]))
     parts = [parts[0]] + [permuted(parts[k], "inner", -k) for k in range(1, SHARDS)]
-    attended, query_grad = unpack_early((ad_0, ad_1, ad_3))
-    term, attended = lax.optimization_barrier((term, attended))
     terms = lax.cond(
         start[0] >= 0,
         functools.partial(sum_by_steps, STEPS),
@@ -477,7 +453,7 @@
         ROWS * lax.axis_size("inner") * lax.axis_size("outer") * lax.axis_size("dp")
     )
     attended, query_grad, key_grad, value_grad, gain_grad = unpack(
-        parts, terms, attended, query_grad, 1.0 / math.sqrt(token_count)
+        parts, terms, (ad_0, ad_1, ad_3), 1.0 / math.sqrt(token_count)
     )
     return attended, query_grad, key_grad, value_grad, gain_grad.reshape(-1)
 

time: 163 us -> 164 us (level)
  waiting for transfers between devices: 71.4 us -> 73.2 us
    ppermute x4, waiting for transfers between devices: 4.89 us -> 7.01 us  [shifted_halves(): lax.ppermute(x, axes, turned)]
    pallas_call x1 -> x0, Pallas kernels: 2.07 us -> none  [unpack_early(): pl.pallas_call(unpack_early_kernel, out_shape=(out, out), in_specs=[vmem_...]
  transfers between devices with their start and end apart: 23 -> 23, of which waited for: 14 -> 14; matrix products, arithmetic and copies ran while one was open for 0% -> 0% of each run, Pallas kernels for 4% -> 2%
where the time goes in v3:
time: 164 us; the launch traced here: 163 us
  waiting for transfers between devices  73.2 us (45%)
  starting transfers between devices  54.3 us (33%)
  Pallas kernels  27.7 us (17%)
  local copies, waits for them, and re-layouts  5.09 us (3%)
    ppermute x8, waiting for transfers between devices, permuted(): return lax.ppermute(value, axis, pairs)  46.8 us
    ppermute x8, starting transfers between devices, permuted(): return lax.ppermute(value, axis, pairs)  19.1 us
    ppermute x5, starting transfers between devices, sum_by_steps(): term = term + lax.ppermute(term, axis, pairs)  18.6 us
    pallas_call x1, Pallas kernels, attend(): pl.pallas_call(attend_kernel, grid_spec=pltpu.PrefetchScalarGridSpec(num_...  14 us
    ppermute x4, starting transfers between devices, shifted_halves(): lax.ppermute(x, axes, straight)  10.5 us
    ppermute x5, waiting for transfers between devices, sum_by_steps(): term = term + lax.ppermute(term, axis, pairs)  7.06 us
    ppermute x4, waiting for transfers between devices, shifted_halves(): lax.ppermute(x, axes, turned)  7.01 us
    ppermute x2, waiting for transfers between devices, gathered(): term = jnp.concatenate([term, lax.ppermute(term, 'inner', pairs)])  6.68 us
  transfers between devices with their start and end apart: 23, of which 14 were waited for; matrix products, arithmetic and copies ran while one was open for 0% of the time, Pallas kernels for 2%

profile of v3, /device:TPU:1, one launch (start us, length us, event | category | flops | bytes accessed | tf_op | source)
XLA Modules:
  0.0 162.5 jit_solution(15798843788704020175)
XLA Ops:
  0.6 3.2 %pack.1 = (bf16[528,512]{1,0:T(8,128)(2,1)}, bf16[528,512]{1,0:T(8,128)(2,1)}, bf16[528,512]{1,0:T(8,128)(2,1)}, bf16[528,512]{1,0:T(8,128)(2,1)}) custom-call(s32[2]{0:T(128)} %order.1, bf16[1,128,2048]{2,1,0:T(8,128)(2,1)} %queries.1, bf16[1,128,2048]{2,1,0:T(8,128)(2,1)} %keys.1, bf16[1,128,2048]{2,1,0:T(8,128)(2,1)} %values.1, bf16[1,128,2048]{2,1,0:T(8,128)(2,1)} %grads.1), custom_call_target="tpu_custom_call" | custom-call | tf_op jit(solution)/shard_map/pack/pallas_call | solution.py:99
  3.8 3.8 %collective-permute-start.18 = (bf16[528,512]{1,0:T(8,128)(2,1)}, bf16[528,512]{1,0:T(8,128)(2,1)S(1)}, u32[]{:S(2)}, u32[]{:S(2)}) collective-permute-start(bf16[528,512]{1,0:T(8,128)(2,1)} %get-tuple-element.41), channel_id=1, source_target_pairs={{0,4},{4,8},{8,12},{12,0},{1,5},{5,9},{9,13},{13,1},{2,6},{6,10},{... | collective-permute-start | bytes 1622024 | tf_op jit(solution)/shard_map/ppermute | solution.py:24
  7.6 3.0 %collective-permute-start.20 = (bf16[528,512]{1,0:T(8,128)(2,1)}, bf16[528,512]{1,0:T(8,128)(2,1)S(1)}, u32[]{:S(2)}, u32[]{:S(2)}) collective-permute-start(bf16[528,512]{1,0:T(8,128)(2,1)} %get-tuple-element.43), channel_id=1, source_target_pairs={{0,12},{4,0},{8,4},{12,8},{1,13},{5,1},{9,5},{13,9},{2,14},{6,2},{... | collective-permute-start | bytes 1622024 | tf_op jit(solution)/shard_map/ppermute | solution.py:24
  10.6 4.5 %collective-permute-start.19 = (bf16[528,512]{1,0:T(8,128)(2,1)}, bf16[528,512]{1,0:T(8,128)(2,1)S(1)}, u32[]{:S(2)}, u32[]{:S(2)}) collective-permute-start(bf16[528,512]{1,0:T(8,128)(2,1)} %get-tuple-element.42), channel_id=1, source_target_pairs={{0,8},{4,12},{8,0},{12,4},{1,9},{5,13},{9,1},{13,5},{2,10},{6,14},... | collective-permute-start | bytes 1622024 | tf_op jit(solution)/shard_map/ppermute | solution.py:24
  15.1 12.1 %collective-permute-done.18.refs_1_ = bf16[528,512]{1,0:T(8,128)(2,1)S(1)} collective-permute-done((bf16[528,512]{1,0:T(8,128)(2,1)}, bf16[528,512]{1,0:T(8,128)(2,1)S(1)}, u32[]{:S(2)}, u32[]{:S(2)}) %collective-permute-start.18) | collective-permute-done | bytes 540704 | tf_op jit(solution)/shard_map/ppermute | solution.py:24
  27.2 21.5 %collective-permute-done.20.refs_2_.refs_3_ = bf16[528,512]{1,0:T(8,128)(2,1)S(1)} collective-permute-done((bf16[528,512]{1,0:T(8,128)(2,1)}, bf16[528,512]{1,0:T(8,128)(2,1)S(1)}, u32[]{:S(2)}, u32[]{:S(2)}) %collective-permute-start.20) | collective-permute-done | bytes 540704 | tf_op jit(solution)/shard_map/ppermute | solution.py:24
  48.7 0.8 copy-done.1
  49.5 2.3 %join.2 = (bf16[816,256]{1,0:T(8,128)(2,1)}, bf16[816,256]{1,0:T(8,128)(2,1)}) custom-call(bf16[528,512]{1,0:T(8,128)(2,1)} %get-tuple-element.40.refs_0_, bf16[528,512]{1,0:T(8,128)(2,1)} %copy-done, bf16[528,512]{1,0:T(8,128)(2,1)} %copy-done.1), custom_call_target="tpu_custom_call" | custom-call | tf_op jit(solution)/shard_map/join/pallas_call | solution.py:81
  51.8 2.2 %collective-permute-start.21 = (bf16[816,256]{1,0:T(8,128)(2,1)}, bf16[816,256]{1,0:T(8,128)(2,1)S(1)}, u32[]{:S(2)}, u32[]{:S(2)}) collective-permute-start(bf16[816,256]{1,0:T(8,128)(2,1)} %get-tuple-element.44), channel_id=1, source_target_pairs={{0,16},{4,20},{8,24},{12,28},{16,32},{20,36},{24,40},{28,44},{32,4... | collective-permute-start | bytes 1253384 | tf_op jit(solution)/shard_map/ppermute | solution.py:400
  54.0 0.0 collective-permute-start.23
  54.0 0.0 collective-permute-done.19.refs_0_.refs_2_
  54.0 0.8 copy-done.2
  54.9 1.8 %join.3 = (bf16[272,256]{1,0:T(8,128)(2,1)}, bf16[272,256]{1,0:T(8,128)(2,1)}) custom-call(bf16[528,512]{1,0:T(8,128)(2,1)} %copy-done.2), custom_call_target="tpu_custom_call" | custom-call | tf_op jit(solution)/shard_map/join/pallas_call | solution.py:81
  56.6 1.7 %collective-permute-start.22 = (bf16[272,256]{1,0:T(8,128)(2,1)}, bf16[272,256]{1,0:T(8,128)(2,1)S(1)}, u32[]{:S(2)}, u32[]{:S(2)}) collective-permute-start(bf16[272,256]{1,0:T(8,128)(2,1)} %get-tuple-element.45), channel_id=1, source_target_pairs={{0,16},{4,20},{8,24},{12,28},{16,32},{20,36},{24,40},{28,44},{32,4... | collective-permute-start | bytes 417800 | tf_op jit(solution)/shard_map/ppermute | solution.py:400
  58.3 0.0 collective-permute-start.24
  59.0 0.6 pad_add_fusion.scalars
  59.6 5.7 %collective-permute-done.22.refs_5_ = bf16[272,256]{1,0:T(8,128)(2,1)S(1)} collective-permute-done((bf16[272,256]{1,0:T(8,128)(2,1)}, bf16[272,256]{1,0:T(8,128)(2,1)S(1)}, u32[]{:S(2)}, u32[]{:S(2)}) %collective-permute-start.22) | collective-permute-done | bytes 139296 | tf_op jit(solution)/shard_map/ppermute | solution.py:400
  65.3 1.5 collective-permute-done.24.refs_7_
  66.8 0.0 collective-permute-done.21.refs_4_
  66.8 0.0 collective-permute-done.23.refs_6_
  66.8 0.0 copy-start.11
  66.8 0.6 copy-done.13
  67.4 0.2 copy-done.10
  67.6 0.1 copy-done.11
  67.7 14.0 %attend.1 = (bf16[256,512]{1,0:T(8,128)(2,1)}, bf16[256,512]{1,0:T(8,128)(2,1)}, bf16[256,512]{1,0:T(8,128)(2,1)}, bf16[256,512]{1,0:T(8,128)(2,1)}, bf16[1024,5...) custom-call(s32[3]{0:T(128)} %pad_add_fusion.scalars, ...), custom_call_target="tpu_custom_call" | custom-call | flops 2415919104 | bytes 7340032 | tf_op jit(solution)/shard_map/attend/pallas_call | solution.py:317
  81.8 6.3 %collective-permute-start.25 = (bf16[1024,256]{1,0:T(8,128)(2,1)}, bf16[1024,256]{1,0:T(8,128)(2,1)S(1)}, u32[]{:S(2)}, u32[]{:S(2)}) collective-permute-start(bf16[1024,256]{1,0:T(8,128)(2,1)} %get-tuple-element.49), channel_id=1, source_target_pairs={{0,240},{4,244},{8,248},{12,252},{16,0},{20,4},{24,8},{28,12},{32,... | collective-permute-start | bytes 1572872 | tf_op jit(solution)/shard_map/ppermute | solution.py:400
  88.0 0.1 collective-permute-start.28
  88.1 4.0 %collective-permute-start.26 = (bf16[256,512]{1,0:T(8,128)(2,1)}, bf16[256,512]{1,0:T(8,128)(2,1)S(1)}, u32[]{:S(2)}, u32[]{:S(2)}) collective-permute-start(bf16[256,512]{1,0:T(8,128)(2,1)} %get-tuple-element.50), channel_id=1, source_target_pairs={{0,12},{4,0},{8,4},{12,8},{1,13},{5,1},{9,5},{13,9},{2,14},{6,2},{... | collective-permute-start | bytes 786440 | tf_op jit(solution)/shard_map/ppermute | solution.py:24
  92.1 0.0 collective-permute-start.27
  92.1 9.2 %collective-permute-done.26.refs_6_ = bf16[256,512]{1,0:T(8,128)(2,1)S(1)} collective-permute-done((bf16[256,512]{1,0:T(8,128)(2,1)}, bf16[256,512]{1,0:T(8,128)(2,1)S(1)}, u32[]{:S(2)}, u32[]{:S(2)}) %collective-permute-start.26) | collective-permute-done | bytes 262176 | tf_op jit(solution)/shard_map/ppermute | solution.py:24
  101.3 4.0 %collective-permute-done.27.refs_7_ = bf16[256,512]{1,0:T(8,128)(2,1)S(1)} collective-permute-done((bf16[256,512]{1,0:T(8,128)(2,1)}, bf16[256,512]{1,0:T(8,128)(2,1)S(1)}, u32[]{:S(2)}, u32[]{:S(2)}) %collective-permute-start.27) | collective-permute-done | bytes 262176 | tf_op jit(solution)/shard_map/ppermute | solution.py:24
  105.3 0.0 collective-permute-done.25.back_0
  105.3 0.0 collective-permute-done.28.back_1
  105.3 0.0 copy-start.5
  105.3 0.8 copy-done.4
  106.1 0.2 copy-done.5
  106.3 2.8 %finish.1 = (bf16[256,512]{1,0:T(8,128)(2,1)}, bf16[256,512]{1,0:T(8,128)(2,1)}, bf16[512,512]{1,0:T(8,128)(2,1)}, bf16[256,512]{1,0:T(8,128)(2,1)}) custom-call(f32[1,2048]{1,0:T(1,128)} %bitcast.6, bf16[1024,512]{1,0:T(8,128)(2,1)} %get-tuple-element.48.own, bf16[1024,256]{1,0:T(8,128)(2,1)} %copy-done.4, bf16[1024,256]{1,0:T(8,128)(2,1)} %copy-done.5, ...), custom_call_target="tpu_custom_call" | custom-call | flops 1048576 | bytes 3145728 | tf_op jit(solution)/shard_map/finish/pallas_call | solution.py:373
  109.1 1.4 collective-permute-start.30
  110.5 2.0 %collective-permute-start.29 = (bf16[256,512]{1,0:T(8,128)(2,1)}, bf16[256,512]{1,0:T(8,128)(2,1)S(1)}, u32[]{:S(2)}, u32[]{:S(2)}) collective-permute-start(bf16[256,512]{1,0:T(8,128)(2,1)} %get-tuple-element.56), channel_id=1, source_target_pairs={{0,12},{4,0},{8,4},{12,8},{1,13},{5,1},{9,5},{13,9},{2,14},{6,2},{... | collective-permute-start | bytes 786440 | tf_op jit(solution)/shard_map/ppermute | solution.py:24
  112.5 0.4 collective-permute-start.31
  112.8 44.2 %conditional.1 = (f32[4,512]{1,0:T(4,128)S(1)}) conditional(s32[]{:T(128)} %bitcast.3, f32[1,512]{1,0:T(1,128)S(1)} %get-tuple-element.61, f32[1,512]{1,0:T(1,128)S(1)} %get-tuple-element.61), branch_computations={%region_0.1_spmd, %region_1.2_spmd} | conditional | flops 8704 | bytes 139632 | solution.py:446
  112.8 1.2 collective-permute-start.9
  114.1 1.2 collective-permute-done.9
  115.3 2.7 %collective-permute-start.10 = (f32[1,512]{1,0:T(1,128)S(1)}, f32[1,512]{1,0:T(1,128)S(1)}, u32[]{:S(2)}, u32[]{:S(2)}) collective-permute-start(f32[1,512]{1,0:T(1,128)S(1)} %add.33), channel_id=1, source_target_pairs={{0,2},{1,3},{2,0},{3,1},{4,6},{5,7},{6,4},{7,5},{8,10},{9,11},{10,... | collective-permute-start | bytes 6152 | tf_op jit(solution)/shard_map/cond/branch_1_fun/ppermute | solution.py:418
  118.0 1.2 collective-permute-done.10
  119.2 0.0 collective-permute-start.11
  119.2 2.4 %collective-permute-done.11 = f32[1,512]{1,0:T(1,128)S(1)} collective-permute-done((f32[1,512]{1,0:T(1,128)S(1)}, f32[1,512]{1,0:T(1,128)S(1)}, u32[]{:S(2)}, u32[]{:S(2)}) %collective-permute-start.11) | collective-permute-done | bytes 2080 | tf_op jit(solution)/shard_map/cond/branch_1_fun/ppermute | solution.py:418
  121.7 2.8 %collective-permute-start.12 = (f32[1,512]{1,0:T(1,128)S(1)}, f32[1,512]{1,0:T(1,128)S(1)}, u32[]{:S(2)}, u32[]{:S(2)}) collective-permute-start(f32[1,512]{1,0:T(1,128)S(1)} %add.35), channel_id=1, source_target_pairs={{0,64},{16,80},{32,96},{48,112},{64,0},{80,16},{96,32},{112,48},{1... | collective-permute-start | bytes 6152 | tf_op jit(solution)/shard_map/cond/branch_1_fun/ppermute | solution.py:418
  124.5 1.4 collective-permute-done.12
  125.9 11.8 %collective-permute-start.13 = (f32[1,512]{1,0:T(1,128)S(1)}, f32[1,512]{1,0:T(1,128)S(1)}, u32[]{:S(2)}, u32[]{:S(2)}) collective-permute-start(f32[1,512]{1,0:T(1,128)S(1)} %add.36), channel_id=1, source_target_pairs={{0,16},{16,0},{32,48},{48,32},{64,80},{80,64},{96,112},{112,96},{1... | collective-permute-start | bytes 6152 | tf_op jit(solution)/shard_map/cond/branch_1_fun/ppermute | solution.py:418
  137.7 0.8 collective-permute-done.13
  138.6 0.4 collective-permute-start.14
  139.0 2.8 %collective-permute-start.15 = (f32[1,256]{1,0:T(1,128)S(1)}, f32[1,256]{1,0:T(1,128)S(1)}, u32[]{:S(2)}, u32[]{:S(2)}) collective-permute-start(f32[1,256]{1,0:T(1,128)S(1)} %get-tuple-element.73), channel_id=1, source_target_pairs={{0,140},{4,128},{8,132},{12,136},{16,156},{20,144},{24,148},{28,15... | collective-permute-start | bytes 3080 | tf_op jit(solution)/shard_map/cond/branch_1_fun/ppermute | solution.py:401
  141.7 0.0 collective-permute-done.14
  141.7 5.5 %collective-permute-done.15 = f32[1,256]{1,0:T(1,128)S(1)} collective-permute-done((f32[1,256]{1,0:T(1,128)S(1)}, f32[1,256]{1,0:T(1,128)S(1)}, u32[]{:S(2)}, u32[]{:S(2)}) %collective-permute-start.15) | collective-permute-done | bytes 1056 | tf_op jit(solution)/shard_map/cond/branch_1_fun/ppermute | solution.py:401
  147.3 0.6 collective-permute-start.16
  147.9 2.7 %collective-permute-done.16 = f32[1,512]{1,0:T(1,128)S(1)} collective-permute-done((f32[1,512]{1,0:T(1,128)S(1)}, f32[1,512]{1,0:T(1,128)S(1)}, u32[]{:S(2)}, u32[]{:S(2)}) %collective-permute-start.16) | collective-permute-done | bytes 2080 | tf_op jit(solution)/shard_map/cond/branch_1_fun/ppermute | solution.py:408
  150.6 2.5 %collective-permute-start.17 = (f32[2,512]{1,0:T(2,128)S(1)}, f32[2,512]{1,0:T(2,128)S(1)}, u32[]{:S(2)}, u32[]{:S(2)}) collective-permute-start(f32[2,512]{1,0:T(2,128)S(1)} %pad_maximum_fusion.3), channel_id=1, source_target_pairs={{0,8},{4,12},{8,0},{12,4},{1,9},{5,13},{9,1},{13,5},{2,10},{6,14},... | collective-permute-start | bytes 12296 | tf_op jit(solution)/shard_map/cond/branch_1_fun/ppermute | solution.py:408
  153.1 4.0 %collective-permute-done.17 = f32[2,512]{1,0:T(2,128)S(1)} collective-permute-done((f32[2,512]{1,0:T(2,128)S(1)}, f32[2,512]{1,0:T(2,128)S(1)}, u32[]{:S(2)}, u32[]{:S(2)}) %collective-permute-start.17) | collective-permute-done | bytes 4128 | tf_op jit(solution)/shard_map/cond/branch_1_fun/ppermute | solution.py:408
  157.1 0.0 collective-permute-done.29.refs_1_
  157.1 0.7 copy-done.8
  157.8 0.1 copy-done.9
  157.9 0.8 copy-done.3
  158.7 3.7 %unpack.1 = (bf16[1,128,2048]{2,1,0:T(8,128)(2,1)}, bf16[1,128,2048]{2,1,0:T(8,128)(2,1)}, bf16[1,128,2048]{2,1,0:T(8,128)(2,1)}, bf16[1,128,2048]{2,1,0:T(8,128)(2,1)}, f32[1,2048]{1,0:T(1,128)}) custom-call(bf16[256,512]{1,0:T(8,128)(2,1)} %get-tuple-element.55.refs_0_, bf16[256,512]{1,0:T(8,128)(2,1)} %copy-done.8, bf16[512,512]{1,0:T(8,128)(2,1)} %copy-done.3, ...), custom_call_target="tpu_custom_call" | custom-call | tf_op jit(solution)/shard_map/unpack/pallas_call | solution.py:141
  (27 shorter events, 0.1 us)
Async XLA Ops:
  3.8 23.4 %collective-permute-start.18 = (bf16[528,512]{1,0:T(8,128)(2,1)}, bf16[528,512]{1,0:T(8,128)(2,1)S(1)}, u32[]{:S(2)}, u32[]{:S(2)}) collective-permute-start(bf16[528,512]{1,0:T(8,128)(2,1)} %get-tuple-element.41), channel_id=1, source_target_pairs={{0,4},{4,8},{8,12},{12,0},{1,5},{5,9},{9,13},{13,1},{2,6},{6,10},{... | collective-permute-start | bytes 1622024 | tf_op jit(solution)/shard_map/ppermute | solution.py:24
  7.6 41.1 %collective-permute-start.20 = (bf16[528,512]{1,0:T(8,128)(2,1)}, bf16[528,512]{1,0:T(8,128)(2,1)S(1)}, u32[]{:S(2)}, u32[]{:S(2)}) collective-permute-start(bf16[528,512]{1,0:T(8,128)(2,1)} %get-tuple-element.43), channel_id=1, source_target_pairs={{0,12},{4,0},{8,4},{12,8},{1,13},{5,1},{9,5},{13,9},{2,14},{6,2},{... | collective-permute-start | bytes 1622024 | tf_op jit(solution)/shard_map/ppermute | solution.py:24
  10.6 43.4 %collective-permute-start.19 = (bf16[528,512]{1,0:T(8,128)(2,1)}, bf16[528,512]{1,0:T(8,128)(2,1)S(1)}, u32[]{:S(2)}, u32[]{:S(2)}) collective-permute-start(bf16[528,512]{1,0:T(8,128)(2,1)} %get-tuple-element.42), channel_id=1, source_target_pairs={{0,8},{4,12},{8,0},{12,4},{1,9},{5,13},{9,1},{13,5},{2,10},{6,14},... | collective-permute-start | bytes 1622024 | tf_op jit(solution)/shard_map/ppermute | solution.py:24
  27.2 21.5 %copy-start = (bf16[528,512]{1,0:T(8,128)(2,1)}, bf16[528,512]{1,0:T(8,128)(2,1)S(1)}, u32[]{:S(2)}) copy-start(bf16[528,512]{1,0:T(8,128)(2,1)S(1)} %collective-permute-done.18.refs_1_) | copy-start | bytes 1622020
  48.7 0.8 copy-start.1
  51.8 15.0 %collective-permute-start.21 = (bf16[816,256]{1,0:T(8,128)(2,1)}, bf16[816,256]{1,0:T(8,128)(2,1)S(1)}, u32[]{:S(2)}, u32[]{:S(2)}) collective-permute-start(bf16[816,256]{1,0:T(8,128)(2,1)} %get-tuple-element.44), channel_id=1, source_target_pairs={{0,16},{4,20},{8,24},{12,28},{16,32},{20,36},{24,40},{28,44},{32,4... | collective-permute-start | bytes 1253384 | tf_op jit(solution)/shard_map/ppermute | solution.py:400
  54.0 12.8 %collective-permute-start.23 = (bf16[816,256]{1,0:T(8,128)(2,1)}, bf16[816,256]{1,0:T(8,128)(2,1)S(1)}, u32[]{:S(2)}, u32[]{:S(2)}) collective-permute-start(bf16[816,256]{1,0:T(8,128)(2,1)} %get-tuple-element.46), channel_id=1, source_target_pairs={{0,16},{4,20},{8,24},{12,28},{16,32},{20,36},{24,40},{28,44},{32,4... | collective-permute-start | bytes 1253384 | tf_op jit(solution)/shard_map/ppermute | solution.py:401
  54.0 0.8 copy-start.2
  56.6 8.7 %collective-permute-start.22 = (bf16[272,256]{1,0:T(8,128)(2,1)}, bf16[272,256]{1,0:T(8,128)(2,1)S(1)}, u32[]{:S(2)}, u32[]{:S(2)}) collective-permute-start(bf16[272,256]{1,0:T(8,128)(2,1)} %get-tuple-element.45), channel_id=1, source_target_pairs={{0,16},{4,20},{8,24},{12,28},{16,32},{20,36},{24,40},{28,44},{32,4... | collective-permute-start | bytes 417800 | tf_op jit(solution)/shard_map/ppermute | solution.py:400
  58.3 8.5 %collective-permute-start.24 = (bf16[272,256]{1,0:T(8,128)(2,1)}, bf16[272,256]{1,0:T(8,128)(2,1)S(1)}, u32[]{:S(2)}, u32[]{:S(2)}) collective-permute-start(bf16[272,256]{1,0:T(8,128)(2,1)} %get-tuple-element.47), channel_id=1, source_target_pairs={{0,16},{4,20},{8,24},{12,28},{16,32},{20,36},{24,40},{28,44},{32,4... | collective-permute-start | bytes 417800 | tf_op jit(solution)/shard_map/ppermute | solution.py:401
  65.3 1.5 copy-start.12
  66.8 0.6 copy-start.13
  66.8 0.8 copy-start.10
  66.8 0.9 copy-start.11
  81.8 23.5 %collective-permute-start.25 = (bf16[1024,256]{1,0:T(8,128)(2,1)}, bf16[1024,256]{1,0:T(8,128)(2,1)S(1)}, u32[]{:S(2)}, u32[]{:S(2)}) collective-permute-start(bf16[1024,256]{1,0:T(8,128)(2,1)} %get-tuple-element.49), channel_id=1, source_target_pairs={{0,240},{4,244},{8,248},{12,252},{16,0},{20,4},{24,8},{28,12},{32,... | collective-permute-start | bytes 1572872 | tf_op jit(solution)/shard_map/ppermute | solution.py:400
  88.0 17.3 %collective-permute-start.28 = (bf16[1024,256]{1,0:T(8,128)(2,1)}, bf16[1024,256]{1,0:T(8,128)(2,1)S(1)}, u32[]{:S(2)}, u32[]{:S(2)}) collective-permute-start(bf16[1024,256]{1,0:T(8,128)(2,1)} %get-tuple-element.53), channel_id=1, source_target_pairs={{0,252},{4,240},{8,244},{12,248},{16,0},{20,4},{24,8},{28,12},{32,... | collective-permute-start | bytes 1572872 | tf_op jit(solution)/shard_map/ppermute | solution.py:401
  88.1 13.2 %collective-permute-start.26 = (bf16[256,512]{1,0:T(8,128)(2,1)}, bf16[256,512]{1,0:T(8,128)(2,1)S(1)}, u32[]{:S(2)}, u32[]{:S(2)}) collective-permute-start(bf16[256,512]{1,0:T(8,128)(2,1)} %get-tuple-element.50), channel_id=1, source_target_pairs={{0,12},{4,0},{8,4},{12,8},{1,13},{5,1},{9,5},{13,9},{2,14},{6,2},{... | collective-permute-start | bytes 786440 | tf_op jit(solution)/shard_map/ppermute | solution.py:24
  92.1 13.2 %collective-permute-start.27 = (bf16[256,512]{1,0:T(8,128)(2,1)}, bf16[256,512]{1,0:T(8,128)(2,1)S(1)}, u32[]{:S(2)}, u32[]{:S(2)}) collective-permute-start(bf16[256,512]{1,0:T(8,128)(2,1)} %get-tuple-element.51), channel_id=1, source_target_pairs={{0,4},{4,8},{8,12},{12,0},{1,5},{5,9},{9,13},{13,1},{2,6},{6,10},{... | collective-permute-start | bytes 786440 | tf_op jit(solution)/shard_map/ppermute | solution.py:24
  101.3 7.8 %copy-start.6 = (bf16[256,512]{1,0:T(8,128)(2,1)}, bf16[256,512]{1,0:T(8,128)(2,1)S(1)}, u32[]{:S(2)}) copy-start(bf16[256,512]{1,0:T(8,128)(2,1)S(1)} %collective-permute-done.26.refs_6_) | copy-start | bytes 786436
  105.3 3.8 %copy-start.7 = (bf16[256,512]{1,0:T(8,128)(2,1)}, bf16[256,512]{1,0:T(8,128)(2,1)S(1)}, u32[]{:S(2)}) copy-start(bf16[256,512]{1,0:T(8,128)(2,1)S(1)} %collective-permute-done.27.refs_7_) | copy-start | bytes 786436
  105.3 0.8 copy-start.4
  105.3 1.0 copy-start.5
  109.1 48.0 %collective-permute-start.30 = (bf16[512,512]{1,0:T(8,128)(2,1)}, bf16[512,512]{1,0:T(8,128)(2,1)S(1)}, u32[]{:S(2)}, u32[]{:S(2)}) collective-permute-start(bf16[512,512]{1,0:T(8,128)(2,1)} %get-tuple-element.57), channel_id=1, source_target_pairs={{0,8},{4,12},{8,0},{12,4},{1,9},{5,13},{9,1},{13,5},{2,10},{6,14},... | collective-permute-start | bytes 1572872 | tf_op jit(solution)/shard_map/ppermute | solution.py:24
  110.5 46.6 %collective-permute-start.29 = (bf16[256,512]{1,0:T(8,128)(2,1)}, bf16[256,512]{1,0:T(8,128)(2,1)S(1)}, u32[]{:S(2)}, u32[]{:S(2)}) collective-permute-start(bf16[256,512]{1,0:T(8,128)(2,1)} %get-tuple-element.56), channel_id=1, source_target_pairs={{0,12},{4,0},{8,4},{12,8},{1,13},{5,1},{9,5},{13,9},{2,14},{6,2},{... | collective-permute-start | bytes 786440 | tf_op jit(solution)/shard_map/ppermute | solution.py:24
  112.5 44.6 %collective-permute-start.31 = (bf16[256,512]{1,0:T(8,128)(2,1)}, bf16[256,512]{1,0:T(8,128)(2,1)S(1)}, u32[]{:S(2)}, u32[]{:S(2)}) collective-permute-start(bf16[256,512]{1,0:T(8,128)(2,1)} %get-tuple-element.58), channel_id=1, source_target_pairs={{0,4},{4,8},{8,12},{12,0},{1,5},{5,9},{9,13},{13,1},{2,6},{6,10},{... | collective-permute-start | bytes 786440 | tf_op jit(solution)/shard_map/ppermute | solution.py:24
  112.8 2.4 %collective-permute-start.9 = (f32[1,512]{1,0:T(1,128)S(1)}, f32[1,512]{1,0:T(1,128)S(1)}, u32[]{:S(2)}, u32[]{:S(2)}) collective-permute-start(f32[1,512]{1,0:T(1,128)S(1)} %param.1), channel_id=1, source_target_pairs={{0,1},{1,0},{2,3},{3,2},{4,5},{5,4},{6,7},{7,6},{8,9},{9,8},{10,11... | collective-permute-start | bytes 6152 | tf_op jit(solution)/shard_map/cond/branch_1_fun/ppermute | solution.py:418
  115.3 3.9 %collective-permute-start.10 = (f32[1,512]{1,0:T(1,128)S(1)}, f32[1,512]{1,0:T(1,128)S(1)}, u32[]{:S(2)}, u32[]{:S(2)}) collective-permute-start(f32[1,512]{1,0:T(1,128)S(1)} %add.33), channel_id=1, source_target_pairs={{0,2},{1,3},{2,0},{3,1},{4,6},{5,7},{6,4},{7,5},{8,10},{9,11},{10,... | collective-permute-start | bytes 6152 | tf_op jit(solution)/shard_map/cond/branch_1_fun/ppermute | solution.py:418
  119.2 2.4 %collective-permute-start.11 = (f32[1,512]{1,0:T(1,128)S(1)}, f32[1,512]{1,0:T(1,128)S(1)}, u32[]{:S(2)}, u32[]{:S(2)}) collective-permute-start(f32[1,512]{1,0:T(1,128)S(1)} %add.34), channel_id=1, source_target_pairs={{0,32},{16,48},{32,0},{48,16},{64,96},{80,112},{96,64},{112,80},{1... | collective-permute-start | bytes 6152 | tf_op jit(solution)/shard_map/cond/branch_1_fun/ppermute | solution.py:418
  121.7 4.2 %collective-permute-start.12 = (f32[1,512]{1,0:T(1,128)S(1)}, f32[1,512]{1,0:T(1,128)S(1)}, u32[]{:S(2)}, u32[]{:S(2)}) collective-permute-start(f32[1,512]{1,0:T(1,128)S(1)} %add.35), channel_id=1, source_target_pairs={{0,64},{16,80},{32,96},{48,112},{64,0},{80,16},{96,32},{112,48},{1... | collective-permute-start | bytes 6152 | tf_op jit(solution)/shard_map/cond/branch_1_fun/ppermute | solution.py:418
  125.9 12.7 %collective-permute-start.13 = (f32[1,512]{1,0:T(1,128)S(1)}, f32[1,512]{1,0:T(1,128)S(1)}, u32[]{:S(2)}, u32[]{:S(2)}) collective-permute-start(f32[1,512]{1,0:T(1,128)S(1)} %add.36), channel_id=1, source_target_pairs={{0,16},{16,0},{32,48},{48,32},{64,80},{80,64},{96,112},{112,96},{1... | collective-permute-start | bytes 6152 | tf_op jit(solution)/shard_map/cond/branch_1_fun/ppermute | solution.py:418
  138.6 3.2 %collective-permute-start.14 = (f32[1,256]{1,0:T(1,128)S(1)}, f32[1,256]{1,0:T(1,128)S(1)}, u32[]{:S(2)}, u32[]{:S(2)}) collective-permute-start(f32[1,256]{1,0:T(1,128)S(1)} %get-tuple-element.72), channel_id=1, source_target_pairs={{0,128},{4,132},{8,136},{12,140},{16,144},{20,148},{24,152},{28,15... | collective-permute-start | bytes 3080 | tf_op jit(solution)/shard_map/cond/branch_1_fun/ppermute | solution.py:400
  139.0 8.3 %collective-permute-start.15 = (f32[1,256]{1,0:T(1,128)S(1)}, f32[1,256]{1,0:T(1,128)S(1)}, u32[]{:S(2)}, u32[]{:S(2)}) collective-permute-start(f32[1,256]{1,0:T(1,128)S(1)} %get-tuple-element.73), channel_id=1, source_target_pairs={{0,140},{4,128},{8,132},{12,136},{16,156},{20,144},{24,148},{28,15... | collective-permute-start | bytes 3080 | tf_op jit(solution)/shard_map/cond/branch_1_fun/ppermute | solution.py:401
  147.3 3.3 %collective-permute-start.16 = (f32[1,512]{1,0:T(1,128)S(1)}, f32[1,512]{1,0:T(1,128)S(1)}, u32[]{:S(2)}, u32[]{:S(2)}) collective-permute-start(f32[1,512]{1,0:T(1,128)S(1)} %maximum_add_fusion.1), channel_id=1, source_target_pairs={{0,4},{4,0},{8,12},{12,8},{1,5},{5,1},{9,13},{13,9},{2,6},{6,2},{1... | collective-permute-start | bytes 6152 | tf_op jit(solution)/shard_map/cond/branch_1_fun/ppermute | solution.py:408
  150.6 6.5 %collective-permute-start.17 = (f32[2,512]{1,0:T(2,128)S(1)}, f32[2,512]{1,0:T(2,128)S(1)}, u32[]{:S(2)}, u32[]{:S(2)}) collective-permute-start(f32[2,512]{1,0:T(2,128)S(1)} %pad_maximum_fusion.3), channel_id=1, source_target_pairs={{0,8},{4,12},{8,0},{12,4},{1,9},{5,13},{9,1},{13,5},{2,10},{6,14},... | collective-permute-start | bytes 12296 | tf_op jit(solution)/shard_map/cond/branch_1_fun/ppermute | solution.py:408
  157.1 0.7 copy-start.8
  157.1 0.8 copy-start.9
  157.9 0.8 copy-start.3
